TPU v7x, 32 devices: a whole 2x2x4 slice. The times are simulated.
32 devices in a mesh: wide: 8 (over y, x, core), narrow: 4 (over z).
Axes of the slice: x: 2, y: 2, z: 4, core: 2. Of those that a mesh axis runs over, the one named last changes fastest.
Arguments:
- tokens: bfloat16 [4, 2048, 1152], P('narrow', 'wide'), may hold values from -6 to 6
- mixer_gain: bfloat16 [1152], P(('wide', 'narrow')), may hold values from 0.099609375 to 1.8984375
- in_weight: bfloat16 [1152, 4608], P(('wide', 'narrow')), may hold values from -0.1875 to 0.1875
- conv_weight: bfloat16 [4, 2304], P(None, ('wide', 'narrow')), may hold values from -3 to 3
- conv_bias: bfloat16 [2304], P(('wide', 'narrow')), may hold values from -3 to 3
- select_weight: bfloat16 [2304, 104], P(('wide', 'narrow')), may hold values from -0.125 to 0.125
- step_weight: bfloat16 [72, 2304], P(None, ('wide', 'narrow')), may hold values from -0.75 to 0.75
- step_bias: bfloat16 [2304], P(('wide', 'narrow')), may hold values from -6 to -2
- decay_log: bfloat16 [16, 2304], P(None, ('wide', 'narrow')), may hold values from -4 to 1
- skip_weight: bfloat16 [2304], P(('wide', 'narrow')), may hold values from 0.5 to 1.5
- out_weight: bfloat16 [2304, 1152], P(('wide', 'narrow')), may hold values from -0.125 to 0.125
- expert_gain: bfloat16 [1152], P(('wide', 'narrow')), may hold values from 0.099609375 to 1.8984375
- router_weight: bfloat16 [1152, 2], P(('wide', 'narrow')), may hold values from -0.125 to 0.125
- up_weight: bfloat16 [2, 1152, 3072], P(None, ('wide', 'narrow')), may hold values from -0.1875 to 0.1875
- down_weight: bfloat16 [2, 3072, 1152], P(None, ('wide', 'narrow')), may hold values from -0.109375 to 0.109375
- routes: int32 [4, 2048], P('narrow', 'wide'), may hold values from 0 to 1
- lengths: int32 [4], P('narrow'), may hold values from 256 to 2048, as said below
- cotangent: bfloat16 [4, 2048, 1152], P('narrow', 'wide'), may hold values from -6 to 6
Outputs:
- output: bfloat16 [4, 2048, 1152], P('narrow', 'wide')
- token_grad: float32 [4, 2048, 1152], P('narrow', 'wide')
- grad_mixer_gain: float32 [1152], P(('wide', 'narrow'))
- grad_in_weight: float32 [1152, 4608], P(('wide', 'narrow'))
- grad_conv_weight: float32 [4, 2304], P(None, ('wide', 'narrow'))
- grad_conv_bias: float32 [2304], P(('wide', 'narrow'))
- grad_select_weight: float32 [2304, 104], P(('wide', 'narrow'))
- grad_step_weight: float32 [72, 2304], P(None, ('wide', 'narrow'))
- grad_step_bias: float32 [2304], P(('wide', 'narrow'))
- grad_decay_log: float32 [16, 2304], P(None, ('wide', 'narrow'))
- grad_skip_weight: float32 [2304], P(('wide', 'narrow'))
- grad_out_weight: float32 [2304, 1152], P(('wide', 'narrow'))
- grad_expert_gain: float32 [1152], P(('wide', 'narrow'))
- grad_router_weight: float32 [1152, 2], P(('wide', 'narrow'))
- grad_up_weight: float32 [2, 1152, 3072], P(None, ('wide', 'narrow'))
- grad_down_weight: float32 [2, 3072, 1152], P(None, ('wide', 'narrow'))
Inputs may be any that keep to these rules, and one draw needn't show every extreme that they name: `lengths`: one sequence, chosen by the seed, counts all its 2048 tokens.
All inputs are finite; a program needn't handle non-finite values.
Results may differ from a plain program's by a relative error of at most 0.011.
Values may be sent and summed in bfloat16 or wider, within the bound.
No kernel may reach another device: no remote copies, remote signals or barrier semaphores. Data moves between devices by JAX's collectives and lax.ppermute only.
A program may use at most 384 MiB of HBM per device.

v0:
```python
import jax
import jax.numpy as jnp
from jax import lax
from jax.sharding import PartitionSpec as P

DI = 2304
NS = 16
DT_RANK = 72
CONV = 4
SCAN_BLOCK = 64
ROW_BLOCK = 128


EPSILON = 1e-05


def passed_along(shard, axis, by):
    size = lax.axis_size(axis)
    pairs = [(i, i + by) for i in range(size) if 0 <= i + by < size]
    return lax.ppermute(shard, axis, pairs)


def prefix(shard, axis, combine, identity):
    size, mine = (lax.axis_size(axis), lax.axis_index(axis))
    everything = jax.tree.map(lambda part: lax.all_gather(part, axis), shard)
    start = jax.tree.map(
        lambda part, zero: jnp.broadcast_to(jnp.asarray(zero, part.dtype), part.shape),
        shard,
        identity,
    )

    def lap(k, before):
        reached = k < mine
        new = combine(before, jax.tree.map(lambda part: part[k], everything))
        return jax.tree.map(lambda a, b: jnp.where(reached, a, b), new, before)

    return lax.fori_loop(0, size, lap, start)


def carried_in_2(shard, axis, join, neutral):
    count = lax.axis_size(axis)
    place = lax.axis_index(axis)
    ahead = count - 1 - place
    gathered = jax.tree.map(
        lambda a, kind: lax.all_gather(a.astype(kind), axis), shard, (jnp.bfloat16, jnp.bfloat16)
    )
    state = jax.tree.map(lambda a, e: jnp.zeros_like(a) + jnp.asarray(e, a.dtype), shard, neutral)

    def one(lap, state):
        source = count - 1 - lap
        return join(
            state,
            jax.tree.map(
                lambda a, own: lax.dynamic_index_in_dim(a, source, 0, False).astype(own.dtype),
                gathered,
                shard,
            ),
        )

    return lax.fori_loop(0, ahead, one, state)


def norm_forward(values, gain_vec):
    inverse = lax.rsqrt(jnp.mean(values * values, axis=-1, keepdims=True) + EPSILON)
    return (values * inverse * gain_vec, inverse)


def norm_backward(values, inverse, gain_vec, upstream):
    scaled = upstream * gain_vec
    inner_mean = jnp.mean(values * scaled, axis=-1, keepdims=True)
    grad_values = inverse * scaled - values * (inverse * inverse * inverse) * inner_mean
    return (grad_values, jnp.sum(upstream * values * inverse, axis=0))


def linked(first, second):
    return (first[0] * second[0], second[0] * first[1] + second[1])


def block_scan(carry_state, pieces, a_neg):
    conv_act, step_size, in_select, out_select = pieces
    decays = jnp.exp(step_size[:, None, :] * a_neg[None, :, :])
    drives = (step_size * conv_act)[:, None, :] * in_select[:, :, None]
    factor, summed = lax.associative_scan(linked, (decays, drives), axis=0)
    states = factor * carry_state[None] + summed
    return (states[-1], jnp.sum(out_select[:, :, None] * states, axis=1))


def local_scan(conv_act, step_size, in_select, out_select, a_neg, start_state):
    length = conv_act.shape[0]
    block_count = length // SCAN_BLOCK

    def advance(carry_state, pieces):
        return block_scan(carry_state, pieces, a_neg)

    def to_blocks(values):
        return values.reshape(block_count, SCAN_BLOCK, values.shape[1])

    end_state, outputs = lax.scan(
        jax.checkpoint(advance),
        start_state,
        (to_blocks(conv_act), to_blocks(step_size), to_blocks(in_select), to_blocks(out_select)),
    )
    return (outputs.reshape(length, conv_act.shape[1]), end_state)


def carried_in(out_select, cumulative, a_neg, entry_state):
    length = out_select.shape[0]
    block_count = length // SCAN_BLOCK

    def one_block(pieces):
        select_blk, cumul_blk = pieces
        factor = jnp.exp(cumul_blk[:, None, :] * a_neg[None]) * entry_state[None]
        return jnp.sum(select_blk[:, :, None] * factor, axis=1)

    shaped = (
        out_select.reshape(block_count, SCAN_BLOCK, out_select.shape[1]),
        cumulative.reshape(block_count, SCAN_BLOCK, cumulative.shape[1]),
    )
    return lax.map(one_block, shaped).reshape(length, cumulative.shape[1])


def pulled_back(out_select, cumulative, a_neg, upstream):
    length = out_select.shape[0]
    block_count = length // SCAN_BLOCK

    def one_block(pieces):
        select_blk, cumul_blk, upper_blk = pieces
        factor = jnp.exp(cumul_blk[:, None, :] * a_neg[None])
        return jnp.sum(factor * select_blk[:, :, None] * upper_blk[:, None, :], axis=0)

    shaped = (
        out_select.reshape(block_count, SCAN_BLOCK, out_select.shape[1]),
        cumulative.reshape(block_count, SCAN_BLOCK, cumulative.shape[1]),
        upstream.reshape(block_count, SCAN_BLOCK, upstream.shape[1]),
    )
    return jnp.sum(lax.map(one_block, shaped), axis=0)


def expert_rows(sorted_rows, weights, owners, flipped):
    block_count = sorted_rows.shape[0] // ROW_BLOCK
    out_width = weights.shape[1] if flipped else weights.shape[2]

    def one_block(block_index):
        block_rows = lax.dynamic_slice_in_dim(sorted_rows, block_index * ROW_BLOCK, ROW_BLOCK, 0)
        marks_blk = lax.dynamic_slice_in_dim(owners, block_index * ROW_BLOCK, ROW_BLOCK, 0)

        def add_expert(expert, running):
            weight = lax.dynamic_index_in_dim(weights, expert, 0, keepdims=False)
            if flipped:
                product = lax.dot_general(
                    block_rows, weight, (((1,), (1,)), ((), ())), preferred_element_type=jnp.float32
                )
            else:
                product = jnp.dot(block_rows, weight, preferred_element_type=jnp.float32)
            return running + jnp.where((marks_blk == expert)[:, None], product, 0.0)

        empty = jnp.zeros((ROW_BLOCK, out_width), jnp.float32)
        return lax.fori_loop(marks_blk[0], marks_blk[ROW_BLOCK - 1] + 1, add_expert, empty)

    results = lax.map(one_block, jnp.arange(block_count))
    return results.reshape(sorted_rows.shape[0], out_width)


def expert_grads(sorted_rows, upstream, owners, experts):
    block_count = sorted_rows.shape[0] // ROW_BLOCK
    start_total = jnp.zeros((experts, sorted_rows.shape[1], upstream.shape[1]), jnp.float32)

    def one_block(block_index, running):
        block_rows = lax.dynamic_slice_in_dim(sorted_rows, block_index * ROW_BLOCK, ROW_BLOCK, 0)
        upper_blk = lax.dynamic_slice_in_dim(upstream, block_index * ROW_BLOCK, ROW_BLOCK, 0)
        marks_blk = lax.dynamic_slice_in_dim(owners, block_index * ROW_BLOCK, ROW_BLOCK, 0)

        def add_expert(expert, totals):
            masked = jnp.where((marks_blk == expert)[:, None], upper_blk, jnp.zeros_like(upper_blk))
            term = lax.dot_general(
                block_rows, masked, (((0,), (0,)), ((), ())), preferred_element_type=jnp.float32
            )
            current = lax.dynamic_index_in_dim(totals, expert, 0, keepdims=False)
            return lax.dynamic_update_index_in_dim(totals, current + term, expert, 0)

        return lax.fori_loop(marks_blk[0], marks_blk[ROW_BLOCK - 1] + 1, add_expert, running)

    return lax.fori_loop(0, block_count, one_block, start_total)


def local(
    tokens,
    mixer_gain,
    in_weight,
    conv_weight,
    conv_bias,
    select_weight,
    step_weight,
    step_bias,
    decay_log,
    skip_weight,
    out_weight,
    expert_gain,
    router_weight,
    up_weight,
    down_weight,
    routes,
    lengths,
    cotangent,
):
    gathered = (
        lax.all_gather(mixer_gain, ("wide", "narrow"), axis=0, tiled=True),
        lax.all_gather(in_weight, ("wide", "narrow"), axis=0, tiled=True),
        lax.all_gather(conv_weight, ("wide", "narrow"), axis=1, tiled=True),
        lax.all_gather(conv_bias, ("wide", "narrow"), axis=0, tiled=True),
        lax.all_gather(select_weight, ("wide", "narrow"), axis=0, tiled=True),
        lax.all_gather(step_weight, ("wide", "narrow"), axis=1, tiled=True),
        lax.all_gather(step_bias, ("wide", "narrow"), axis=0, tiled=True),
        lax.all_gather(decay_log, ("wide", "narrow"), axis=1, tiled=True),
        lax.all_gather(skip_weight, ("wide", "narrow"), axis=0, tiled=True),
        lax.all_gather(out_weight, ("wide", "narrow"), axis=0, tiled=True),
        lax.all_gather(expert_gain, ("wide", "narrow"), axis=0, tiled=True),
        lax.all_gather(router_weight, ("wide", "narrow"), axis=0, tiled=True),
        lax.all_gather(up_weight, ("wide", "narrow"), axis=1, tiled=True),
        lax.all_gather(down_weight, ("wide", "narrow"), axis=1, tiled=True),
    )
    gain_one = gathered[0].astype(jnp.float32)
    taps_full = gathered[2].astype(jnp.float32)
    conv_shift = gathered[3].astype(jnp.float32)
    step_shift = gathered[6].astype(jnp.float32)
    a_neg = -jnp.exp(gathered[7].astype(jnp.float32))
    skip_full = gathered[8].astype(jnp.float32)
    gain_two = gathered[10].astype(jnp.float32)
    inputs = tokens[0].astype(jnp.float32)
    length = inputs.shape[0]
    normed, inverse_one = norm_forward(inputs, gain_one)
    normed_low = normed.astype(jnp.bfloat16)
    projected = jnp.dot(normed_low, gathered[1], preferred_element_type=jnp.float32)
    x_branch = projected[:, :DI]
    z_branch = projected[:, DI:]
    rim_rows = passed_along(x_branch[length - (CONV - 1) :], "wide", 1)
    padded = jnp.concatenate([rim_rows, x_branch], axis=0)
    conv_sum = conv_shift + jnp.zeros_like(x_branch)
    for offset in range(CONV):
        conv_sum = conv_sum + taps_full[offset] * padded[offset : offset + length]
    conv_silu, conv_pull = jax.vjp(jax.nn.silu, conv_sum)
    conv_act = conv_silu.astype(jnp.bfloat16)
    conv_full = conv_act.astype(jnp.float32)
    selected = jnp.dot(conv_act, gathered[4], preferred_element_type=jnp.float32)
    step_low = selected[:, :DT_RANK].astype(jnp.bfloat16)
    in_select = selected[:, DT_RANK : DT_RANK + NS]
    out_select = selected[:, DT_RANK + NS :]
    step_lin = jnp.dot(step_low, gathered[5], preferred_element_type=jnp.float32) + step_shift
    step_size = jax.nn.softplus(step_lin)
    zero_state = jnp.zeros((NS, DI), jnp.float32)
    ones_state = jnp.ones((NS, DI), jnp.float32)
    local_out, local_end = local_scan(
        conv_full, step_size, in_select, out_select, a_neg, zero_state
    )
    cumulative = jnp.cumsum(step_size, axis=0)
    through = jnp.exp(a_neg * cumulative[length - 1][None, :])
    chained = prefix((through, local_end), "wide", linked, (ones_state, zero_state))
    entry_state = chained[1]
    scanned = local_out + carried_in(out_select, cumulative, a_neg, entry_state)
    mixer_out = scanned + skip_full * conv_full
    silu_z, silu_pull = jax.vjp(jax.nn.silu, z_branch)
    gated_act = (mixer_out * silu_z).astype(jnp.bfloat16)
    hidden_one = inputs + jnp.dot(gated_act, gathered[9], preferred_element_type=jnp.float32)
    normed_two, inverse_two = norm_forward(hidden_one, gain_two)
    normed_low_two = normed_two.astype(jnp.bfloat16)
    logits = jnp.dot(normed_low_two, gathered[11], preferred_element_type=jnp.float32)
    router_probs = jax.nn.softmax(logits, axis=-1)
    owners_raw = routes[0]
    onehot = (owners_raw[:, None] == jnp.arange(gathered[11].shape[1])[None, :]).astype(jnp.float32)
    gate_val = jnp.sum(router_probs * onehot, axis=-1)
    order = jnp.argsort(owners_raw, stable=True)
    restore = jnp.zeros_like(order).at[order].set(jnp.arange(length, dtype=order.dtype))
    owners = owners_raw[order]
    sorted_rows = normed_low_two[order]
    pre_act = expert_rows(sorted_rows, gathered[12], owners, False)
    hidden, gelu_pull = jax.vjp(lambda values: jax.nn.gelu(values, approximate=False), pre_act)
    hidden_low = hidden.astype(jnp.bfloat16)
    expert_out = expert_rows(hidden_low, gathered[13], owners, False)[restore]
    output = hidden_one + gate_val[:, None] * expert_out
    positions = lax.axis_index("wide") * length + jnp.arange(length)
    valid = (positions < lengths[0]).astype(jnp.float32)
    upstream = cotangent[0].astype(jnp.float32) * valid[:, None]
    weights_back = (
        lax.all_gather(mixer_gain, ("wide", "narrow"), axis=0, tiled=True),
        lax.all_gather(in_weight, ("wide", "narrow"), axis=0, tiled=True),
        lax.all_gather(conv_weight, ("wide", "narrow"), axis=1, tiled=True),
        lax.all_gather(conv_bias, ("wide", "narrow"), axis=0, tiled=True),
        lax.all_gather(select_weight, ("wide", "narrow"), axis=0, tiled=True),
        lax.all_gather(step_weight, ("wide", "narrow"), axis=1, tiled=True),
        lax.all_gather(step_bias, ("wide", "narrow"), axis=0, tiled=True),
        lax.all_gather(decay_log, ("wide", "narrow"), axis=1, tiled=True),
        lax.all_gather(skip_weight, ("wide", "narrow"), axis=0, tiled=True),
        lax.all_gather(out_weight, ("wide", "narrow"), axis=0, tiled=True),
        lax.all_gather(expert_gain, ("wide", "narrow"), axis=0, tiled=True),
        lax.all_gather(router_weight, ("wide", "narrow"), axis=0, tiled=True),
        lax.all_gather(up_weight, ("wide", "narrow"), axis=1, tiled=True),
        lax.all_gather(down_weight, ("wide", "narrow"), axis=1, tiled=True),
    )
    full_in = weights_back[1]
    full_select = weights_back[4]
    full_step = weights_back[5]
    full_out = weights_back[9]
    full_router = weights_back[11]
    full_up = weights_back[12]
    full_down = weights_back[13]
    d_gate = jnp.sum(expert_out * upstream, axis=-1)
    d_expert = (gate_val[:, None] * upstream).astype(jnp.bfloat16)
    d_expert_sorted = d_expert[order]
    d_hidden = expert_rows(d_expert_sorted, full_down, owners, True)
    grad_down = expert_grads(hidden_low, d_expert_sorted, owners, full_down.shape[0])
    d_pre = gelu_pull(d_hidden)[0].astype(jnp.bfloat16)
    grad_up = expert_grads(sorted_rows, d_pre, owners, full_up.shape[0])
    d_rows_sorted = expert_rows(d_pre, full_up, owners, True)
    d_logits = (router_probs * d_gate[:, None] * (onehot - gate_val[:, None])).astype(jnp.bfloat16)
    grad_router = lax.dot_general(
        normed_low_two, d_logits, (((0,), (0,)), ((), ())), preferred_element_type=jnp.float32
    )
    d_normed_two = d_rows_sorted[restore] + lax.dot_general(
        d_logits, full_router, (((1,), (1,)), ((), ())), preferred_element_type=jnp.float32
    )
    d_through_two, grad_gain_two = norm_backward(hidden_one, inverse_two, gain_two, d_normed_two)
    d_hidden_one = upstream + d_through_two
    d_mix = d_hidden_one.astype(jnp.bfloat16)
    grad_out = lax.dot_general(
        gated_act, d_mix, (((0,), (0,)), ((), ())), preferred_element_type=jnp.float32
    )
    d_gated = lax.dot_general(
        d_mix, full_out, (((1,), (1,)), ((), ())), preferred_element_type=jnp.float32
    )
    d_mixer = d_gated * silu_z
    d_z_branch = silu_pull(d_gated * mixer_out)[0]
    grad_skip = jnp.sum(d_mixer * conv_full, axis=0)
    entry_grad = pulled_back(out_select, cumulative, a_neg, d_mixer)
    adjoint = carried_in_2((through, entry_grad), "wide", linked, (ones_state, zero_state))
    exit_grad = adjoint[1]
    scan_value, scan_pull = jax.vjp(
        local_scan, conv_full, step_size, in_select, out_select, a_neg, entry_state
    )
    scan_grads = scan_pull((d_mixer, exit_grad))
    d_conv_scan = scan_grads[0]
    d_step = scan_grads[1]
    d_in_select = scan_grads[2]
    d_out_select = scan_grads[3]
    grad_decay = scan_grads[4] * a_neg
    step_grad = d_step * jax.nn.sigmoid(step_lin)
    grad_step_bias = jnp.sum(step_grad, axis=0)
    step_grad_low = step_grad.astype(jnp.bfloat16)
    grad_step = lax.dot_general(
        step_low, step_grad_low, (((0,), (0,)), ((), ())), preferred_element_type=jnp.float32
    )
    d_step_low = lax.dot_general(
        step_grad_low, full_step, (((1,), (1,)), ((), ())), preferred_element_type=jnp.float32
    )
    d_selected = jnp.concatenate([d_step_low, d_in_select, d_out_select], axis=1).astype(
        jnp.bfloat16
    )
    grad_select = lax.dot_general(
        conv_act, d_selected, (((0,), (0,)), ((), ())), preferred_element_type=jnp.float32
    )
    d_conv_act = (
        lax.dot_general(
            d_selected, full_select, (((1,), (1,)), ((), ())), preferred_element_type=jnp.float32
        )
        + skip_full * d_mixer
        + d_conv_scan
    )
    d_conv_sum = conv_pull(d_conv_act)[0]
    grad_conv_bias = jnp.sum(d_conv_sum, axis=0)
    grad_conv = jnp.stack(
        [jnp.sum(d_conv_sum * padded[offset : offset + length], axis=0) for offset in range(CONV)]
    )
    d_padded = jnp.zeros((length + CONV - 1, DI), jnp.float32)
    for offset in range(CONV):
        d_padded = d_padded + jnp.pad(
            taps_full[offset] * d_conv_sum, ((offset, CONV - 1 - offset), (0, 0))
        )
    rim_grad = passed_along(d_padded[: CONV - 1], "wide", -1)
    d_x_branch = d_padded[CONV - 1 :] + jnp.pad(rim_grad, ((length - (CONV - 1), 0), (0, 0)))
    d_projected = jnp.concatenate([d_x_branch, d_z_branch], axis=1).astype(jnp.bfloat16)
    grad_in = lax.dot_general(
        normed_low, d_projected, (((0,), (0,)), ((), ())), preferred_element_type=jnp.float32
    )
    d_normed = lax.dot_general(
        d_projected, full_in, (((1,), (1,)), ((), ())), preferred_element_type=jnp.float32
    )
    d_inputs, grad_gain_one = norm_backward(inputs, inverse_one, gain_one, d_normed)
    token_grad = d_hidden_one + d_inputs
    shards = tuple(
        (
            lax.psum_scatter(grad_gain_one, ("wide", "narrow"), scatter_dimension=0, tiled=True),
            lax.psum_scatter(grad_in, ("wide", "narrow"), scatter_dimension=0, tiled=True),
            lax.psum_scatter(grad_conv, ("wide", "narrow"), scatter_dimension=1, tiled=True),
            lax.psum_scatter(grad_conv_bias, ("wide", "narrow"), scatter_dimension=0, tiled=True),
            lax.psum_scatter(grad_select, ("wide", "narrow"), scatter_dimension=0, tiled=True),
            lax.psum_scatter(grad_step, ("wide", "narrow"), scatter_dimension=1, tiled=True),
            lax.psum_scatter(grad_step_bias, ("wide", "narrow"), scatter_dimension=0, tiled=True),
            lax.psum_scatter(grad_decay, ("wide", "narrow"), scatter_dimension=1, tiled=True),
            lax.psum_scatter(grad_skip, ("wide", "narrow"), scatter_dimension=0, tiled=True),
            lax.psum_scatter(grad_out, ("wide", "narrow"), scatter_dimension=0, tiled=True),
            lax.psum_scatter(grad_gain_two, ("wide", "narrow"), scatter_dimension=0, tiled=True),
            lax.psum_scatter(grad_router, ("wide", "narrow"), scatter_dimension=0, tiled=True),
            lax.psum_scatter(grad_up, ("wide", "narrow"), scatter_dimension=1, tiled=True),
            lax.psum_scatter(grad_down, ("wide", "narrow"), scatter_dimension=1, tiled=True),
        )
    )
    return (output.astype(jnp.bfloat16)[None], token_grad[None]) + shards


def solution(mesh):
    return jax.shard_map(
        local,
        mesh=mesh,
        in_specs=(
            P("narrow", "wide", None),
            P(("wide", "narrow")),
            P(("wide", "narrow"), None),
            P(None, ("wide", "narrow")),
            P(("wide", "narrow")),
            P(("wide", "narrow"), None),
            P(None, ("wide", "narrow")),
            P(("wide", "narrow")),
            P(None, ("wide", "narrow")),
            P(("wide", "narrow")),
            P(("wide", "narrow"), None),
            P(("wide", "narrow")),
            P(("wide", "narrow"), None),
            P(None, ("wide", "narrow"), None),
            P(None, ("wide", "narrow"), None),
            P("narrow", "wide"),
            P("narrow"),
            P("narrow", "wide", None),
        ),
        out_specs=(
            P("narrow", "wide", None),
            P("narrow", "wide", None),
            P(("wide", "narrow")),
            P(("wide", "narrow"), None),
            P(None, ("wide", "narrow")),
            P(("wide", "narrow")),
            P(("wide", "narrow"), None),
            P(None, ("wide", "narrow")),
            P(("wide", "narrow")),
            P(None, ("wide", "narrow")),
            P(("wide", "narrow")),
            P(("wide", "narrow"), None),
            P(("wide", "narrow")),
            P(("wide", "narrow"), None),
            P(None, ("wide", "narrow"), None),
            P(None, ("wide", "narrow"), None),
        ),
        check_vma=False,
    )
```

profile of v0, /device:TPU:0, one launch (start us, length us, event | category | flops | bytes accessed | tf_op | source)
XLA Modules:
  0.0 7368.4 jit_solution(11559311636895576050)
XLA Ops:
  12.2 43.7 all-reduce.153
  56.0 66.9 all-gather.4
  123.8 64.6 all-gather.6
  189.7 70.2 all_gather.76
  260.6 69.2 all_gather.75
  373.7 1161.1 %while.243 = (s32[]{:T(128)}, f32[16,2304]{1,0:T(8,128)}, f32[4,64,2304]{2,1,0:T(8,128)}, f32[4,64,2304]{2,1,0:T(8,128)}, f32[16,2304]{1,0:T(8,128)S(1)}, /*inde...) while((s32[]{:T(128)}, f32[16,2304]{1,0:T(8,128)}, ...), condition=%wide.region_3.4_spmd, body=%wide.region_1.3_spmd.sunk | while | flops 45490176 | bytes 535913024 | solution.py:98
  1544.2 64.7 all-gather.7
  1636.2 814.1 %while.255 = (s32[]{:T(128)}, f32[16,2304]{1,0:T(8,128)}, f32[4,16,2304]{2,1,0:T(8,128)}, f32[4,64,2304]{2,1,0:T(8,128)}, f32[1,16,2304]{2,1,0:T(8,128)S(1)}, /*...) while((s32[]{:T(128)}, f32[16,2304]{1,0:T(8,128)}, ...), condition=%wide.region_42.43_spmd, body=%wide.region_41.42_spmd.sunk | while | flops 23556096 | bytes 370283200 | solution.py:98
  1760.0 22.1 pad.1797
  1818.4 21.7 pad.1800
  1963.6 21.7 pad.1797
  2166.5 21.7 pad.1797
  2451.9 24.2 while.244
  2492.5 31.2 while.250
  2538.9 30.8 while.246
  2591.5 30.2 while.252
  2627.3 32.2 while.248
  2714.2 2944.4 %while.261 = (s32[]{:T(128)}, f32[16,2304]{1,0:T(8,128)}, f32[16,2304]{1,0:T(8,128)S(1)}, f32[4,64,2304]{2,1,0:T(8,128)}, f32[4,64,2304]{2,1,0:T(8,128)}, /*inde...) while((s32[]{:T(128)}, f32[16,2304]{1,0:T(8,128)}, ...), condition=%wide.region_50.51_spmd.clone, body=%wide.region_43.50_spmd.clone.sunk | while | flops 142514176 | bytes 1542841472 | solution.py:98
  3646.6 21.7 slice_multiply_fusion.86
  5690.4 81.0 %while.257 = (s32[]{:T(128)}, f32[2,1152,3072]{1,2,0:T(8,128)}, s32[256]{0:T(256)S(1)}, bf16[256,3072]{1,0:T(8,128)(2,1)S(1)}, bf16[256,1152]{1,0:T(8,128)(2,1)}...) while((s32[]{:T(128)}, f32[2,1152,3072]{1,2,0:T(8,128)}, ...), condition=%wide.region_76.77_spmd, body=%wide.region_73.76_spmd.sunk | while | flops 909901952 | bytes 59869360 | solution.py:183
  5692.8 50.6 while.266
  5745.8 25.6 while.266
  5785.6 41.9 copy.193
  5850.4 83.5 %while.259 = (s32[]{:T(128)}, f32[2,3072,1152]{1,2,0:T(8,128)}, s32[256]{0:T(256)S(1)}, bf16[256,1152]{1,0:T(8,128)(2,1)S(1)}, bf16[256,3072]{1,0:T(8,128)(2,1)S...) while((s32[]{:T(128)}, f32[2,3072,1152]{1,2,0:T(8,128)}, ...), condition=%wide.region_81.82_spmd, body=%wide.region_78.81_spmd.sunk | while | flops 909656192 | bytes 59869360 | solution.py:183
  5851.8 52.6 while.267
  5905.9 28.0 while.267
  5933.9 28.1 copy.194
  5974.1 768.4 %fusion = f32[40,4608]{1,0:T(8,128)S(1)} fusion(f32[1152,4608]{1,0:T(8,128)} %fusion.124), kind=kCustom, calls=%all-reduce-scatter | all-reduce-scatter fusion | flops 5898241 | bytes 21970944
  6776.3 25.5 collective-permute-done.3
  6847.8 98.2 %reduce-scatter.16.cloned.1.call-done = f32[72,104]{1,0:T(8,128)} async-done(((f32[2304,104]{1,0:T(8,128)}), f32[72,104]{1,0:T(8,128)}) %reduce-scatter.16.cloned.1.call-update) | async-done | bytes 29968
  6946.1 147.5 %reduce-scatter.18.cloned.1.call-done = f32[72,1152]{1,0:T(8,128)} async-done(((f32[2304,1152]{1,0:T(8,128)}), f32[72,1152]{1,0:T(8,128)}) %reduce-scatter.18.cloned.1.call-update) | async-done | bytes 331792
  7093.6 268.1 %reduce-scatter.14.cloned.1.call-done = f32[2,96,1152]{2,1,0:T(8,128)} async-done(((f32[2,3072,1152]{2,1,0:T(8,128)}), f32[2,96,1152]{2,1,0:T(8,128)}) %reduce-scatter.14.cloned.1.call-update) | async-done | bytes 884752 | tf_op jit(solution)/shard_map/reduce_scatter | solution.py:403
  (2768 shorter events, 5536.7 us)
Async XLA Ops:
  7.2 322.6 %all-gather.25.cloned.1.call-start = ((), (), s32[]{:S(2)}) async-start(), calls=%async_computation.9 | async-start | bytes 12165120 | tf_op jit(solution)/shard_map/all_gather | solution.py:208
  7.9 1617.8 %all-gather.21.cloned.1.call-start = ((), (), s32[]{:S(2)}) async-start(), calls=%async_computation.7 | async-start | bytes 1327104 | tf_op jit(solution)/shard_map/all_gather | solution.py:25
  56.0 288.2 %copy-start.170 = (f32[1152]{0:T(1024)}, f32[1152]{0:T(1024)S(1)}, u32[]{:S(2)}) copy-start(f32[1152]{0:T(1024)S(1)} %convert_element_type.132) | copy-start | bytes 13828
  259.9 102.5 %copy-start.160 = (bf16[72,2304]{0,1:T(8,128)(2,1)}, bf16[72,2304]{0,1:T(8,128)(2,1)S(1)}, u32[]{:S(2)}) copy-start(bf16[72,2304]{0,1:T(8,128)(2,1)S(1)} %all_gather.76) | copy-start | bytes 995332
  260.5 83.6 %copy-start.203 = (f32[256]{0:T(256)}, f32[256]{0:T(256)S(1)}, u32[]{:S(2)}) copy-start(f32[256]{0:T(256)S(1)} %get-tuple-element.2002) | copy-start | bytes 3076
  352.4 3.7 collective-permute-start
  371.3 1254.4 %all-gather.23.cloned.1.call-start = ((), (), s32[]{:S(2)}) async-start(), calls=%async_computation.8 | async-start | bytes 1327104 | tf_op jit(solution)/shard_map/all_gather | solution.py:25
  373.7 1163.0 %copy-start.217 = (bf16[2304]{0:T(1024)(128)(2,1)S(1)}, bf16[2304]{0:T(1024)(128)(2,1)}, u32[]{:S(2)}) copy-start(bf16[2304]{0:T(1024)(128)(2,1)} %get-tuple-element.1803) | copy-start | bytes 13828
  373.7 1163.6 %copy-start.218 = (bf16[1152]{0:T(1024)(128)(2,1)S(1)}, bf16[1152]{0:T(1024)(128)(2,1)}, u32[]{:S(2)}) copy-start(bf16[1152]{0:T(1024)(128)(2,1)} %get-tuple-element.1805) | copy-start | bytes 6916
  373.7 1164.2 %copy-start.7 = (s32[1,256]{1,0:T(1,128)S(1)}, s32[1,256]{1,0:T(1,128)}, u32[]{:S(2)}) copy-start(s32[1,256]{1,0:T(1,128)} %param.71) | copy-start | bytes 3076
  1534.8 946.4 %all-gather.15.cloned.1.call-start = ((), (), s32[]{:S(2)}) async-start(), calls=%async_computation.3 | async-start | bytes 5474304 | tf_op jit(solution)/shard_map/all_gather | solution.py:216
  1535.4 957.1 %all-gather.19.cloned.1.call-start = ((), (), s32[]{:S(2)}) async-start(), calls=%async_computation.5 | async-start | bytes 14598144 | tf_op jit(solution)/shard_map/all_gather | solution.py:220
  1536.0 987.8 %all-gather.17.cloned.1.call-start = ((), (), s32[]{:S(2)}) async-start(), calls=%async_computation.4 | async-start | bytes 14598144 | tf_op jit(solution)/shard_map/all_gather | solution.py:219
  1536.6 5219.3 %all-reduce.157.cloned.1.call-start = ((), (), s32[]{:S(2)}) async-start(), calls=%async_computation.12 | async-start | bytes 198656
  5674.8 98.3 %collective-permute-start.1 = (f32[3,2304]{1,0:T(4,128)}, f32[3,2304]{1,0:T(4,128)}, u32[]{:S(2)}, u32[]{:S(2)}) collective-permute-start(f32[3,2304]{1,0:T(4,128)} %pad_add_fusion.21), channel_id=1, source_target_pairs={{4,0},{8,4},{12,8},{16,12},{20,16},{24,20},{28,24},{5,1},{9,5},{13... | collective-permute-start | bytes 82952 | tf_op jit(solution)/shard_map/ppermute | solution.py:20
  5690.4 81.1 %copy-start.192 = (f32[1,2304]{1,0:T(1,128)S(1)}, f32[1,2304]{1,0:T(1,128)}, u32[]{:S(2)}) copy-start(f32[1,2304]{1,0:T(1,128)} %stack.16) | copy-start | bytes 27652
  5690.4 81.8 %copy-start.10 = (s32[1,256]{1,0:T(1,128)S(1)}, s32[1,256]{1,0:T(1,128)}, u32[]{:S(2)}) copy-start(s32[1,256]{1,0:T(1,128)} %param.71) | copy-start | bytes 3076
  5690.4 81.8 %copy-start.81 = (bf16[256,1152]{1,0:T(8,128)(2,1)S(1)}, bf16[256,1152]{1,0:T(8,128)(2,1)}, u32[]{:S(2)}) copy-start(bf16[256,1152]{1,0:T(8,128)(2,1)} %copy-done.80) | copy-start | bytes 1769476
  5690.4 81.8 %copy-start.202 = (f32[256]{0:T(256)S(1)}, f32[256]{0:T(256)}, u32[]{:S(2)}) copy-start(f32[256]{0:T(256)} %copy-done.200) | copy-start | bytes 3076
  5690.4 81.8 %copy-start.207 = (f32[256,2]{0,1:T(2,128)S(1)}, f32[256,2]{0,1:T(2,128)}, u32[]{:S(2)}) copy-start(f32[256,2]{0,1:T(2,128)} %get-tuple-element.1833) | copy-start | bytes 6148
  5690.4 81.8 %copy-start.216 = (f32[256]{0:T(256)S(1)}, f32[256]{0:T(256)}, u32[]{:S(2)}) copy-start(f32[256]{0:T(256)} %copy-done.215) | copy-start | bytes 3076
  5784.4 1058.4 %all-reduce.159.cloned.1.call-start = ((), (), s32[]{:S(2)}) async-start(), calls=%async_computation.13 | async-start | bytes 58245120
  5827.6 1118.5 %reduce-scatter.16.cloned.1.call-start = ((), (), s32[]{:S(2)}) async-start(), calls=%async_computation.10 | async-start | bytes 1216512
  5831.2 1262.4 %reduce-scatter.18.cloned.1.call-start = ((), (), s32[]{:S(2)}) async-start(), calls=%async_computation.11 | async-start | bytes 10948608
  5837.3 1524.3 %reduce-scatter.14.cloned.1.call-start = ((), (), s32[]{:S(2)}) async-start(), calls=%async_computation.6 | async-start | bytes 29196288 | tf_op jit(solution)/shard_map/reduce_scatter | solution.py:403
  5974.1 779.1 %copy-start.221 = (f32[256]{0:T(256)S(1)}, f32[256]{0:T(256)}, u32[]{:S(2)}) copy-start(f32[256]{0:T(256)} %get-tuple-element.1544) | copy-start | bytes 3076
  5974.1 779.1 %copy-start.127 = (f32[256,1152]{1,0:T(8,128)S(1)}, f32[256,1152]{1,0:T(8,128)}, u32[]{:S(2)}) copy-start(f32[256,1152]{1,0:T(8,128)} %copy-done.125) | copy-start | bytes 3538948
  5974.1 779.1 %copy-start.219 = (f32[256]{0:T(256)S(1)}, f32[256]{0:T(256)}, u32[]{:S(2)}) copy-start(f32[256]{0:T(256)} %get-tuple-element.2001) | copy-start | bytes 3076
  6742.6 33.8 collective-permute-start.4
  6743.9 57.9 collective-permute-start.3
  6748.2 72.1 collective-permute-start.2
  6750.4 14.4 collective-permute-start.5
  (618 other events, 5311.7 us)
Sparse Core Ops, SparseCore 0:
  10.8 96.0 all-gather.24
  371.5 24.6 all-gather.20
  1534.9 24.6 all-gather.22
  1562.3 67.0 all-gather.14
  1632.4 101.7 all-gather.18
  1736.9 101.3 all-gather.16
  5784.5 122.4 all-reduce.156
  5914.5 928.1 all-reduce.158
  6848.4 97.6 reduce-scatter.15
  6952.6 140.9 reduce-scatter.17
  7100.6 261.0 reduce-scatter.13
where the time goes:
time: 7440 us; the launch traced here: 7370 us
  local copies, waits for them, and re-layouts  3720 us (50%)
  other arithmetic  1600 us (22%)
  blocking collectives  1170 us (16%)
  waiting for transfers between devices  581 us (8%)
  matrix products  197 us (3%)
    pad x376, local copies, waits for them, and re-layouts, block_scan(): factor, summed = lax.associative_scan(linked, (decays, drives), axis=0)  2890 us
    unnamed x2, blocking collectives  812 us
    mul x136, other arithmetic, linked(): return (first[0] * second[0], second[0] * first[1] + second[1])  490 us
    add x120, other arithmetic, block_scan(): factor, summed = lax.associative_scan(linked, (decays, drives), axis=0)  359 us
    unnamed x19, waiting for transfers between devices  313 us
    while x984, local copies, waits for them, and re-layouts  312 us
    reduce_scatter x1, waiting for transfers between devices, local(): lax.psum_scatter(grad_down, ('wide', 'narrow'), scatter_dimension=1, tile...  268 us
    concatenate x112, other arithmetic, block_scan(): factor, summed = lax.associative_scan(linked, (decays, drives), axis=0)  180 us
  transfers between devices with their start and end apart: 17, of which 7 were waited for; matrix products, arithmetic and copies ran while one was open for 42% of the time, Pallas kernels for 0%

commit v1 on v0

v1 whole, which is shorter than its diff:
```python
import math

import jax
import jax.numpy as jnp
from jax import lax
from jax.experimental import pallas as pl
from jax.experimental.pallas import tpu as pltpu
from jax.sharding import PartitionSpec as P

D = 1152
DI = 2304
NS = 16
DT_RANK = 72
CONV = 4
FF = 3072
EXPERTS = 2
EPSILON = 1e-05
TIME_BLOCK = 128
UNROLL = 64
LANES = 128
LN2 = math.log(2.0)

f32 = jnp.float32
bf16 = jnp.bfloat16


def swap(x, k):
    n = lax.axis_size("wide")
    return lax.ppermute(x, "wide", [(i, i ^ k) for i in range(n)])


def turn(x, k):
    n = lax.axis_size("narrow")
    return lax.ppermute(x, "narrow", [(i, (i + k) % n) for i in range(n)])


def place():
    w = lax.axis_index("wide")
    return w // 2, w % 2


def pick(x, i, axis=0):
    return lax.dynamic_index_in_dim(x, i, axis, False)


def gather_wide(block):
    n = lax.axis_size("wide")
    if n != 8:
        return lax.all_gather(block, "wide", axis=0, tiled=True)
    chip, core = place()
    rows, cols = block.shape
    half = rows // 2
    mate = swap(block, 1)
    a, b = swap(block, 2), swap(block, 4)
    c = jnp.concatenate([swap(a[:half], 4), swap(b[half:], 2)], axis=0)
    mine = (block, a, b, c)
    theirs = (mate, swap(a, 1), swap(b, 1), swap(c, 1))
    out = jnp.zeros((8, rows, cols), block.dtype)
    for q in range(4):
        at = (chip ^ q) * 2
        out = lax.dynamic_update_index_in_dim(out, mine[q], at + core, 0)
        out = lax.dynamic_update_index_in_dim(out, theirs[q], at + 1 - core, 0)
    return out.reshape(8 * rows, cols)


def scatter_wide(partial):
    n = lax.axis_size("wide")
    if n != 8:
        return lax.psum_scatter(partial, "wide", scatter_dimension=0, tiled=True).astype(f32)
    chip, core = place()
    rows = partial.shape[0] // 8
    half = rows // 2
    parts = partial.reshape(4, 2, rows, partial.shape[1])
    own = pick(parts, core, 1)
    other = swap(pick(parts, 1 - core, 1), 1)

    def summed(q):
        return pick(own, chip ^ q).astype(f32) + pick(other, chip ^ q).astype(f32)

    far = summed(3).astype(bf16)
    sx, sy = summed(1), summed(2)
    r0, r1 = swap(far[:half], 2), swap(far[half:], 4)
    x0, y1 = swap(sx[:half].astype(bf16), 2), swap(sy[half:].astype(bf16), 4)
    x1 = swap((sx[half:] + r1.astype(f32)).astype(bf16), 2)
    y0 = swap((sy[:half] + r0.astype(f32)).astype(bf16), 4)
    x = jnp.concatenate([x0, x1], axis=0).astype(f32)
    y = jnp.concatenate([y0, y1], axis=0).astype(f32)
    return summed(0) + x + y


def reduce_wide(partial):
    n = lax.axis_size("wide")
    if n != 8:
        return lax.psum(partial.astype(bf16), "wide")
    _, core = place()
    half = partial.shape[0] // 2
    parts = partial.astype(bf16).reshape(2, half, partial.shape[1])
    total = pick(parts, core).astype(f32) + swap(pick(parts, 1 - core), 1).astype(f32)
    low = total.astype(bf16)
    total = (
        total + swap(low, 2).astype(f32) + swap(low, 4).astype(f32) + swap(low, 6).astype(f32)
    )
    low = total.astype(bf16)
    out = jnp.zeros((2, half, partial.shape[1]), bf16)
    out = lax.dynamic_update_index_in_dim(out, low, core, 0)
    out = lax.dynamic_update_index_in_dim(out, swap(low, 1), 1 - core, 0)
    return out.reshape(partial.shape)


def gather_narrow(x):
    n, z = lax.axis_size("narrow"), lax.axis_index("narrow")
    out = lax.dynamic_update_index_in_dim(jnp.zeros((n,) + x.shape, x.dtype), x, z, 0)
    for k in range(1, n):
        out = lax.dynamic_update_index_in_dim(out, turn(x, k), (z - k) % n, 0)
    return out


def scatter_narrow(x):
    n, z = lax.axis_size("narrow"), lax.axis_index("narrow")
    total = pick(x, z).astype(f32)
    for k in range(1, n):
        total = total + turn(pick(x, (z + k) % n), k).astype(f32)
    return total


def exchange_wide(x):
    return lax.all_to_all(x, "wide", 0, 0)


def scan_forward_kernel(x_ref, dt_ref, b_ref, c_ref, a_ref, y_ref, kept_ref, end_ref, state):
    @pl.when(pl.program_id(0) == 0)
    def _():
        state[...] = jnp.zeros_like(state)

    a2 = a_ref[...]
    in_sel, out_sel = b_ref[...], c_ref[...]

    def group(g, h):
        t0 = pl.multiple_of(g * UNROLL, UNROLL)
        back = lax.rem(TIME_BLOCK - t0, TIME_BLOCK)
        b, c = pltpu.roll(in_sel, back, 1), pltpu.roll(out_sel, back, 1)
        dt = dt_ref[pl.ds(t0, UNROLL), :]
        u = dt * x_ref[pl.ds(t0, UNROLL), :].astype(f32)
        for j in range(UNROLL):
            kept_ref[t0 + j] = h
            h = jnp.exp2(dt[j : j + 1, :] * a2) * h + u[j : j + 1, :] * b[:, j : j + 1]
            y_ref[pl.ds(t0 + j, 1), :] = jnp.sum(h * c[:, j : j + 1], axis=0, keepdims=True)
        return h

    h = lax.fori_loop(0, TIME_BLOCK // UNROLL, group, state[...])
    state[...] = h
    end_ref[...] = h


def scan_forward(x, dt, in_sel, out_sel, a2):
    length, chans = x.shape
    row = pl.BlockSpec((TIME_BLOCK, chans), lambda i: (i, 0))
    sel = pl.BlockSpec((NS, TIME_BLOCK), lambda i: (0, i))
    whole = pl.BlockSpec((NS, chans), lambda i: (0, 0))
    return pl.pallas_call(
        scan_forward_kernel,
        grid=(length // TIME_BLOCK,),
        in_specs=[row, row, sel, sel, whole],
        out_specs=[row, pl.BlockSpec((TIME_BLOCK, NS, chans), lambda i: (i, 0, 0)), whole],
        out_shape=[
            jax.ShapeDtypeStruct((length, chans), f32),
            jax.ShapeDtypeStruct((length, NS, chans), f32),
            jax.ShapeDtypeStruct((NS, chans), f32),
        ],
        scratch_shapes=[pltpu.VMEM((NS, chans), f32)],
        compiler_params=pltpu.CompilerParams(vmem_limit_bytes=24 * 2**20),
        cost_estimate=pl.CostEstimate(
            flops=8 * length * NS * chans,
            bytes_accessed=4 * length * chans * (NS + 3),
            transcendentals=length * NS * chans,
        ),
    )(x, dt, in_sel, out_sel, a2)


def scan_backward_kernel(
    x_ref,
    dt_ref,
    dy_ref,
    b_ref,
    c_ref,
    a_ref,
    kept_ref,
    end_ref,
    dstep_ref,
    dconv_ref,
    db_ref,
    dc_ref,
    da_ref,
    lam_s,
    next_s,
    pb_s,
    pc_s,
):
    chans = x_ref.shape[1]
    groups = TIME_BLOCK // UNROLL

    @pl.when(pl.program_id(0) == 0)
    def _():
        lam_s[...] = jnp.zeros_like(lam_s)
        next_s[...] = end_ref[...]
        da_ref[...] = jnp.zeros_like(da_ref)

    a2 = a_ref[...]
    in_sel, out_sel = b_ref[...], c_ref[...]

    def fold(v):
        total = v[:, :LANES]
        for k in range(1, chans // LANES):
            total = total + v[:, k * LANES : (k + 1) * LANES]
        return total

    def group(i, carry):
        p, after, acc = carry
        t0 = pl.multiple_of((groups - 1 - i) * UNROLL, UNROLL)
        back = lax.rem(TIME_BLOCK - t0, TIME_BLOCK)
        b, c = pltpu.roll(in_sel, back, 1), pltpu.roll(out_sel, back, 1)
        dt = dt_ref[pl.ds(t0, UNROLL), :]
        x = x_ref[pl.ds(t0, UNROLL), :].astype(f32)
        dy = dy_ref[pl.ds(t0, UNROLL), :]
        u = dt * x
        for j in range(UNROLL - 1, -1, -1):
            before = kept_ref[t0 + j]
            dt_j, dy_j = dt[j : j + 1, :], dy[j : j + 1, :]
            lam = dy_j * c[:, j : j + 1] + p
            p = lam * jnp.exp2(dt_j * a2)
            moved = p * before
            acc = acc + dt_j * moved
            dconv_ref[pl.ds(t0 + j, 1), :] = jnp.sum(lam * b[:, j : j + 1], axis=0, keepdims=True)
            dstep_ref[pl.ds(t0 + j, 1), :] = jnp.sum(a2 * moved, axis=0, keepdims=True)
            pb_s[t0 + j] = fold(lam * u[j : j + 1, :])
            pc_s[t0 + j] = fold(after * dy_j)
            after = before
        through = dconv_ref[pl.ds(t0, UNROLL), :]
        dstep_ref[pl.ds(t0, UNROLL), :] = dstep_ref[pl.ds(t0, UNROLL), :] * LN2 + x * through
        dconv_ref[pl.ds(t0, UNROLL), :] = dt * through
        return p, after, acc

    p, after, acc = lax.fori_loop(0, groups, group, (lam_s[...], next_s[...], da_ref[...]))
    lam_s[...] = p
    next_s[...] = after
    da_ref[...] = acc
    ones = jnp.ones((LANES, LANES), bf16)
    lane = lax.broadcasted_iota(jnp.int32, (NS, TIME_BLOCK), 1)
    for part, out in ((pb_s, db_ref), (pc_s, dc_ref)):

        def reduced(g, total):
            t0 = pl.multiple_of(g * 16, 16)
            rows = part[pl.ds(t0, 16)].reshape(16 * NS, LANES).astype(bf16)
            sums = jnp.dot(rows, ones, preferred_element_type=f32).reshape(16, NS, LANES)
            for j in range(16):
                total = jnp.where(lane == t0 + j, sums[j], total)
            return total

        out[...] = lax.fori_loop(0, TIME_BLOCK // 16, reduced, jnp.zeros((NS, TIME_BLOCK), f32))


def scan_backward(x, dt, dy, in_sel, out_sel, a2, kept, end):
    length, chans = x.shape
    n = length // TIME_BLOCK
    row = pl.BlockSpec((TIME_BLOCK, chans), lambda i: (n - 1 - i, 0))
    sel = pl.BlockSpec((NS, TIME_BLOCK), lambda i: (0, n - 1 - i))
    whole = pl.BlockSpec((NS, chans), lambda i: (0, 0))
    states = pl.BlockSpec((TIME_BLOCK, NS, chans), lambda i: (n - 1 - i, 0, 0))
    return pl.pallas_call(
        scan_backward_kernel,
        grid=(n,),
        in_specs=[row, row, row, sel, sel, whole, states, whole],
        out_specs=[row, row, sel, sel, whole],
        out_shape=[jax.ShapeDtypeStruct((length, chans), f32)] * 2
        + [jax.ShapeDtypeStruct((NS, length), f32)] * 2
        + [jax.ShapeDtypeStruct((NS, chans), f32)],
        scratch_shapes=[pltpu.VMEM((NS, chans), f32)] * 2
        + [pltpu.VMEM((TIME_BLOCK, NS, LANES), f32)] * 2,
        compiler_params=pltpu.CompilerParams(vmem_limit_bytes=24 * 2**20),
        cost_estimate=pl.CostEstimate(
            flops=20 * length * NS * chans,
            bytes_accessed=4 * length * chans * (NS + 5),
            transcendentals=length * NS * chans,
        ),
    )(x, dt, dy, in_sel, out_sel, a2, kept, end)


def mm(a, b):
    return jnp.dot(a, b, preferred_element_type=f32)


def mm_t(a, b):
    return lax.dot_general(a, b, (((1,), (1,)), ((), ())), preferred_element_type=f32)


def t_mm(a, b):
    return lax.dot_general(a, b, (((0,), (0,)), ((), ())), preferred_element_type=f32)


def norm_backward(values, inverse, gain_vec, upstream):
    scaled = upstream * gain_vec
    inner_mean = jnp.mean(values * scaled, axis=-1, keepdims=True)
    return inverse * scaled - values * (inverse * inverse * inverse) * inner_mean


def pad_to(x, axis, size):
    pads = [(0, 0)] * x.ndim
    pads[axis] = (0, size - x.shape[axis])
    return jnp.pad(x, pads)


def local(
    tokens,
    mixer_gain,
    in_weight,
    conv_weight,
    conv_bias,
    select_weight,
    step_weight,
    step_bias,
    decay_log,
    skip_weight,
    out_weight,
    expert_gain,
    router_weight,
    up_weight,
    down_weight,
    routes,
    lengths,
    cotangent,
):
    wide, narrow = lax.axis_size("wide"), lax.axis_size("narrow")
    w = lax.axis_index("wide")
    rows = tokens.shape[1]
    length = rows * wide
    chans = DI // wide
    wid = -(-chans // LANES) * LANES
    ff = FF // wide
    d_rows = D // (wide * narrow)
    c_rows = DI // (wide * narrow)
    f_rows = FF // (wide * narrow)
    sel_cols = DT_RANK + 2 * NS

    tokens_own = tokens[0].astype(f32)
    tokens_all = gather_wide(tokens[0])

    in_parts = in_weight.reshape(d_rows, 2, wide, chans).transpose(1, 2, 0, 3)
    gains = jnp.stack([mixer_gain, expert_gain], axis=1)
    gains = jnp.broadcast_to(gains[None], (wide, d_rows, 2))
    x_parts = exchange_wide(jnp.concatenate([in_parts[0], gains], axis=2))
    z_parts = exchange_wide(in_parts[1])
    x_full = gather_narrow(x_parts).transpose(1, 0, 2, 3).reshape(D, chans + 2)
    z_full = gather_narrow(z_parts).transpose(1, 0, 2, 3).reshape(D, chans)
    weight_x = pad_to(x_full[:, :chans], 1, wid)
    weight_z = pad_to(z_full, 1, wid)
    gain_one = x_full[:, chans].astype(f32)
    gain_two = x_full[:, chans + 1].astype(f32)

    channel_pack = jnp.concatenate(
        [
            conv_weight.T,
            conv_bias[:, None],
            step_bias[:, None],
            skip_weight[:, None],
            decay_log.T,
            step_weight.T,
            select_weight,
        ],
        axis=1,
    )
    packed = gather_narrow(channel_pack).reshape(chans, channel_pack.shape[1])
    packed = pad_to(packed, 0, wid)
    flat = packed[:, : CONV + 3 + NS].T.astype(f32)
    taps, conv_shift, step_shift, skip = flat[:CONV], flat[CONV], flat[CONV + 1], flat[CONV + 2]
    a_neg = -jnp.exp(flat[CONV + 3 :])
    a2 = a_neg * (1.0 / LN2)
    at = CONV + 3 + NS
    weight_step = packed[:, at : at + DT_RANK]
    weight_sel = pad_to(packed[:, at + DT_RANK :], 1, LANES)
    weight_out = pad_to(gather_narrow(out_weight).reshape(chans, D), 0, wid)

    up_parts = up_weight.reshape(EXPERTS, d_rows, wide, ff).transpose(2, 1, 0, 3)
    up_parts = up_parts.reshape(wide, d_rows, EXPERTS * ff)
    router_parts = jnp.broadcast_to(router_weight[None], (wide, d_rows, EXPERTS))
    up_parts = exchange_wide(jnp.concatenate([up_parts, router_parts], axis=2))
    up_full = gather_narrow(up_parts).transpose(1, 0, 2, 3).reshape(D, EXPERTS * ff + EXPERTS)
    up_cols = -(-(EXPERTS * ff + EXPERTS) // LANES) * LANES
    up_full = pad_to(up_full, 1, up_cols)
    down_full = gather_narrow(down_weight).transpose(1, 0, 2, 3).reshape(EXPERTS * ff, D)

    cot_ext = jnp.concatenate(
        [cotangent[0], pad_to(routes[0].astype(bf16)[:, None], 1, LANES)], axis=1
    )
    cot_all = gather_wide(cot_ext)
    second = cot_all[:, D : D + 1] > 0.5
    count = lengths[0]
    valid_all = jnp.arange(length)[:, None] < count
    up_low = jnp.where(valid_all, cot_all[:, :D], jnp.zeros((), bf16))
    valid_own = (w * rows + jnp.arange(rows))[:, None] < count
    upstream = jnp.where(valid_own, cotangent[0].astype(f32), 0.0)

    values = tokens_all.astype(f32)
    inverse_all = lax.rsqrt(jnp.mean(values * values, axis=-1, keepdims=True) + EPSILON)
    normed = (values * inverse_all * gain_one).astype(bf16)
    proj_x = mm(normed, weight_x)
    padded = jnp.concatenate([jnp.zeros((CONV - 1, wid), f32), proj_x], axis=0)
    conv_sum = conv_shift + sum(taps[k] * padded[k : k + length] for k in range(CONV))
    conv_gate = jax.nn.sigmoid(conv_sum)
    conv_act = (conv_sum * conv_gate).astype(bf16)
    selected = reduce_wide(mm(conv_act, weight_sel))
    proj_z = mm(normed, weight_z)
    step_low = selected[:, :DT_RANK]
    step_lin = mm_t(step_low, weight_step) + step_shift
    step_size = jax.nn.softplus(step_lin)
    turned = selected[:, DT_RANK:sel_cols].astype(f32).T
    in_sel, out_sel = turned[:NS], turned[NS:]
    scanned, kept, end = scan_forward(conv_act, step_size, in_sel, out_sel, a2)
    conv_full = conv_act.astype(f32)
    mixer_out = scanned + skip * conv_full
    z_gate = jax.nn.sigmoid(proj_z)
    silu_z = proj_z * z_gate
    gated = (mixer_out * silu_z).astype(bf16)
    hidden_one = tokens_own + scatter_wide(mm(gated, weight_out).astype(bf16))
    inverse_two = lax.rsqrt(jnp.mean(hidden_one * hidden_one, axis=-1, keepdims=True) + EPSILON)
    normed_two = gather_wide((hidden_one * inverse_two * gain_two).astype(bf16))

    raised = mm(normed_two, up_full)
    logits = raised[:, EXPERTS * ff : EXPERTS * ff + EXPERTS]
    probs = jax.nn.softmax(logits, axis=-1)
    onehot = jnp.concatenate([~second, second], axis=1).astype(f32)
    gate = jnp.sum(probs * onehot, axis=-1, keepdims=True)
    pre = jnp.where(second, raised[:, ff : 2 * ff], raised[:, :ff])
    bell = (1.0 + lax.erf(pre * (1.0 / math.sqrt(2.0)))) * 0.5
    hidden = (pre * bell).astype(bf16)
    slope = bell + pre * jnp.exp(-0.5 * pre * pre) * (1.0 / math.sqrt(2.0 * math.pi))
    zero = jnp.zeros((), bf16)

    def split(v):
        return [jnp.where(second, zero, v), jnp.where(second, v, zero)]

    hidden_both = jnp.concatenate(split(hidden), axis=1)
    expert_part = mm(hidden_both, down_full).astype(bf16)

    lowered = mm_t(up_low, down_full)
    d_hid = jnp.where(second, lowered[:, ff:], lowered[:, :ff])
    d_gate = jnp.sum(hidden.astype(f32) * d_hid, axis=-1, keepdims=True)
    d_pre = (gate * d_hid * slope).astype(bf16)
    d_logits = (probs * d_gate * (onehot - gate)).astype(bf16)
    d_both = pad_to(jnp.concatenate(split(d_pre) + [d_logits], axis=1), 1, up_cols)
    d_normed_two = scatter_wide(mm_t(d_both, up_full).astype(bf16))
    expert_out = scatter_wide(expert_part)
    gate_own = lax.dynamic_slice_in_dim(gate, w * rows, rows, 0)
    output = (hidden_one + gate_own * expert_out).astype(bf16)
    d_hidden_one = upstream + norm_backward(hidden_one, inverse_two, gain_two, d_normed_two)
    d_mix = gather_wide(d_hidden_one.astype(bf16))

    d_expert = (gate * up_low.astype(f32)).astype(bf16)
    grad_down = t_mm(hidden_both, d_expert).astype(bf16)
    grad_down = grad_down.reshape(EXPERTS, narrow, f_rows, D).transpose(1, 0, 2, 3)
    grad_down = scatter_narrow(grad_down)
    grad_up = t_mm(normed_two, d_both)[:, : EXPERTS * ff + EXPERTS].astype(bf16)
    grad_up = grad_up.reshape(wide, narrow, d_rows, EXPERTS * ff + EXPERTS).transpose(1, 0, 2, 3)
    grad_up = exchange_wide(scatter_narrow(grad_up).astype(bf16)).astype(f32)
    grad_router = jnp.sum(grad_up[:, :, EXPERTS * ff :], axis=0)
    grad_up = grad_up[:, :, : EXPERTS * ff].reshape(wide, d_rows, EXPERTS, ff)
    grad_up = grad_up.transpose(2, 1, 0, 3).reshape(EXPERTS, d_rows, FF)
    grad_gain_two = (
        jnp.sum(up_weight.astype(f32) * grad_up, axis=(0, 2))
        + jnp.sum(router_weight.astype(f32) * grad_router, axis=1)
    ) / expert_gain.astype(f32)

    d_gated = mm_t(d_mix, weight_out)
    grad_out = t_mm(gated, d_mix).astype(bf16)[:chans].reshape(narrow, c_rows, D)
    grad_out = scatter_narrow(grad_out)
    d_mixer = d_gated * silu_z
    d_z = (d_gated * mixer_out * (z_gate * (1.0 + proj_z * (1.0 - z_gate)))).astype(bf16)
    grad_skip = jnp.sum(d_mixer * conv_full, axis=0)
    d_step, d_conv_scan, d_in, d_out, d_a = scan_backward(
        conv_act, step_size, d_mixer, in_sel, out_sel, a2, kept, end
    )
    grad_decay = d_a * a_neg
    step_grad = d_step * jax.nn.sigmoid(step_lin)
    grad_step_bias = jnp.sum(step_grad, axis=0)
    step_grad_low = step_grad.astype(bf16)
    d_sel = jnp.concatenate([mm(step_grad_low, weight_step), d_in.T, d_out.T], axis=1)
    d_sel = reduce_wide(pad_to(d_sel, 1, LANES))
    grad_step = t_mm(step_grad_low, step_low)
    grad_sel = t_mm(conv_act, d_sel)[:, :sel_cols]
    d_act = mm_t(d_sel, weight_sel) + skip * d_mixer + d_conv_scan
    d_conv = d_act * (conv_gate * (1.0 + conv_sum * (1.0 - conv_gate)))
    grad_conv_bias = jnp.sum(d_conv, axis=0)
    grad_conv = jnp.stack(
        [jnp.sum(d_conv * padded[k : k + length], axis=0) for k in range(CONV)], axis=1
    )
    d_ext = jnp.concatenate([d_conv, jnp.zeros((CONV - 1, wid), f32)], axis=0)
    d_x = sum(taps[k] * d_ext[CONV - 1 - k : CONV - 1 - k + length] for k in range(CONV))
    d_x = d_x.astype(bf16)
    d_normed = scatter_wide((mm_t(d_x, weight_x) + mm_t(d_z, weight_z)).astype(bf16))
    inverse_one = lax.rsqrt(jnp.mean(tokens_own * tokens_own, axis=-1, keepdims=True) + EPSILON)
    token_grad = d_hidden_one + norm_backward(tokens_own, inverse_one, gain_one, d_normed)

    def in_grad(d_part):
        grad = t_mm(normed, d_part)[:, :chans].astype(bf16)
        grad = grad.reshape(wide, narrow, d_rows, chans).transpose(1, 0, 2, 3)
        grad = exchange_wide(scatter_narrow(grad).astype(bf16))
        return grad.astype(f32).transpose(1, 0, 2).reshape(d_rows, DI)

    grad_in = jnp.concatenate([in_grad(d_x), in_grad(d_z)], axis=1)
    grad_gain_one = jnp.sum(in_weight.astype(f32) * grad_in, axis=1) / mixer_gain.astype(f32)

    channel_grads = jnp.concatenate(
        [
            grad_conv,
            grad_conv_bias[:, None],
            grad_step_bias[:, None],
            grad_skip[:, None],
            grad_decay.T,
            grad_step,
            grad_sel,
        ],
        axis=1,
    ).astype(bf16)
    channel_grads = channel_grads[:chans].reshape(narrow, c_rows, channel_grads.shape[1])
    channel_grads = scatter_narrow(channel_grads)
    flat_grads = channel_grads[:, :at].T
    return (
        output[None],
        token_grad[None],
        grad_gain_one,
        grad_in,
        flat_grads[:CONV],
        flat_grads[CONV],
        channel_grads[:, at + DT_RANK :],
        channel_grads[:, at : at + DT_RANK].T,
        flat_grads[CONV + 1],
        flat_grads[CONV + 3 :],
        flat_grads[CONV + 2],
        grad_out,
        grad_gain_two,
        grad_router,
        grad_up,
        grad_down,
    )


def solution(mesh):
    both = ("wide", "narrow")
    return jax.shard_map(
        local,
        mesh=mesh,
        in_specs=(
            P("narrow", "wide", None),
            P(both),
            P(both, None),
            P(None, both),
            P(both),
            P(both, None),
            P(None, both),
            P(both),
            P(None, both),
            P(both),
            P(both, None),
            P(both),
            P(both, None),
            P(None, both, None),
            P(None, both, None),
            P("narrow", "wide"),
            P("narrow"),
            P("narrow", "wide", None),
        ),
        out_specs=(
            P("narrow", "wide", None),
            P("narrow", "wide", None),
            P(both),
            P(both, None),
            P(None, both),
            P(both),
            P(both, None),
            P(None, both),
            P(both),
            P(None, both),
            P(both),
            P(both, None),
            P(both),
            P(both, None),
            P(None, both, None),
            P(None, both, None),
        ),
        check_vma=False,
    )
```

time: 7440 us -> 1100 us (0.15)
  local copies, waits for them, and re-layouts: 3720 us -> 427 us
  other arithmetic: 1600 us -> 86.8 us
  blocking collectives: 1170 us -> 0 us
  waiting for transfers between devices: 581 us -> 180 us
  starting transfers between devices: 14 us -> 183 us
  Pallas kernels: 0 us -> 114 us
  matrix products: 197 us -> 87.7 us
    pad x376 -> x1, local copies, waits for them, and re-layouts: 2890 us -> 1.15 us  [pad_to(): return jnp.pad(x, pads)]
    unnamed x2 -> x0, blocking collectives: 812 us -> none
    mul x162 -> x1, other arithmetic: 530 us -> 0.01 us  [local(): a2 = a_neg * (1.0 / LN2)]
    while x989 -> x0, local copies, waits for them, and re-layouts: 399 us -> none
    add x150 -> x8, other arithmetic: 406 us -> 19.3 us  [the longest x4 12 us: summed(): return pick(own, chip ^ q).astype(f32) + pick(other, chip ^ q).astype(f32)]
    all_gather x7 -> x0, blocking collectives: 358 us -> none  [the longest x1 70.2 us: local(): lax.all_gather(step_weight, ('wide', 'narrow'), axis=1, tiled=True)]
    unnamed x19 -> x0, waiting for transfers between devices: 313 us -> none
    reduce_scatter x1 -> x0, waiting for transfers between devices: 268 us -> none  [local(): lax.psum_scatter(grad_down, ('wide', 'narrow'), scatter_dimension=1, tile...]
  transfers between devices with their start and end apart: 17 -> 112, of which waited for: 7 -> 38; matrix products, arithmetic and copies ran while one was open for 42% -> 48% of each run, Pallas kernels for 0% -> 11%
where the time goes in v1:
time: 1100 us; the launch traced here: 1080 us
  local copies, waits for them, and re-layouts  427 us (39%)
  starting transfers between devices  183 us (17%)
  waiting for transfers between devices  180 us (16%)
  Pallas kernels  114 us (10%)
  matrix products  87.7 us (8%)
  other arithmetic  86.8 us (8%)
    dynamic_update_slice x14, local copies, waits for them, and re-layouts, gather_wide(): out = lax.dynamic_update_index_in_dim(out, mine[q], at + core, 0)  121 us
    dynamic_update_slice x16, local copies, waits for them, and re-layouts, gather_wide(): out = lax.dynamic_update_index_in_dim(out, theirs[q], at + 1 - core, 0)  119 us
    ppermute x36, starting transfers between devices, turn(): return lax.ppermute(x, 'narrow', [(i, (i + k) % n) for i in range(n)])  98.3 us
    pallas_call x1, Pallas kernels, scan_backward(): pl.pallas_call(scan_backward_kernel, grid=(n,), in_specs=[row, row, row,...  87.6 us
    ppermute x70, waiting for transfers between devices, swap(): return lax.ppermute(x, 'wide', [(i, i ^ k) for i in range(n)])  86.9 us
    ppermute x36, waiting for transfers between devices, turn(): return lax.ppermute(x, 'narrow', [(i, (i + k) % n) for i in range(n)])  82.6 us
    ppermute x70, starting transfers between devices, swap(): return lax.ppermute(x, 'wide', [(i, i ^ k) for i in range(n)])  61.1 us
    dot_general x7, matrix products, mm_t(): lax.dot_general(a, b, (((1,), (1,)), ((), ())), preferred_element_type=f32)  35.6 us
  transfers between devices with their start and end apart: 112, of which 38 were waited for; matrix products, arithmetic and copies ran while one was open for 48% of the time, Pallas kernels for 11%

profile of v1, /device:TPU:0, one launch (start us, length us, event | category | flops | bytes accessed | tf_op | source)
XLA Modules:
  0.0 1082.3 jit_solution(16768307977264326309)
XLA Ops:
  39.4 28.2 %dynamic_update_slice.215 = bf16[8,256,1280]{1,0,2:T(8,128)(2,1)} dynamic-update-slice(bf16[8,256,1280]{1,0,2:T(8,128)(2,1)} %broadcast_in_dim.355, bf16[1,256,1280]{1,0,2:T(2,128)(2,1)S(1)} %copy.450, s32[]{:T(128)S(6)} %select_n.366, s32[]{:T(128)} %constant.803.clone.1, s32[]{:T(128)} %constant.803.clone.1) | dynamic-update-slice | bytes 1310724 | tf_op jit(solution)/shard_map/jit(dynamic_update_index_in_dim)/dynamic_update_slice | solution.py:61
  94.5 7.7 collective-permute-done.11
  103.6 11.7 %collective-permute-done.12 = bf16[8,36,290]{2,1,0:T(8,128)(2,1)S(1)} collective-permute-done((bf16[8,36,290]{2,1,0:T(8,128)(2,1)S(1)}, bf16[8,36,290]{2,1,0:T(8,128)(2,1)S(1)}, u32[]{:S(2)}, u32[]{:S(2)}) %collective-permute-start.12) | collective-permute-done | bytes 167072 | tf_op jit(solution)/shard_map/ppermute | solution.py:34
  182.5 10.7 collective-permute-done.21
  202.4 9.3 dynamic_update_slice.205
  213.6 9.4 dynamic_update_slice.206
  227.9 26.6 %shard_map.297 = (f32[2048,384]{1,0:T(8,128)S(1)}, f32[2048,16,384]{2,1,0:T(8,128)}, f32[16,384]{1,0:T(8,128)S(1)}) custom-call(bf16[2048,384]{1,0:T(8,128)(2,1)S(1)} %get-tuple-element.183.x_ref, f32[2048,384]{1,0:T(8,128)S(1)} %get-tuple-element.239.dt_ref, f32[16,2048]{1,0:T(8,128)S(1)} %get-tuple-element.230.b_ref, ...), custom_call_target="tpu_custom_call" | custom-call | flops 100663296 | bytes 59768832 | tf_op jit(solution)/shard_map/pallas_call | solution.py:160
  277.7 14.7 %collective-permute-done.53 = bf16[2,96,1152]{2,1,0:T(8,128)(2,1)S(1)} collective-permute-done((bf16[2,96,1152]{2,1,0:T(8,128)(2,1)}, bf16[2,96,1152]{2,1,0:T(8,128)(2,1)S(1)}, u32[]{:S(2)}, u32[]{:S(2)}) %collective-permute-start.53) | collective-permute-done | bytes 442400 | tf_op jit(solution)/shard_map/ppermute | solution.py:34
  305.5 28.3 %dynamic_update_slice.216 = bf16[8,256,1280]{1,0,2:T(8,128)(2,1)} dynamic-update-slice(bf16[8,256,1280]{1,0,2:T(8,128)(2,1)} %dynamic_update_slice.215, bf16[1,256,1280]{1,0,2:T(2,128)(2,1)} %copy.451, s32[]{:T(128)S(6)} %select_n.367, s32[]{:T(128)} %constant.803.clone.1, s32[]{:T(128)} %constant.803.clone.1) | dynamic-update-slice | bytes 1310724 | tf_op jit(solution)/shard_map/jit(dynamic_update_index_in_dim)/dynamic_update_slice | solution.py:62
  333.8 28.3 %dynamic_update_slice.217 = bf16[8,256,1280]{1,0,2:T(8,128)(2,1)} dynamic-update-slice(bf16[8,256,1280]{1,0,2:T(8,128)(2,1)} %dynamic_update_slice.216, bf16[1,256,1280]{1,0,2:T(2,128)(2,1)} %copy.452, s32[]{:T(128)S(6)} %select_n.368, s32[]{:T(128)} %constant.803.clone.1, s32[]{:T(128)} %constant.803.clone.1) | dynamic-update-slice | bytes 1310724 | tf_op jit(solution)/shard_map/jit(dynamic_update_index_in_dim)/dynamic_update_slice | solution.py:61
  391.0 28.3 %dynamic_update_slice.218 = bf16[8,256,1280]{1,0,2:T(8,128)(2,1)} dynamic-update-slice(bf16[8,256,1280]{1,0,2:T(8,128)(2,1)} %dynamic_update_slice.217, bf16[1,256,1280]{1,0,2:T(2,128)(2,1)} %copy.453, s32[]{:T(128)S(6)} %select_n.369, s32[]{:T(128)} %constant.803.clone.1, s32[]{:T(128)} %constant.803.clone.1) | dynamic-update-slice | bytes 1310724 | tf_op jit(solution)/shard_map/jit(dynamic_update_index_in_dim)/dynamic_update_slice | solution.py:62
  419.3 28.3 %dynamic_update_slice.219 = bf16[8,256,1280]{1,0,2:T(8,128)(2,1)} dynamic-update-slice(bf16[8,256,1280]{1,0,2:T(8,128)(2,1)} %dynamic_update_slice.218, bf16[1,256,1280]{1,0,2:T(2,128)(2,1)} %copy.454, s32[]{:T(128)S(6)} %select_n.370, s32[]{:T(128)} %constant.803.clone.1, s32[]{:T(128)} %constant.803.clone.1) | dynamic-update-slice | bytes 1310724 | tf_op jit(solution)/shard_map/jit(dynamic_update_index_in_dim)/dynamic_update_slice | solution.py:61
  447.6 28.3 %dynamic_update_slice.220 = bf16[8,256,1280]{1,0,2:T(8,128)(2,1)} dynamic-update-slice(bf16[8,256,1280]{1,0,2:T(8,128)(2,1)} %dynamic_update_slice.219, bf16[1,256,1280]{1,0,2:T(2,128)(2,1)} %copy.455, s32[]{:T(128)S(6)} %select_n.371, s32[]{:T(128)} %constant.803.clone.1, s32[]{:T(128)} %constant.803.clone.1) | dynamic-update-slice | bytes 1310724 | tf_op jit(solution)/shard_map/jit(dynamic_update_index_in_dim)/dynamic_update_slice | solution.py:62
  475.9 28.3 %dynamic_update_slice.221 = bf16[8,256,1280]{1,0,2:T(8,128)(2,1)} dynamic-update-slice(bf16[8,256,1280]{1,0,2:T(8,128)(2,1)} %dynamic_update_slice.220, bf16[1,256,1280]{1,0,2:T(2,128)(2,1)} %copy.456, s32[]{:T(128)S(6)} %select_n.372, s32[]{:T(128)} %constant.803.clone.1, s32[]{:T(128)} %constant.803.clone.1) | dynamic-update-slice | bytes 1310724 | tf_op jit(solution)/shard_map/jit(dynamic_update_index_in_dim)/dynamic_update_slice | solution.py:61
  508.0 28.3 %dynamic_update_slice.222 = bf16[8,256,1280]{1,0,2:T(8,128)(2,1)} dynamic-update-slice(bf16[8,256,1280]{1,0,2:T(8,128)(2,1)} %dynamic_update_slice.221, bf16[1,256,1280]{1,0,2:T(2,128)(2,1)} %copy.457, s32[]{:T(128)S(6)} %select_n.373, s32[]{:T(128)} %constant.803.clone.1, s32[]{:T(128)} %constant.803.clone.1) | dynamic-update-slice | bytes 1310724 | tf_op jit(solution)/shard_map/jit(dynamic_update_index_in_dim)/dynamic_update_slice | solution.py:62
  545.4 8.0 fusion.10
  616.5 6.7 multiply_reduce_fusion.5
  623.1 6.3 broadcast_select_fusion.1
  633.2 7.6 fusion.130
  640.8 7.2 convolution_convert_fusion
  667.7 6.7 fusion.11
  674.4 6.6 convolution_convert_fusion.1
  684.2 14.0 %collective-permute-start.104 = (bf16[2,96,1152]{2,1,0:T(8,128)(2,1)}, bf16[2,96,1152]{2,1,0:T(8,128)(2,1)}, u32[]{:S(2)}, u32[]{:S(2)}) collective-permute-start(bf16[2,96,1152]{2,1,0:T(8,128)(2,1)} %get-tuple-element.205), channel_id=1, source_target_pairs={{0,2},{1,3},{2,0},{3,1},{4,6},{5,7},{6,4},{7,5},{8,10},{9,11},{10,... | collective-permute-start | bytes 1327112 | tf_op jit(solution)/shard_map/ppermute | solution.py:34
  698.6 21.1 %collective-permute-start.105 = (bf16[2,96,1152]{2,1,0:T(8,128)(2,1)}, bf16[2,96,1152]{2,1,0:T(8,128)(2,1)}, u32[]{:S(2)}, u32[]{:S(2)}) collective-permute-start(bf16[2,96,1152]{2,1,0:T(8,128)(2,1)} %get-tuple-element.204), channel_id=1, source_target_pairs={{0,3},{1,0},{2,1},{3,2},{4,7},{5,4},{6,5},{7,6},{8,11},{9,8},{10,9... | collective-permute-start | bytes 1327112 | tf_op jit(solution)/shard_map/ppermute | solution.py:34
  726.4 11.3 %collective-permute-done.104 = bf16[2,96,1152]{2,1,0:T(8,128)(2,1)} collective-permute-done((bf16[2,96,1152]{2,1,0:T(8,128)(2,1)}, bf16[2,96,1152]{2,1,0:T(8,128)(2,1)}, u32[]{:S(2)}, u32[]{:S(2)}) %collective-permute-start.104) | collective-permute-done | bytes 442400 | tf_op jit(solution)/shard_map/ppermute | solution.py:34
  764.3 11.3 %collective-permute-done.58 = bf16[128,1152]{1,0:T(8,128)(2,1)S(1)} collective-permute-done((bf16[128,1152]{1,0:T(8,128)(2,1)S(1)}, bf16[128,1152]{1,0:T(8,128)(2,1)S(1)}, u32[]{:S(2)}, u32[]{:S(2)}) %collective-permute-start.58) | collective-permute-done | bytes 294944 | tf_op jit(solution)/shard_map/ppermute | solution.py:29
  780.4 6.5 collective-permute-done.64
  821.4 10.3 collective-permute-start.97
  831.8 5.7 fusion.13
  837.5 87.6 %shard_map.298 = (f32[2048,384]{1,0:T(8,128)S(1)}, f32[2048,384]{1,0:T(8,128)S(1)}, f32[16,2048]{1,0:T(8,128)S(1)}, f32[16,2048]{1,0:T(8,128)S(1)}, f32[16,384]{1,0:T(8,128)S(1)}) custom-call(bf16[2048,384]{1,0:T(8,128)(2,1)S(1)} %get-tuple-element.183.x_ref, f32[2048,384]{1,0:T(8,128)S(1)} %copy-done.1, f32[2048,384]{1,0:T(8,128)S(1)} %get-tuple-element.164.dy_ref, ...), custom_call_target="tpu_custom_call" | custom-call | flops 251658240 | bytes 66060288 | tf_op jit(solution)/shard_map/pallas_call | solution.py:269
  1026.2 6.9 collective-permute-done.88
  1033.0 8.0 collective-permute-done.89
  (684 shorter events, 530.3 us)
Async XLA Ops:
  0.7 129.2 %collective-permute-start.3 = (bf16[256,1152]{1,0:T(8,128)(2,1)}, bf16[256,1152]{1,0:T(8,128)(2,1)}, u32[]{:S(2)}, u32[]{:S(2)}) collective-permute-start(bf16[256,1152]{1,0:T(8,128)(2,1)} %bitcast.483), channel_id=1, source_target_pairs={{0,4},{4,0},{8,12},{12,8},{16,20},{20,16},{24,28},{28,24},{1,5},{5... | collective-permute-start | bytes 1769480 | tf_op jit(solution)/shard_map/ppermute | solution.py:29
  1.2 123.6 %collective-permute-start.4 = (bf16[256,1152]{1,0:T(8,128)(2,1)}, bf16[256,1152]{1,0:T(8,128)(2,1)}, u32[]{:S(2)}, u32[]{:S(2)}) collective-permute-start(bf16[256,1152]{1,0:T(8,128)(2,1)} %bitcast.484), channel_id=1, source_target_pairs={{0,8},{4,12},{8,0},{12,4},{16,24},{20,28},{24,16},{28,20},{1,9},{5... | collective-permute-start | bytes 1769480 | tf_op jit(solution)/shard_map/ppermute | solution.py:29
  3.8 123.6 %collective-permute-start.6 = (bf16[256,1152]{1,0:T(8,128)(2,1)}, bf16[256,1152]{1,0:T(8,128)(2,1)}, u32[]{:S(2)}, u32[]{:S(2)}) collective-permute-start(bf16[256,1152]{1,0:T(8,128)(2,1)} %bitcast.485), channel_id=1, source_target_pairs={{0,16},{4,20},{8,24},{12,28},{16,0},{20,4},{24,8},{28,12},{1,17},{... | collective-permute-start | bytes 1769480 | tf_op jit(solution)/shard_map/ppermute | solution.py:29
  10.8 56.7 %collective-permute-start = (bf16[72,199]{1,0:T(8,128)(2,1)S(1)}, bf16[72,199]{1,0:T(8,128)(2,1)S(1)}, u32[]{:S(2)}, u32[]{:S(2)}) collective-permute-start(bf16[72,199]{1,0:T(8,128)(2,1)S(1)} %concatenate.185), channel_id=1, source_target_pairs={{0,1},{1,2},{2,3},{3,0},{4,5},{5,6},{6,7},{7,4},{8,9},{9,10},{10,1... | collective-permute-start | bytes 85976 | tf_op jit(solution)/shard_map/ppermute | solution.py:34
  12.5 56.4 %collective-permute-start.1 = (bf16[72,199]{1,0:T(8,128)(2,1)S(1)}, bf16[72,199]{1,0:T(8,128)(2,1)S(1)}, u32[]{:S(2)}, u32[]{:S(2)}) collective-permute-start(bf16[72,199]{1,0:T(8,128)(2,1)S(1)} %concatenate.185), channel_id=1, source_target_pairs={{0,2},{1,3},{2,0},{3,1},{4,6},{5,7},{6,4},{7,5},{8,10},{9,11},{10,... | collective-permute-start | bytes 85976 | tf_op jit(solution)/shard_map/ppermute | solution.py:34
  17.5 54.7 %all-to-all-start.1 = ((bf16[8,36,288]{2,1,0:T(8,128)(2,1)}), bf16[8,36,288]{2,1,0:T(8,128)(2,1)}, u32[]{:S(2)}, u32[]{:S(2)}) async-start(bf16[8,36,288]{2,1,0:T(8,128)(2,1)} %get-tuple-element.227), calls=%async_computation.1 | async-start | bytes 491520 | tf_op jit(solution)/shard_map/all_to_all | solution.py:127
  83.0 111.6 %all-to-all-start.2 = ((bf16[8,36,770]{2,1,0:T(8,128)(2,1)}), bf16[8,36,770]{2,1,0:T(8,128)(2,1)}, u32[]{:S(2)}, u32[]{:S(2)}) async-start(bf16[8,36,770]{2,1,0:T(8,128)(2,1)} %copy.460), calls=%async_computation.2 | async-start | bytes 1146880 | tf_op jit(solution)/shard_map/all_to_all | solution.py:127
  87.4 73.2 %collective-permute-start.24 = (bf16[72,1152]{1,0:T(8,128)(2,1)}, bf16[72,1152]{1,0:T(8,128)(2,1)}, u32[]{:S(2)}, u32[]{:S(2)}) collective-permute-start(bf16[72,1152]{1,0:T(8,128)(2,1)} %param.28), channel_id=1, source_target_pairs={{0,3},{1,0},{2,1},{3,2},{4,7},{5,4},{6,5},{7,6},{8,11},{9,8},{10,9... | collective-permute-start | bytes 497672 | tf_op jit(solution)/shard_map/ppermute | solution.py:34
  123.9 169.3 %collective-permute-start.32 = (bf16[256,1280]{1,0:T(8,128)(2,1)}, bf16[256,1280]{1,0:T(8,128)(2,1)}, u32[]{:S(2)}, u32[]{:S(2)}) collective-permute-start(bf16[256,1280]{1,0:T(8,128)(2,1)} %get-tuple-element.217), channel_id=1, source_target_pairs={{0,4},{4,0},{8,12},{12,8},{16,20},{20,16},{24,28},{28,24},{1,5},{5... | collective-permute-start | bytes 1966088 | tf_op jit(solution)/shard_map/ppermute | solution.py:29
  135.3 30.0 %collective-permute-start.19 = (bf16[8,36,288]{2,1,0:T(8,128)(2,1)}, bf16[8,36,288]{2,1,0:T(8,128)(2,1)S(1)}, u32[]{:S(2)}, u32[]{:S(2)}) collective-permute-start(bf16[8,36,288]{2,1,0:T(8,128)(2,1)} %all-to-all-done.1), channel_id=1, source_target_pairs={{0,1},{1,2},{2,3},{3,0},{4,5},{5,6},{6,7},{7,4},{8,9},{9,10},{10,1... | collective-permute-start | bytes 497672 | tf_op jit(solution)/shard_map/ppermute | solution.py:34
  165.9 106.2 %collective-permute-start.33 = (bf16[256,1280]{1,0:T(8,128)(2,1)}, bf16[256,1280]{1,0:T(8,128)(2,1)}, u32[]{:S(2)}, u32[]{:S(2)}) collective-permute-start(bf16[256,1280]{1,0:T(8,128)(2,1)} %get-tuple-element.217), channel_id=1, source_target_pairs={{0,8},{4,12},{8,0},{12,4},{16,24},{20,28},{24,16},{28,20},{1,9},{5... | collective-permute-start | bytes 1966088 | tf_op jit(solution)/shard_map/ppermute | solution.py:29
  171.5 102.7 %collective-permute-start.35 = (bf16[256,1280]{1,0:T(8,128)(2,1)}, bf16[256,1280]{1,0:T(8,128)(2,1)}, u32[]{:S(2)}, u32[]{:S(2)}) collective-permute-start(bf16[256,1280]{1,0:T(8,128)(2,1)} %get-tuple-element.217), channel_id=1, source_target_pairs={{0,16},{4,20},{8,24},{12,28},{16,0},{20,4},{24,8},{28,12},{1,17},{... | collective-permute-start | bytes 1966088 | tf_op jit(solution)/shard_map/ppermute | solution.py:29
  177.7 86.5 %collective-permute-start.51 = (bf16[2,96,1152]{2,1,0:T(8,128)(2,1)}, bf16[2,96,1152]{2,1,0:T(8,128)(2,1)}, u32[]{:S(2)}, u32[]{:S(2)}) collective-permute-start(bf16[2,96,1152]{2,1,0:T(8,128)(2,1)} %param.32), channel_id=1, source_target_pairs={{0,1},{1,2},{2,3},{3,0},{4,5},{5,6},{6,7},{7,4},{8,9},{9,10},{10,1... | collective-permute-start | bytes 1327112 | tf_op jit(solution)/shard_map/ppermute | solution.py:34
  211.7 54.8 %collective-permute-start.52 = (bf16[2,96,1152]{2,1,0:T(8,128)(2,1)}, bf16[2,96,1152]{2,1,0:T(8,128)(2,1)}, u32[]{:S(2)}, u32[]{:S(2)}) collective-permute-start(bf16[2,96,1152]{2,1,0:T(8,128)(2,1)} %param.32), channel_id=1, source_target_pairs={{0,2},{1,3},{2,0},{3,1},{4,6},{5,7},{6,4},{7,5},{8,10},{9,11},{10,... | collective-permute-start | bytes 1327112 | tf_op jit(solution)/shard_map/ppermute | solution.py:34
  264.1 276.9 %collective-permute-start.25 = (bf16[4,256,1152]{2,1,0:T(8,128)(2,1)}, bf16[4,256,1152]{2,1,0:T(8,128)(2,1)}, u32[]{:S(2)}, u32[]{:S(2)}) collective-permute-start(bf16[4,256,1152]{2,1,0:T(8,128)(2,1)} %dynamic-slice_bitcast_fusion.3), channel_id=1, source_target_pairs={{0,4},{4,0},{8,12},{12,8},{16,20},{20,16},{24,28},{28,24},{1,5},{5... | collective-permute-start | bytes 7077896 | tf_op jit(solution)/shard_map/ppermute | solution.py:29
  272.1 95.6 %collective-permute-start.48 = (bf16[8,36,770]{2,0,1:T(8,128)(2,1)S(1)}, bf16[8,36,770]{2,0,1:T(8,128)(2,1)}, u32[]{:S(2)}, u32[]{:S(2)}) collective-permute-start(bf16[8,36,770]{2,0,1:T(8,128)(2,1)S(1)} %copy-done.62), channel_id=1, source_target_pairs={{0,1},{1,2},{2,3},{3,0},{4,5},{5,6},{6,7},{7,4},{8,9},{9,10},{10,1... | collective-permute-start | bytes 1330568 | tf_op jit(solution)/shard_map/ppermute | solution.py:34
  274.2 87.9 %collective-permute-start.37 = (bf16[128,1280]{1,0:T(8,128)(2,1)}, bf16[128,1280]{1,0:T(8,128)(2,1)}, u32[]{:S(2)}, u32[]{:S(2)}) collective-permute-start(bf16[128,1280]{1,0:T(8,128)(2,1)} %slice.372), channel_id=1, source_target_pairs={{0,16},{4,20},{8,24},{12,28},{16,0},{20,4},{24,8},{28,12},{1,17},{... | collective-permute-start | bytes 983048 | tf_op jit(solution)/shard_map/ppermute | solution.py:29
  292.5 74.1 %collective-permute-start.38 = (bf16[128,1280]{1,0:T(8,128)(2,1)}, bf16[128,1280]{1,0:T(8,128)(2,1)}, u32[]{:S(2)}, u32[]{:S(2)}) collective-permute-start(bf16[128,1280]{1,0:T(8,128)(2,1)} %slice.373), channel_id=1, source_target_pairs={{0,8},{4,12},{8,0},{12,4},{16,24},{20,28},{24,16},{28,20},{1,9},{5... | collective-permute-start | bytes 983048 | tf_op jit(solution)/shard_map/ppermute | solution.py:29
  293.3 75.0 %collective-permute-start.49 = (bf16[8,36,770]{2,0,1:T(8,128)(2,1)S(1)}, bf16[8,36,770]{2,0,1:T(8,128)(2,1)}, u32[]{:S(2)}, u32[]{:S(2)}) collective-permute-start(bf16[8,36,770]{2,0,1:T(8,128)(2,1)S(1)} %copy-done.62), channel_id=1, source_target_pairs={{0,2},{1,3},{2,0},{3,1},{4,6},{5,7},{6,4},{7,5},{8,10},{9,11},{10,... | collective-permute-start | bytes 1330568 | tf_op jit(solution)/shard_map/ppermute | solution.py:34
  368.2 135.9 %collective-permute-start.39 = (bf16[256,1280]{1,0:T(8,128)(2,1)S(1)}, bf16[256,1280]{1,0:T(8,128)(2,1)}, u32[]{:S(2)}, u32[]{:S(2)}) collective-permute-start(bf16[256,1280]{1,0:T(8,128)(2,1)S(1)} %constant_dynamic-update-slice_fusion.3), channel_id=1, source_target_pairs={{0,4},{4,0},{8,12},{12,8},{16,20},{20,16},{24,28},{28,24},{1,5},{5... | collective-permute-start | bytes 1966088 | tf_op jit(solution)/shard_map/ppermute | solution.py:29
  660.5 38.1 %collective-permute-start.101 = (bf16[8,36,770]{2,0,1:T(8,128)(2,1)S(1)}, bf16[8,36,770]{2,0,1:T(8,128)(2,1)S(1)}, u32[]{:S(2)}, u32[]{:S(2)}) collective-permute-start(bf16[8,36,770]{2,0,1:T(8,128)(2,1)S(1)} %bitcast.559), channel_id=1, source_target_pairs={{0,2},{1,3},{2,0},{3,1},{4,6},{5,7},{6,4},{7,5},{8,10},{9,11},{10,... | collective-permute-start | bytes 1330568 | tf_op jit(solution)/shard_map/ppermute | solution.py:34
  667.7 82.0 %collective-permute-start.61 = (bf16[4,256,1152]{2,1,0:T(8,128)(2,1)}, bf16[4,256,1152]{2,1,0:T(8,128)(2,1)}, u32[]{:S(2)}, u32[]{:S(2)}) collective-permute-start(bf16[4,256,1152]{2,1,0:T(8,128)(2,1)} %dynamic-slice_bitcast_fusion.1), channel_id=1, source_target_pairs={{0,4},{4,0},{8,12},{12,8},{16,20},{20,16},{24,28},{28,24},{1,5},{5... | collective-permute-start | bytes 7077896 | tf_op jit(solution)/shard_map/ppermute | solution.py:29
  681.0 40.2 %collective-permute-start.102 = (bf16[8,36,770]{2,0,1:T(8,128)(2,1)S(1)}, bf16[8,36,770]{2,0,1:T(8,128)(2,1)S(1)}, u32[]{:S(2)}, u32[]{:S(2)}) collective-permute-start(bf16[8,36,770]{2,0,1:T(8,128)(2,1)S(1)} %bitcast.561), channel_id=1, source_target_pairs={{0,3},{1,0},{2,1},{3,2},{4,7},{5,4},{6,5},{7,6},{8,11},{9,8},{10,9... | collective-permute-start | bytes 1330568 | tf_op jit(solution)/shard_map/ppermute | solution.py:34
  682.4 44.0 %collective-permute-start.103 = (bf16[2,96,1152]{2,1,0:T(8,128)(2,1)}, bf16[2,96,1152]{2,1,0:T(8,128)(2,1)}, u32[]{:S(2)}, u32[]{:S(2)}) collective-permute-start(bf16[2,96,1152]{2,1,0:T(8,128)(2,1)} %get-tuple-element.203), channel_id=1, source_target_pairs={{0,1},{1,2},{2,3},{3,0},{4,5},{5,6},{6,7},{7,4},{8,9},{9,10},{10,1... | collective-permute-start | bytes 1327112 | tf_op jit(solution)/shard_map/ppermute | solution.py:34
  684.2 53.4 %collective-permute-start.104 = (bf16[2,96,1152]{2,1,0:T(8,128)(2,1)}, bf16[2,96,1152]{2,1,0:T(8,128)(2,1)}, u32[]{:S(2)}, u32[]{:S(2)}) collective-permute-start(bf16[2,96,1152]{2,1,0:T(8,128)(2,1)} %get-tuple-element.205), channel_id=1, source_target_pairs={{0,2},{1,3},{2,0},{3,1},{4,6},{5,7},{6,4},{7,5},{8,10},{9,11},{10,... | collective-permute-start | bytes 1327112 | tf_op jit(solution)/shard_map/ppermute | solution.py:34
  698.6 39.1 %collective-permute-start.105 = (bf16[2,96,1152]{2,1,0:T(8,128)(2,1)}, bf16[2,96,1152]{2,1,0:T(8,128)(2,1)}, u32[]{:S(2)}, u32[]{:S(2)}) collective-permute-start(bf16[2,96,1152]{2,1,0:T(8,128)(2,1)} %get-tuple-element.204), channel_id=1, source_target_pairs={{0,3},{1,0},{2,1},{3,2},{4,7},{5,4},{6,5},{7,6},{8,11},{9,8},{10,9... | collective-permute-start | bytes 1327112 | tf_op jit(solution)/shard_map/ppermute | solution.py:34
  721.3 35.4 %collective-permute-start.54 = (bf16[4,256,1152]{2,1,0:T(8,128)(2,1)}, bf16[4,256,1152]{2,1,0:T(8,128)(2,1)}, u32[]{:S(2)}, u32[]{:S(2)}) collective-permute-start(bf16[4,256,1152]{2,1,0:T(8,128)(2,1)} %dynamic-slice_bitcast_fusion.2), channel_id=1, source_target_pairs={{0,4},{4,0},{8,12},{12,8},{16,20},{20,16},{24,28},{28,24},{1,5},{5... | collective-permute-start | bytes 7077896 | tf_op jit(solution)/shard_map/ppermute | solution.py:29
  821.4 179.1 %collective-permute-start.97 = (bf16[72,1152]{1,0:T(8,128)(2,1)}, bf16[72,1152]{1,0:T(8,128)(2,1)}, u32[]{:S(2)}, u32[]{:S(2)}) collective-permute-start(bf16[72,1152]{1,0:T(8,128)(2,1)} %get-tuple-element.214), channel_id=1, source_target_pairs={{0,1},{1,2},{2,3},{3,0},{4,5},{5,6},{6,7},{7,4},{8,9},{9,10},{10,1... | collective-permute-start | bytes 497672 | tf_op jit(solution)/shard_map/ppermute | solution.py:34
  831.7 168.9 %collective-permute-start.98 = (bf16[72,1152]{1,0:T(8,128)(2,1)}, bf16[72,1152]{1,0:T(8,128)(2,1)}, u32[]{:S(2)}, u32[]{:S(2)}) collective-permute-start(bf16[72,1152]{1,0:T(8,128)(2,1)} %get-tuple-element.216), channel_id=1, source_target_pairs={{0,2},{1,3},{2,0},{3,1},{4,6},{5,7},{6,4},{7,5},{8,10},{9,11},{10,... | collective-permute-start | bytes 497672 | tf_op jit(solution)/shard_map/ppermute | solution.py:34
  955.0 38.7 %collective-permute-start.91 = (bf16[8,36,288]{2,1,0:T(8,128)(2,1)}, bf16[8,36,288]{2,1,0:T(8,128)(2,1)}, u32[]{:S(2)}, u32[]{:S(2)}) collective-permute-start(bf16[8,36,288]{2,1,0:T(8,128)(2,1)} %get-tuple-element.211), channel_id=1, source_target_pairs={{0,1},{1,2},{2,3},{3,0},{4,5},{5,6},{6,7},{7,4},{8,9},{9,10},{10,1... | collective-permute-start | bytes 497672 | tf_op jit(solution)/shard_map/ppermute | solution.py:34
  960.8 34.3 %collective-permute-start.92 = (bf16[8,36,288]{2,1,0:T(8,128)(2,1)}, bf16[8,36,288]{2,1,0:T(8,128)(2,1)}, u32[]{:S(2)}, u32[]{:S(2)}) collective-permute-start(bf16[8,36,288]{2,1,0:T(8,128)(2,1)} %get-tuple-element.213), channel_id=1, source_target_pairs={{0,2},{1,3},{2,0},{3,1},{4,6},{5,7},{6,4},{7,5},{8,10},{9,11},{10,... | collective-permute-start | bytes 497672 | tf_op jit(solution)/shard_map/ppermute | solution.py:34
  995.1 50.2 %collective-permute-start.81 = (bf16[4,256,1152]{2,1,0:T(8,128)(2,1)}, bf16[4,256,1152]{2,1,0:T(8,128)(2,1)}, u32[]{:S(2)}, u32[]{:S(2)}) collective-permute-start(bf16[4,256,1152]{2,1,0:T(8,128)(2,1)} %dynamic-slice_bitcast_fusion), channel_id=1, source_target_pairs={{0,4},{4,0},{8,12},{12,8},{16,20},{20,16},{24,28},{28,24},{1,5},{5... | collective-permute-start | bytes 7077896 | tf_op jit(solution)/shard_map/ppermute | solution.py:29
  (177 other events, 3573.0 us)

commit v2 on v1

v2 whole, which is shorter than its diff:
```python
import math

import jax
import jax.numpy as jnp
from jax import lax
from jax.experimental import pallas as pl
from jax.experimental.pallas import tpu as pltpu
from jax.sharding import PartitionSpec as P

D = 1152
DI = 2304
NS = 16
DT_RANK = 72
CONV = 4
FF = 3072
EXPERTS = 2
EPSILON = 1e-05
TIME_BLOCK = 128
VMEM = 40 * 2**20
LANES = 128
LN2 = math.log(2.0)

f32 = jnp.float32
bf16 = jnp.bfloat16


def relative():
    return lax.axis_size("wide") == 8


def swap(x, k):
    n = lax.axis_size("wide")
    return lax.ppermute(x, "wide", [(i, i ^ k) for i in range(n)])


def turn(x, k):
    n = lax.axis_size("narrow")
    return lax.ppermute(x, "narrow", [(i, (i + k) % n) for i in range(n)])


def pick(x, i, axis=0):
    return lax.dynamic_index_in_dim(x, i, axis, False)


def gather_wide(block, meanwhile=None):
    if not relative():
        made = meanwhile(block) if meanwhile else ()
        return lax.all_gather(block, "wide", axis=0, tiled=True), made
    half = block.shape[0] // 2
    mate = swap(block, 1)
    a, b = swap(block, 2), swap(block, 4)
    made = ()
    if meanwhile:
        made = meanwhile(block)
        a, b, made = lax.optimization_barrier((a, b, made))
    c0, c1 = swap(a[:half], 4), swap(b[half:], 2)
    out = jnp.concatenate(
        [block, mate, a, swap(a, 1), b, swap(b, 1), c0, c1, swap(c0, 1), swap(c1, 1)], axis=0
    )
    return out, made


def scatter_wide(partial):
    if not relative():
        return lax.psum_scatter(partial, "wide", scatter_dimension=0, tiled=True).astype(f32)
    rows = partial.shape[0] // 8
    half = rows // 2
    parts = partial.reshape(8, rows, partial.shape[1])

    def summed(q):
        return parts[2 * q].astype(f32) + swap(parts[2 * q + 1], 1).astype(f32)

    far = summed(3).astype(bf16)
    r0, r1 = swap(far[:half], 2), swap(far[half:], 4)
    sx, sy = summed(1), summed(2)
    x0, y1 = swap(sx[:half].astype(bf16), 2), swap(sy[half:].astype(bf16), 4)
    x1 = swap((sx[half:] + r1.astype(f32)).astype(bf16), 2)
    y0 = swap((sy[:half] + r0.astype(f32)).astype(bf16), 4)
    x = jnp.concatenate([x0, x1], axis=0).astype(f32)
    y = jnp.concatenate([y0, y1], axis=0).astype(f32)
    return summed(0) + x + y


def reduce_wide(partial, meanwhile):
    if not relative():
        return lax.psum(partial, "wide"), meanwhile(partial)
    core = lax.axis_index("wide") % 2
    half = partial.shape[0] // 2
    parts = partial.reshape(2, half, partial.shape[1])
    total = pick(parts, core).astype(f32) + swap(pick(parts, 1 - core), 1).astype(f32)
    low = total.astype(bf16)
    got = [swap(low, 2), swap(low, 4), swap(low, 6)]
    got, made = lax.optimization_barrier((got, meanwhile(low)))
    total = total + sum(p.astype(f32) for p in got)
    low = total.astype(bf16)
    mate = swap(low, 1)
    first = core == 0
    out = jnp.concatenate([jnp.where(first, low, mate), jnp.where(first, mate, low)], axis=0)
    return out, made


def after(x, *others):
    return lax.optimization_barrier((x,) + others)[0]


def turns(x):
    return [x] + [turn(x, k) for k in range(1, lax.axis_size("narrow"))]


def pad_to(x, axis, size):
    pads = [(0, 0)] * x.ndim
    pads[axis] = (0, size - x.shape[axis])
    return jnp.pad(x, pads)


def gather_channels(x, splits, total):
    n, z = lax.axis_size("narrow"), lax.axis_index("narrow")
    rows, cols = x.shape
    pieces = [x] + [turn(x, k) for k in range(1, n)]
    order = jnp.stack([(z - k) % n * rows for k in range(n)]).astype(jnp.int32)

    def kernel(order_ref, *refs):
        value = jnp.zeros((total, cols), f32)
        r = lax.broadcasted_iota(jnp.int32, (total, rows), 0)
        j = lax.broadcasted_iota(jnp.int32, (total, rows), 1)
        for k in range(n):
            spots = jnp.where(r == j + order_ref[k], 1.0, 0.0).astype(bf16)
            value = value + jnp.dot(spots, refs[k][...], preferred_element_type=f32)
        value = value.astype(bf16)
        at = 0
        for out in refs[n:]:
            out[...] = value[:, at : at + out.shape[1]]
            at += out.shape[1]

    vmem = pl.BlockSpec(memory_space=pltpu.VMEM)
    return pl.pallas_call(
        kernel,
        in_specs=[pl.BlockSpec(memory_space=pltpu.SMEM)] + [vmem] * n,
        out_specs=[vmem] * len(splits),
        out_shape=[jax.ShapeDtypeStruct((total, c), bf16) for c in splits],
        compiler_params=pltpu.CompilerParams(vmem_limit_bytes=VMEM),
    )(order, *pieces)


def turned(pieces):
    return [pieces[0]] + [turn(pieces[k], k) for k in range(1, len(pieces))]


def split_narrow(x, axis):
    n, z = lax.axis_size("narrow"), lax.axis_index("narrow")
    return [pick(x, (z + k) % n, axis) for k in range(n)]


def exchange(x):
    return lax.all_to_all(x, ("wide", "narrow"), 0, 0)


def gather_rows(parts):
    wide, rows, cols = parts.shape
    narrow = lax.axis_size("narrow")
    parts = jnp.broadcast_to(parts[:, None], (wide, narrow, rows, cols))
    got = exchange(parts.reshape(wide * narrow, rows, cols))
    return got.reshape(wide * narrow * rows, cols)


def scatter_rows(grad, rows):
    wide, narrow = lax.axis_size("wide"), lax.axis_size("narrow")
    got = exchange(grad.reshape(wide * narrow, rows, grad.shape[1]))
    return got.reshape(wide, narrow, rows, grad.shape[1])


def summed_rows(got):
    return sum(got[:, k].astype(f32) for k in range(got.shape[1]))


def mm(a, b):
    return jnp.dot(a, b, preferred_element_type=f32)


def mm_t(a, b):
    return lax.dot_general(a, b, (((1,), (1,)), ((), ())), preferred_element_type=f32)


def t_mm(a, b):
    return lax.dot_general(a, b, (((0,), (0,)), ((), ())), preferred_element_type=f32)


def sigmoid(v):
    return 1.0 / (1.0 + jnp.exp(-v))


def softplus(v):
    return jnp.maximum(v, 0.0) + jnp.log1p(jnp.exp(-jnp.abs(v)))


def call(kernel, grid, flip, ins, outs, scratch, flops, exps=0):
    def spec(block, where):
        if where is None:
            zeros = (0,) * len(block)
            return pl.BlockSpec(block, lambda i, s: zeros)
        return pl.BlockSpec(block, lambda i, s: (where(i, s[0]),) + (0,) * (len(block) - 1))

    size = sum(a.size * a.dtype.itemsize for a, _, _ in ins)
    size += sum(math.prod(o[0]) * jnp.dtype(o[1]).itemsize for o in outs)
    return pl.pallas_call(
        kernel,
        grid_spec=pltpu.PrefetchScalarGridSpec(
            num_scalar_prefetch=1,
            grid=(grid,),
            in_specs=[spec(b, f) for _, b, f in ins],
            out_specs=[spec(b, f) for _, _, b, f in outs],
            scratch_shapes=scratch,
        ),
        out_shape=[jax.ShapeDtypeStruct(o[0], o[1]) for o in outs],
        compiler_params=pltpu.CompilerParams(vmem_limit_bytes=VMEM),
        cost_estimate=pl.CostEstimate(flops=flops, bytes_accessed=size, transcendentals=exps),
    )(flip, *[a for a, _, _ in ins])


def front(flip, tokens, gain, weight_x, taps, shift, weight_sel):
    length, wid = tokens.shape[0], weight_x.shape[1]
    blocks = lax.axis_size("wide")
    rows = length // blocks

    def kernel(s_ref, tok, gain_r, wx, taps_r, shift_r, wsel, normed, proj, conv, act, part, pad):
        @pl.when(pl.program_id(0) == 0)
        def _():
            pad[:8, :] = jnp.zeros((8, wid), f32)

        values = tok[...].astype(f32)
        inverse = lax.rsqrt(jnp.mean(values * values, axis=-1, keepdims=True) + EPSILON)
        low = (values * inverse * gain_r[...]).astype(bf16)
        normed[...] = low
        x = mm(low, wx[...])
        proj[...] = x
        pad[8:, :] = x
        total = shift_r[...] + taps_r[CONV - 1 : CONV, :] * x
        for k in range(CONV - 1):
            start = 8 - (CONV - 1) + k
            total = total + taps_r[k : k + 1, :] * pad[start : start + rows, :]
        pad[:8, :] = x[rows - 8 :, :]
        conv[...] = total
        low = (total * sigmoid(total)).astype(bf16)
        act[...] = low
        part[...] = mm(low, wsel[...]).astype(bf16)

    here = lambda i, s: i
    rel = lambda i, s: i ^ s
    return call(
        kernel,
        blocks,
        flip,
        [
            (tokens, (rows, D), rel),
            (gain, (1, D), None),
            (weight_x, (D, wid), None),
            (taps, (CONV, wid), None),
            (shift, (1, wid), None),
            (weight_sel, (wid, LANES), None),
        ],
        [
            ((length, D), bf16, (rows, D), rel),
            ((length, wid), f32, (rows, wid), here),
            ((length, wid), f32, (rows, wid), here),
            ((length, wid), bf16, (rows, wid), here),
            ((length, LANES), bf16, (rows, LANES), here),
        ],
        [pltpu.VMEM((rows + 8, wid), f32)],
        2 * length * wid * (D + LANES),
    )


FLAT = CONV + 4 + NS
def row_sums(terms, masks):
    high, mid, low = masks
    c = [
        jnp.where(high, terms[i + 4], terms[i])
        + pltpu.roll(jnp.where(high, terms[i], terms[i + 4]), 4, 0)
        for i in range(4)
    ]
    c = [
        jnp.where(mid, c[i + 2] + pltpu.roll(c[i + 2], 2, 0), c[i] + pltpu.roll(c[i], 6, 0))
        for i in range(2)
    ]
    return jnp.where(low, c[1] + pltpu.roll(c[1], 1, 0), c[0] + pltpu.roll(c[0], 7, 0))


def row_masks(wid):
    row = lax.broadcasted_iota(jnp.int32, (8, wid), 0)
    return row >= 4, (row & 2) > 0, (row & 1) > 0


IN_AT = DT_RANK
OUT_AT = DT_RANK + NS


def middle(flip, sel, act, proj_z, weight_step, shift, skip, a2, weight_out):
    length, wid = act.shape
    blocks = length // TIME_BLOCK
    per = blocks // lax.axis_size("wide")

    def kernel(
        s_ref, sel_r, act_r, z_r, wstep, shift_r, skip_r, a_r, wout, lin_o, kept, end, mixed, gated_o, part, state, dt_s, u_s, y_s
    ):
        @pl.when(pl.program_id(0) == 0)
        def _():
            state[...] = jnp.zeros_like(state)

        low = sel_r[...]
        lin = mm_t(low, wstep[...]) + shift_r[...]
        lin_o[...] = lin
        dt_s[...] = softplus(lin)
        u_s[...] = dt_s[...] * act_r[...].astype(f32)
        turned = low.astype(f32).T
        in_sel, out_sel = turned[IN_AT : IN_AT + NS, :], turned[OUT_AT : OUT_AT + NS, :]
        a2 = a_r[...]

        masks = row_masks(wid)
        h = state[...]
        terms = [None] * 8
        for t in range(TIME_BLOCK):
            kept[t] = h
            h = jnp.exp2(dt_s[t : t + 1, :] * a2) * h + u_s[t : t + 1, :] * in_sel[:, t : t + 1]
            y = h * out_sel[:, t : t + 1]
            terms[t % 8] = y[:8] + y[8:]
            if t % 8 == 7:
                y_s[t - 7 : t + 1, :] = row_sums(terms, masks)
        state[...] = h
        end[...] = h
        out = y_s[...] + skip_r[...] * act_r[...].astype(f32)
        mixed[...] = out
        z = z_r[...]
        gated = (out * z * sigmoid(z)).astype(bf16)
        gated_o[...] = gated
        part[...] = mm(gated, wout[...]).astype(bf16)

    here = lambda i, s: i
    rel = lambda i, s: ((i // per) ^ s) * per + i % per
    row = (TIME_BLOCK, wid)
    return call(
        kernel,
        blocks,
        flip,
        [
            (sel, (TIME_BLOCK, LANES), here),
            (act, row, here),
            (proj_z, row, rel),
            (weight_step, (wid, LANES), None),
            (shift, (1, wid), None),
            (skip, (1, wid), None),
            (a2, (NS, wid), None),
            (weight_out, (wid, D), None),
        ],
        [
            ((length, wid), f32, row, here),
            ((length, NS, wid), f32, (TIME_BLOCK, NS, wid), here),
            ((NS, wid), f32, (NS, wid), None),
            ((length, wid), f32, row, here),
            ((length, wid), bf16, row, rel),
            ((length, D), bf16, (TIME_BLOCK, D), rel),
        ],
        [pltpu.VMEM((NS, wid), f32)] + [pltpu.VMEM(row, f32)] * 3,
        length * wid * (8 * NS + 2 * D + 2 * LANES),
        length * NS * wid,
    )


def experts(span, normed, cot, up, down, ff):
    length = normed.shape[0]
    blocks = lax.axis_size("wide")
    rows = length // blocks
    cols = up.shape[1]

    def kernel(s_ref, n_r, cot_r, up_r, down_r, out_part, back_part, hid_o, both_o, dex_o):
        i = pl.program_id(0)
        position = (i ^ s_ref[0]) * rows + lax.broadcasted_iota(jnp.int32, (rows, 1), 0)
        cot_b = cot_r[...]
        second = cot_b[:, D : D + 1] > 0.5
        upstream = jnp.where(position < s_ref[1], cot_b[:, :D], jnp.zeros((), bf16))
        raised = mm(n_r[...], up_r[...])
        first_l, second_l = raised[:, EXPERTS * ff : EXPERTS * ff + 1], raised[:, EXPERTS * ff + 1 : EXPERTS * ff + 2]
        lead = jnp.where(second, second_l - first_l, first_l - second_l)
        gate = sigmoid(lead)
        other = sigmoid(-lead)
        pre = jnp.where(second, raised[:, ff : 2 * ff], raised[:, :ff])
        bell = (1.0 + lax.erf(pre * (1.0 / math.sqrt(2.0)))) * 0.5
        hidden = pre * bell
        slope = bell + pre * jnp.exp(-0.5 * pre * pre) * (1.0 / math.sqrt(2.0 * math.pi))
        hidden = hidden.astype(bf16)
        hid_f = hidden.astype(f32)
        both = jnp.concatenate(
            [jnp.where(second, 0.0, hid_f), jnp.where(second, hid_f, 0.0)], axis=1
        ).astype(bf16)
        hid_o[...] = both
        out_part[...] = (gate * mm(both, down_r[...])).astype(bf16)
        dex_o[...] = (gate * upstream.astype(f32)).astype(bf16)
        lowered = mm_t(upstream, down_r[...])
        d_hid = jnp.where(second, lowered[:, ff:], lowered[:, :ff])
        d_gate = jnp.sum(hid_f * d_hid, axis=-1, keepdims=True)
        d_pre = gate * d_hid * slope
        d_lead = gate * other * d_gate
        lane = lax.broadcasted_iota(jnp.int32, (rows, cols - EXPERTS * ff), 1)
        d_second = jnp.where(second, d_lead, -d_lead)
        d_logits = jnp.where(lane == 1, d_second, jnp.where(lane == 0, -d_second, 0.0))
        d_both = jnp.concatenate(
            [jnp.where(second, 0.0, d_pre), jnp.where(second, d_pre, 0.0), d_logits], axis=1
        ).astype(bf16)
        both_o[...] = d_both
        back_part[...] = mm_t(d_both, up_r[...]).astype(bf16)

    here = lambda i, s: i
    return call(
        kernel,
        blocks,
        span,
        [
            (normed, (rows, D), here),
            (cot, (rows, D + LANES), lambda i, s: i ^ s),
            (up, up.shape, None),
            (down, down.shape, None),
        ],
        [
            ((length, D), bf16, (rows, D), lambda i, s: i ^ s),
            ((length, D), bf16, (rows, D), here),
            ((length, EXPERTS * ff), bf16, (rows, EXPERTS * ff), here),
            ((length, cols), bf16, (rows, cols), here),
            ((length, D), bf16, (rows, D), here),
        ],
        [],
        4 * length * D * (cols + EXPERTS * ff),
        3 * length * ff,
    )


def back(flip, d_mix, weight_out, sel, act, proj_z, lin, mixed, kept, end, weight_step, skip, a2):
    length, wid = act.shape
    blocks = length // TIME_BLOCK
    per = blocks // lax.axis_size("wide")

    def kernel(
        s_ref, mix_r, wout, sel_r, act_r, z_r, lin_r, mixed_r, kept_r, end_r, wstep, skip_r, a_r,
        dz_o, part, dact_o, gstep_o, da_o, dskip_o, dbias_o,
        lam_s, next_s, pb_s, pc_s, dt_s, u_s, dy_s, s1_s, s2_s, turned_s,
    ):
        @pl.when(pl.program_id(0) == 0)
        def _():
            lam_s[...] = jnp.zeros_like(lam_s)
            next_s[...] = end_r[...]
            da_o[...] = jnp.zeros_like(da_o)
            for ref in (gstep_o, dskip_o, dbias_o):
                ref[...] = jnp.zeros_like(ref)
            turned_s[...] = jnp.zeros_like(turned_s)

        d_gated = mm_t(mix_r[...], wout[...])
        z = z_r[...]
        s = sigmoid(z)
        dz_o[...] = (d_gated * mixed_r[...] * (s * (1.0 + z * (1.0 - s)))).astype(bf16)
        dy_s[...] = d_gated * (z * s)
        x_all = act_r[...].astype(f32)
        dskip_o[...] += jnp.sum(dy_s[...] * x_all, axis=0, keepdims=True)
        dt_s[...] = softplus(lin_r[...])
        u_s[...] = dt_s[...] * x_all
        low = sel_r[...]
        turned = low.astype(f32).T
        in_sel, out_sel = turned[IN_AT : IN_AT + NS, :], turned[OUT_AT : OUT_AT + NS, :]
        a2 = a_r[...]

        def fold(v):
            total = v[:, :LANES]
            for k in range(1, wid // LANES):
                total = total + v[:, k * LANES : (k + 1) * LANES]
            return total

        masks = row_masks(wid)
        p, after, acc = lam_s[...], next_s[...], da_o[...]
        first, second = [None] * 8, [None] * 8
        for t in range(TIME_BLOCK - 1, -1, -1):
            before = kept_r[t]
            dt_t, dy_t = dt_s[t : t + 1, :], dy_s[t : t + 1, :]
            lam = dy_t * out_sel[:, t : t + 1] + p
            p = lam * jnp.exp2(dt_t * a2)
            moved = p * before
            acc = acc + dt_t * moved
            term = lam * in_sel[:, t : t + 1]
            first[t % 8] = term[:8] + term[8:]
            term = a2 * moved
            second[t % 8] = term[:8] + term[8:]
            if t % 8 == 0:
                s1_s[t : t + 8, :] = row_sums(first, masks)
                s2_s[t : t + 8, :] = row_sums(second, masks)
            pb_s[t] = fold(lam * u_s[t : t + 1, :])
            pc_s[t] = fold(after * dy_t)
            after = before
        lam_s[...] = p
        next_s[...] = after
        da_o[...] = acc
        ones = jnp.ones((LANES, LANES), bf16)
        lane = lax.broadcasted_iota(jnp.int32, (NS, TIME_BLOCK), 1)
        for source, at in ((pb_s, IN_AT), (pc_s, OUT_AT)):
            sums = mm(source[...].reshape(TIME_BLOCK * NS, LANES).astype(bf16), ones)
            sums = sums.reshape(TIME_BLOCK, NS, LANES)
            parts = [jnp.zeros((NS, TIME_BLOCK), f32)] * 4
            for t in range(TIME_BLOCK):
                parts[t % 4] = jnp.where(lane == t, sums[t], parts[t % 4])
            turned_s[at : at + NS, :] = (parts[0] + parts[1]) + (parts[2] + parts[3])
        through = s1_s[...]
        d_step = s2_s[...] * LN2 + x_all * through
        dact_o[...] = dt_s[...] * through + skip_r[...] * dy_s[...]
        grad = d_step * sigmoid(lin_r[...])
        dbias_o[...] += jnp.sum(grad, axis=0, keepdims=True)
        grad = grad.astype(bf16)
        gstep_o[...] += t_mm(grad, low)
        part[...] = (mm(grad, wstep[...]) + turned_s[...].T).astype(bf16)

    here = lambda i, s: blocks - 1 - i
    rel = lambda i, s: (((blocks - 1 - i) // per) ^ s) * per + (blocks - 1 - i) % per
    row = (TIME_BLOCK, wid)
    one = ((1, wid), f32, (1, wid), None)
    return call(
        kernel,
        blocks,
        flip,
        [
            (d_mix, (TIME_BLOCK, D), rel),
            (weight_out, (wid, D), None),
            (sel, (TIME_BLOCK, LANES), here),
            (act, row, here),
            (proj_z, row, rel),
            (lin, row, here),
            (mixed, row, here),
            (kept, (TIME_BLOCK, NS, wid), here),
            (end, (NS, wid), None),
            (weight_step, (wid, LANES), None),
            (skip, (1, wid), None),
            (a2, (NS, wid), None),
        ],
        [
            ((length, wid), bf16, row, rel),
            ((length, LANES), bf16, (TIME_BLOCK, LANES), here),
            ((length, wid), f32, row, here),
            ((wid, LANES), f32, (wid, LANES), None),
            ((NS, wid), f32, (NS, wid), None),
            one,
            one,
        ],
        [pltpu.VMEM((NS, wid), f32)] * 2
        + [pltpu.VMEM((TIME_BLOCK, NS, LANES), f32)] * 2
        + [pltpu.VMEM(row, f32)] * 5
        + [pltpu.VMEM((LANES, TIME_BLOCK), f32)],
        length * wid * (20 * NS + 2 * D + 2 * LANES),
        length * NS * wid,
    )


def tail(
    flip, d_sel, d_act, conv, proj, d_z, normed, act, weight_x, weight_z, weight_sel, taps,
    grad_step, grad_flat, chans,
):
    length, wid = act.shape
    blocks = lax.axis_size("wide")
    rows = length // blocks

    def kernel(
        s_ref, sel_r, dact_r, conv_r, proj_r, dz_r, n_r, act_r, wx, wz, wsel, taps_r, gstep_r, flat_r,
        part, *refs,
    ):
        gx_o, pack_o, ext, gx, gsel, flat = refs

        @pl.when(pl.program_id(0) == 0)
        def _():
            ext[rows:, :] = jnp.zeros((8, wid), f32)
            gx[...] = jnp.zeros_like(gx)
            gsel[...] = jnp.zeros_like(gsel)
            flat[...] = flat_r[...]

        low = sel_r[...]
        c = conv_r[...]
        q = sigmoid(c)
        d_conv = (mm_t(low, wsel[...]) + dact_r[...]) * (q * (1.0 + c * (1.0 - q)))
        ext[:rows, :] = d_conv
        flat[CONV : CONV + 1, :] += jnp.sum(d_conv, axis=0, keepdims=True)
        x = proj_r[...]
        d_x = jnp.zeros((rows, wid), f32)
        for k in range(CONV):
            moved = ext[CONV - 1 - k : CONV - 1 - k + rows, :]
            d_x = d_x + taps_r[k : k + 1, :] * moved
            flat[k : k + 1, :] += jnp.sum(moved * x, axis=0, keepdims=True)
        ext[rows:, :] = d_conv[:8, :]
        d_x = d_x.astype(bf16)
        part[...] = (mm_t(d_x, wx[...]) + mm_t(dz_r[...], wz[...])).astype(bf16)
        gx[...] += t_mm(n_r[...], d_x)
        gsel[...] += t_mm(act_r[...], low)

        @pl.when(pl.program_id(0) == blocks - 1)
        def _():
            gx_o[...] = gx[:, :chans].astype(bf16)
            tall = jnp.concatenate(
                [jnp.zeros((DT_RANK, wid), f32), flat[...], jnp.zeros((LANES - DT_RANK - FLAT, wid), f32)], axis=0
            )
            lane = lax.broadcasted_iota(jnp.int32, (wid, LANES), 1)
            left = jnp.where(lane < DT_RANK, gstep_r[...], tall.T)
            pack = jnp.concatenate([left, gsel[...]], axis=1).astype(bf16)
            pack_o[...] = pack[:chans]

    here = lambda i, s: blocks - 1 - i
    rel = lambda i, s: (blocks - 1 - i) ^ s
    row = (rows, wid)
    pack = (chans, 2 * LANES)
    return call(
        kernel,
        blocks,
        flip,
        [
            (d_sel, (rows, LANES), here),
            (d_act, row, here),
            (conv, row, here),
            (proj, row, here),
            (d_z, row, rel),
            (normed, (rows, D), rel),
            (act, row, here),
            (weight_x, (D, wid), None),
            (weight_z, (D, wid), None),
            (weight_sel, (wid, LANES), None),
            (taps, (CONV, wid), None),
            (grad_step, (wid, LANES), None),
            (grad_flat, (FLAT, wid), None),
        ],
        [((length, D), bf16, (rows, D), rel), ((D, chans), bf16, (D, chans), None), (pack, bf16, pack, None)],
        [
            pltpu.VMEM((rows + 8, wid), f32),
            pltpu.VMEM((D, wid), f32),
            pltpu.VMEM((wid, LANES), f32),
            pltpu.VMEM((FLAT, wid), f32),
        ],
        2 * length * wid * (3 * D + 2 * LANES),
    )


def row_grad(flip, a, b, cols):
    length, total = a.shape
    n = b.shape[1]
    blocks = lax.axis_size("wide")
    rows = length // blocks

    def kernel(s_ref, a_r, b_r, out, acc):
        @pl.when(pl.program_id(0) == 0)
        def _():
            acc[...] = jnp.zeros_like(acc)

        acc[...] += t_mm(a_r[...], b_r[...])

        @pl.when(pl.program_id(0) == blocks - 1)
        def _():
            out[...] = acc[:, :cols].astype(bf16)

    here = lambda i, s: i
    return call(
        kernel,
        blocks,
        flip,
        [(a, (rows, total), here), (b, (rows, n), here)],
        [((total, cols), bf16, (total, cols), None)],
        [pltpu.VMEM((total, n), f32)],
        2 * length * total * n,
    )[0]


def norm_backward(values, inverse, gain_vec, upstream):
    scaled = upstream * gain_vec
    inner_mean = jnp.mean(values * scaled, axis=-1, keepdims=True)
    return inverse * scaled - values * (inverse * inverse * inverse) * inner_mean


def local(
    tokens,
    mixer_gain,
    in_weight,
    conv_weight,
    conv_bias,
    select_weight,
    step_weight,
    step_bias,
    decay_log,
    skip_weight,
    out_weight,
    expert_gain,
    router_weight,
    up_weight,
    down_weight,
    routes,
    lengths,
    cotangent,
):
    wide, narrow = lax.axis_size("wide"), lax.axis_size("narrow")
    w = lax.axis_index("wide")
    rows = tokens.shape[1]
    chans = DI // wide
    wid = -(-chans // LANES) * LANES
    ff = FF // wide
    d_rows = D // (wide * narrow)
    c_rows = DI // (wide * narrow)
    f_rows = FF // (wide * narrow)
    both = EXPERTS * ff
    flip = w if relative() else 0 * w
    span = jnp.stack([flip, lengths[0]]).astype(jnp.int32)

    tokens_own = tokens[0].astype(f32)
    tokens_all, _ = gather_wide(tokens[0])

    in_parts = in_weight.reshape(d_rows, 2, wide, chans).transpose(1, 2, 0, 3)
    gains = jnp.stack([mixer_gain, expert_gain], axis=1)
    gains = jnp.broadcast_to(gains[None], (wide, d_rows, 2))
    x_full = gather_rows(jnp.concatenate([in_parts[0], gains], axis=2))
    weight_x = pad_to(x_full[:, :chans], 1, wid)
    gains = x_full[:, chans:].T.astype(f32)
    gain_one, gain_two = gains[:1], gains[1:]
    weight_z = pad_to(gather_rows(after(in_parts[1], x_full)), 1, wid)
    zero_col = jnp.zeros((c_rows, 1), bf16)
    channel_pack = jnp.concatenate(
        [
            conv_weight.T,
            conv_bias[:, None],
            step_bias[:, None],
            skip_weight[:, None],
            zero_col,
            decay_log.T,
            step_weight.T,
            select_weight,
        ],
        axis=1,
    )
    pack_cols = channel_pack.shape[1]
    wide_cols = -(-pack_cols // LANES) * LANES
    channel_pack = jnp.concatenate([out_weight, pad_to(channel_pack, 1, wide_cols)], axis=1)
    weight_out, packed = gather_channels(channel_pack, (D, wide_cols), wid)
    flat = packed[:, :FLAT].T.astype(f32)
    taps = flat[:CONV]
    conv_shift, step_shift, skip = (flat[CONV + k : CONV + k + 1] for k in range(3))
    a_neg = -jnp.exp(flat[CONV + 4 :])
    a2 = a_neg * (1.0 / LN2)
    weight_step = pad_to(packed[:, FLAT : FLAT + DT_RANK], 1, LANES)
    weight_sel = pad_to(packed[:, FLAT + DT_RANK : pack_cols], 1, LANES)

    normed, proj_x, conv_sum, conv_act, sel_part = front(
        flip[None], tokens_all, gain_one, weight_x, taps, conv_shift, weight_sel
    )
    sel_part, weight_z = lax.optimization_barrier((sel_part, weight_z))
    selected, proj_z = reduce_wide(sel_part, lambda low: mm(after(normed, low), weight_z))

    up_cols = -(-(both + EXPERTS) // LANES) * LANES
    up_parts = up_weight.reshape(EXPERTS, d_rows, wide, ff).transpose(2, 1, 0, 3)
    up_parts = up_parts.reshape(wide, d_rows, both)
    router_parts = jnp.broadcast_to(router_weight[None], (wide, d_rows, EXPERTS))
    up_parts = jnp.concatenate([up_parts, router_parts], axis=2)
    up_full = gather_rows(after(up_parts, selected))
    down_full = lax.all_gather(after(down_weight, selected), "narrow")
    down_full = down_full.transpose(1, 0, 2, 3).reshape(both, D)
    route_cols = jnp.broadcast_to(routes[0].astype(bf16)[:, None], (rows, LANES))
    cot_ext = jnp.concatenate([cotangent[0], route_cols], axis=1)
    cot_all = lax.all_gather(after(cot_ext, selected), "wide", axis=0, tiled=True)
    valid_own = (w * rows + jnp.arange(rows))[:, None] < lengths[0]
    upstream = jnp.where(valid_own, cotangent[0].astype(f32), 0.0)

    step_lin, kept, end, mixed, gated, mix_part = middle(
        flip[None], selected, conv_act, proj_z, weight_step, step_shift, skip, a2, weight_out
    )
    up_full = pad_to(up_full, 1, up_cols)
    hidden_one = tokens_own + scatter_wide(mix_part)
    inverse_two = lax.rsqrt(jnp.mean(hidden_one * hidden_one, axis=-1, keepdims=True) + EPSILON)
    normed_two, _ = gather_wide((hidden_one * inverse_two * gain_two).astype(bf16))
    out_part, back_part, hidden_both, d_both, d_expert = experts(
        span, normed_two, cot_all, up_full, down_full, ff
    )

    d_normed_two = scatter_wide(back_part)
    grad_down = t_mm(hidden_both, d_expert).astype(bf16)
    grad_down = split_narrow(grad_down.reshape(EXPERTS, narrow, f_rows, D), 1)
    d_normed_two = after(d_normed_two, grad_down)
    d_hidden_one = upstream + norm_backward(hidden_one, inverse_two, gain_two, d_normed_two)
    d_low = d_hidden_one.astype(bf16)
    d_mix, grad_up = gather_wide(
        d_low,
        lambda low: row_grad(flip[None], normed_two, after(d_both, low), both + EXPERTS),
    )
    grad_up = scatter_rows(after(grad_up, d_mix), d_rows)
    grad_down = turned([after(p, d_mix) for p in grad_down])
    expert_sum = lax.psum_scatter(after(out_part, d_mix), "wide", scatter_dimension=0, tiled=True)

    d_z, d_sel_part, d_act, grad_step, d_a, grad_skip, grad_step_bias = back(
        flip[None], d_mix, weight_out, selected, conv_act, proj_z, step_lin, mixed, kept, end,
        weight_step, skip, a2,
    )
    d_sel_part, grad_up, grad_down = lax.optimization_barrier((d_sel_part, grad_up, grad_down))

    def meanwhile(low):
        grad_out = t_mm(after(gated, low), d_mix).astype(bf16)[:chans].reshape(narrow, c_rows, D)
        return split_narrow(grad_out, 0), row_grad(flip[None], after(normed, low), d_z, chans)

    d_sel, (grad_out, grad_z) = reduce_wide(d_sel_part, meanwhile)
    grad_out = turned([after(p, d_sel) for p in grad_out])
    grad_flat = jnp.concatenate(
        [jnp.zeros((CONV + 1, wid), f32), grad_step_bias, grad_skip, jnp.zeros((1, wid), f32), d_a * a_neg],
        axis=0,
    )
    in_part, grad_x, grad_pack = tail(
        flip[None], d_sel, d_act, conv_sum, proj_x, d_z, normed, conv_act, weight_x, weight_z,
        weight_sel, taps, grad_step, grad_flat, chans,
    )
    grad_in = scatter_rows(jnp.concatenate([grad_x, grad_z], axis=1), d_rows)
    in_part, grad_out = lax.optimization_barrier((in_part, grad_out))
    channel_grads = turned(split_narrow(grad_pack.reshape(narrow, c_rows, 2 * LANES), 0))
    d_normed = scatter_wide(in_part)
    d_normed, grad_in, channel_grads, grad_out = lax.optimization_barrier(
        (d_normed, grad_in, channel_grads, grad_out)
    )
    channel_grads = sum(p.astype(f32) for p in channel_grads)
    grad_out = sum(p.astype(f32) for p in grad_out)
    inverse_one = lax.rsqrt(jnp.mean(tokens_own * tokens_own, axis=-1, keepdims=True) + EPSILON)
    token_grad = d_hidden_one + norm_backward(tokens_own, inverse_one, gain_one, d_normed)
    output = (hidden_one + after(expert_sum, in_part).astype(f32)).astype(bf16)

    grad_up, grad_down, _ = lax.optimization_barrier((grad_up, grad_down, in_part))
    grad_up = summed_rows(grad_up)
    grad_down = sum(p.astype(f32) for p in grad_down)
    grad_router = jnp.sum(grad_up[:, :, both:], axis=0)
    grad_up = grad_up[:, :, :both].reshape(wide, d_rows, EXPERTS, ff)
    grad_up = grad_up.transpose(2, 1, 0, 3).reshape(EXPERTS, d_rows, FF)
    grad_gain_two = (
        jnp.sum(up_weight.astype(f32) * grad_up, axis=(0, 2))
        + jnp.sum(router_weight.astype(f32) * grad_router, axis=1)
    ) / expert_gain.astype(f32)

    grad_in = summed_rows(grad_in).reshape(wide, d_rows, 2, chans)
    grad_in = grad_in.transpose(1, 2, 0, 3).reshape(d_rows, 2 * DI)
    grad_gain_one = jnp.sum(in_weight.astype(f32) * grad_in, axis=1) / mixer_gain.astype(f32)
    flat_grads = channel_grads[:, DT_RANK : DT_RANK + FLAT].T
    return (
        output[None],
        token_grad[None],
        grad_gain_one,
        grad_in,
        flat_grads[:CONV],
        flat_grads[CONV],
        channel_grads[:, LANES : LANES + DT_RANK + 2 * NS],
        channel_grads[:, :DT_RANK].T,
        flat_grads[CONV + 1],
        flat_grads[CONV + 4 :],
        flat_grads[CONV + 2],
        grad_out,
        grad_gain_two,
        grad_router,
        grad_up,
        grad_down,
    )


def solution(mesh):
    both = ("wide", "narrow")
    return jax.shard_map(
        local,
        mesh=mesh,
        in_specs=(
            P("narrow", "wide", None),
            P(both),
            P(both, None),
            P(None, both),
            P(both),
            P(both, None),
            P(None, both),
            P(both),
            P(None, both),
            P(both),
            P(both, None),
            P(both),
            P(both, None),
            P(None, both, None),
            P(None, both, None),
            P("narrow", "wide"),
            P("narrow"),
            P("narrow", "wide", None),
        ),
        out_specs=(
            P("narrow", "wide", None),
            P("narrow", "wide", None),
            P(both),
            P(both, None),
            P(None, both),
            P(both),
            P(both, None),
            P(None, both),
            P(both),
            P(None, both),
            P(both),
            P(both, None),
            P(both),
            P(both, None),
            P(None, both, None),
            P(None, both, None),
        ),
        check_vma=False,
    )
```

time: 1100 us -> 622 us (0.57)
  local copies, waits for them, and re-layouts: 427 us -> 129 us
  starting transfers between devices: 183 us -> 91 us
  matrix products: 87.7 us -> 16.7 us
  other arithmetic: 86.8 us -> 35.9 us
  Pallas kernels: 114 us -> 149 us
  between operations: 4.17 us -> 16.1 us
    dynamic_update_slice x58 -> x0, local copies, waits for them, and re-layouts: 287 us -> none  [the longest x14 121 us: gather_wide(): out = lax.dynamic_update_index_in_dim(out, mine[q], at + core, 0)]
    ppermute x36 -> x12, starting transfers between devices: 98.3 us -> 17.9 us  [turn(): return lax.ppermute(x, 'narrow', [(i, (i + k) % n) for i in range(n)])]
    ppermute x70 -> x67, waiting for transfers between devices: 86.9 us -> 148 us  [swap(): return lax.ppermute(x, 'wide', [(i, i ^ k) for i in range(n)])]
    ppermute x36 -> x12, waiting for transfers between devices: 82.6 us -> 25.6 us  [turn(): return lax.ppermute(x, 'narrow', [(i, (i + k) % n) for i in range(n)])]
    unnamed x212 -> x176, local copies, waits for them, and re-layouts: 23.5 us -> 65.9 us
    dot_general x7 -> x0, matrix products: 35.6 us -> none  [mm_t(): lax.dot_general(a, b, (((1,), (1,)), ((), ())), preferred_element_type=f32)]
    pallas_call x2 -> x8, Pallas kernels: 114 us -> 149 us  [the longest x7 147 us: call(): pl.pallas_call(kernel, grid_spec=pltpu.PrefetchScalarGridSpec(num_scalar_...]
    broadcast_in_dim x22 -> x7, local copies, waits for them, and re-layouts: 37.5 us -> 3.75 us  [the longest x3 3.64 us: gather_rows(): parts = jnp.broadcast_to(parts[:, None], (wide, narrow, rows, cols))]
  transfers between devices with their start and end apart: 112 -> 87, of which waited for: 38 -> 33; matrix products, arithmetic and copies ran while one was open for 48% -> 19% of each run, Pallas kernels for 11% -> 20%
where the time goes in v2:
time: 622 us; the launch traced here: 613 us
  waiting for transfers between devices  176 us (28%)
  Pallas kernels  149 us (24%)
  local copies, waits for them, and re-layouts  129 us (21%)
  starting transfers between devices  91 us (15%)
  other arithmetic  35.9 us (6%)
  matrix products  16.7 us (3%)
  between operations  16.1 us (3%)
    ppermute x67, waiting for transfers between devices, swap(): return lax.ppermute(x, 'wide', [(i, i ^ k) for i in range(n)])  148 us
    pallas_call x7, Pallas kernels, call(): pl.pallas_call(kernel, grid_spec=pltpu.PrefetchScalarGridSpec(num_scalar_...  147 us
    unnamed x176, local copies, waits for them, and re-layouts  65.9 us
    ppermute x67, starting transfers between devices, swap(): return lax.ppermute(x, 'wide', [(i, i ^ k) for i in range(n)])  51.5 us
    ppermute x12, waiting for transfers between devices, turn(): return lax.ppermute(x, 'narrow', [(i, (i + k) % n) for i in range(n)])  25.6 us
    all_to_all x5, starting transfers between devices, exchange(): return lax.all_to_all(x, ('wide', 'narrow'), 0, 0)  21 us
    ppermute x12, starting transfers between devices, turn(): return lax.ppermute(x, 'narrow', [(i, (i + k) % n) for i in range(n)])  17.9 us
  transfers between devices with their start and end apart: 87, of which 33 were waited for; matrix products, arithmetic and copies ran while one was open for 19% of the time, Pallas kernels for 20%

profile of v2, /device:TPU:0, one launch (start us, length us, event | category | flops | bytes accessed | tf_op | source)
XLA Modules:
  0.0 613.4 jit_solution(248548776009451000)
XLA Ops:
  13.7 4.1 collective-permute-start.10
  25.0 4.6 all-to-all-start
  29.6 4.7 collective-permute-start.3
  39.1 16.7 %collective-permute-done.3 = bf16[256,1152]{1,0:T(8,128)(2,1)} collective-permute-done((bf16[256,1152]{1,0:T(8,128)(2,1)S(1)}, bf16[256,1152]{1,0:T(8,128)(2,1)}, u32[]{:S(2)}, u32[]{:S(2)}) %collective-permute-start.3) | collective-permute-done | bytes 589856 | tf_op jit(solution)/shard_map/ppermute | solution.py:33
  72.1 4.9 all-to-all-start.1
  81.5 9.4 %shard_map.298 = (bf16[2048,1152]{1,0:T(8,128)(2,1)S(1)}, f32[2048,384]{1,0:T(8,128)S(1)}, f32[2048,384]{1,0:T(8,128)S(1)}, bf16[2048,384]{1,0:T(8,128)(2,1)S(1)}, bf16[2048,128]{1,0:T(8,128)(2,1)S(1)}) custom-call(s32[1]{0:T(128)} %bitcast.1.s_ref, bf16[2048,1152]{1,0:T(8,128)(2,1)} %constant_dynamic-update-slice_fusion.tok, ...), custom_call_target="tpu_custom_call" | custom-call | flops 2013265920 | bytes 18821120 | tf_op jit(solution)/shard_map/pallas_call | solution.py:205
  108.5 4.9 fusion.27.z_r
  114.1 6.3 %collective-permute-done.14 = bf16[1024,128]{1,0:T(8,128)(2,1)S(1)} collective-permute-done((bf16[1024,128]{1,0:T(8,128)(2,1)S(1)}, bf16[1024,128]{1,0:T(8,128)(2,1)S(1)}, u32[]{:S(2)}, u32[]{:S(2)}) %collective-permute-start.14) | collective-permute-done | bytes 262176 | tf_op jit(solution)/shard_map/ppermute | solution.py:33
  131.6 27.3 %shard_map.299 = (f32[2048,384]{1,0:T(8,128)S(1)}, f32[2048,16,384]{2,1,0:T(8,128)}, f32[16,384]{1,0:T(8,128)S(1)}, f32[2048,384]{1,0:T(8,128)S(1)}, bf16[2048,3...) custom-call(s32[1]{0:T(128)} %bitcast.1.s_ref, bf16[2048,128]{1,0:T(8,128)(2,1)S(1)} %copy-done.4, ...), custom_call_target="tpu_custom_call" | custom-call | flops 2113929216 | bytes 69192704 | tf_op jit(solution)/shard_map/pallas_call | solution.py:205
  160.8 4.3 fusion.22
  176.2 8.7 %collective-permute-done.21 = bf16[128,1152]{1,0:T(8,128)(2,1)S(1)} collective-permute-done((bf16[128,1152]{1,0:T(8,128)(2,1)S(1)}, bf16[128,1152]{1,0:T(8,128)(2,1)S(1)}, u32[]{:S(2)}, u32[]{:S(2)}) %collective-permute-start.21) | collective-permute-done | bytes 294944 | tf_op jit(solution)/shard_map/ppermute | solution.py:33
  197.1 8.4 %collective-permute-done.22 = bf16[128,1152]{1,0:T(8,128)(2,1)} collective-permute-done((bf16[128,1152]{1,0:T(8,128)(2,1)}, bf16[128,1152]{1,0:T(8,128)(2,1)}, u32[]{:S(2)}, u32[]{:S(2)}) %collective-permute-start.22) | collective-permute-done | bytes 294944 | tf_op jit(solution)/shard_map/ppermute | solution.py:33
  208.9 5.7 collective-permute-start.28
  215.3 36.4 %collective-permute-done.28 = bf16[256,1152]{1,0:T(8,128)(2,1)S(1)} collective-permute-done((bf16[256,1152]{1,0:T(8,128)(2,1)S(1)}, bf16[256,1152]{1,0:T(8,128)(2,1)S(1)}, u32[]{:S(2)}, u32[]{:S(2)}) %collective-permute-start.28) | collective-permute-done | bytes 589856 | tf_op jit(solution)/shard_map/ppermute | solution.py:33
  255.7 5.5 collective-permute-done.32
  271.4 4.2 reshape.234
  281.6 28.1 %shard_map.300 = (bf16[2048,1152]{1,0:T(8,128)(2,1)}, bf16[2048,1152]{1,0:T(8,128)(2,1)}, bf16[2048,768]{1,0:T(8,128)(2,1)S(1)}, bf16[2048,896]{1,0:T(8,128)(2,1)S(1)}, bf16[2048,1152]{1,0:T(8,128)(2,1)}) custom-call(s32[2]{0:T(128)S(1)} %pad_add_fusion.1.s_ref, bf16[2048,1152]{1,0:T(8,128)(2,1)} %constant_dynamic-update-slice_fusion.10.n_r.a_r, ...), custom_call_target="tpu_custom_call" | custom-call | flops 15703474176 | bytes 34766848 | tf_op jit(solution)/shard_map/pallas_call | solution.py:205
  311.4 4.3 fusion.21
  323.5 6.7 %convolution_convert_fusion = bf16[768,1152]{1,0:T(8,128)(2,1)S(1)} fusion(bf16[2048,768]{1,0:T(8,128)(2,1)S(1)} %copy-done.37, bf16[2048,1152]{1,0:T(8,128)(2,1)} %get-tuple-element.127), kind=kOutput, calls=%fused_computation | convolution fusion | flops 3624763392 | bytes 9633792 | tf_op jit(solution)/shard_map/dot_general | solution.py:185
  334.9 5.2 collective-permute-done.40
  346.4 5.5 collective-permute-done.44
  357.9 8.9 %shard_map.301 = bf16[1152,770]{1,0:T(8,128)(2,1)S(1)} custom-call(s32[1]{0:T(128)} %bitcast.1.s_ref, bf16[2048,1152]{1,0:T(8,128)(2,1)} %constant_dynamic-update-slice_fusion.10.n_r.a_r, bf16[2048,896]{1,0:T(8,128)(2,1)S(1)} %copy-done.35), custom_call_target="tpu_custom_call" | custom-call | flops 4227858432 | bytes 10162688 | tf_op jit(solution)/shard_map/pallas_call | solution.py:205
  375.9 5.5 collective-permute-done.51
  387.5 4.0 reshape.237
  395.1 3.6 collective-permute-start.57
  403.4 53.6 %shard_map.302 = (bf16[2048,384]{1,0:T(8,128)(2,1)S(1)}, bf16[2048,128]{1,0:T(8,128)(2,1)S(1)}, f32[2048,384]{1,0:T(8,128)S(1)}, f32[384,128]{1,0:T(8,128)S(1)},...) custom-call(s32[1]{0:T(128)} %bitcast.1.s_ref, ...), custom_call_target="tpu_custom_call" | custom-call | flops 2264924160 | bytes 73085440 | tf_op jit(solution)/shard_map/pallas_call | solution.py:205
  461.3 25.5 %collective-permute-done.56 = bf16[2,96,1152]{2,1,0:T(8,128)(2,1)} collective-permute-done((bf16[2,96,1152]{2,1,0:T(8,128)(2,1)}, bf16[2,96,1152]{2,1,0:T(8,128)(2,1)}, u32[]{:S(2)}, u32[]{:S(2)}) %collective-permute-start.56) | collective-permute-done | bytes 442400 | tf_op jit(solution)/shard_map/ppermute | solution.py:38
  494.0 5.2 fusion.28
  501.6 4.3 shard_map.303
  519.7 15.2 %shard_map.304 = (bf16[2048,1152]{1,0:T(8,128)(2,1)}, bf16[1152,288]{1,0:T(8,128)(2,1)S(1)}, bf16[288,256]{1,0:T(8,128)(2,1)S(1)}) custom-call(s32[1]{0:T(128)} %bitcast.1.s_ref, bf16[2048,128]{1,0:T(8,128)(2,1)S(1)} %pad_maximum_fusion.3.sel_r, f32[2048,384]{1,0:T(8,128)S(1)} %copy-done.28, f32[2048,384]{1,0:T(8,128)S(1)} %copy-done.33, ...), custom_call_target="tpu_custom_call" | custom-call | flops 5838471168 | bytes 25462784 | tf_op jit(solution)/shard_map/pallas_call | solution.py:205
  540.8 4.6 all-to-all-start.4
  560.6 16.5 %collective-permute-done.73 = bf16[128,1152]{1,0:T(8,128)(2,1)S(1)} collective-permute-done((bf16[128,1152]{1,0:T(8,128)(2,1)S(1)}, bf16[128,1152]{1,0:T(8,128)(2,1)S(1)}, u32[]{:S(2)}, u32[]{:S(2)}) %collective-permute-start.73) | collective-permute-done | bytes 294944 | tf_op jit(solution)/shard_map/ppermute | solution.py:33
  (468 shorter events, 244.7 us)
Async XLA Ops:
  21.3 37.0 %collective-permute-start = (bf16[256,1152]{1,0:T(8,128)(2,1)}, bf16[256,1152]{1,0:T(8,128)(2,1)}, u32[]{:S(2)}, u32[]{:S(2)}) collective-permute-start(bf16[256,1152]{1,0:T(8,128)(2,1)} %bitcast.128), channel_id=1, source_target_pairs={{0,4},{4,0},{8,12},{12,8},{16,20},{20,16},{24,28},{28,24},{1,5},{5... | collective-permute-start | bytes 1769480 | tf_op jit(solution)/shard_map/ppermute | solution.py:33
  25.0 45.6 %all-to-all-start = ((bf16[32,36,290]{2,1,0:T(8,128)(2,1)}), bf16[32,36,290]{2,1,0:T(8,128)(2,1)S(1)}, u32[]{:S(2)}, u32[]{:S(2)}) async-start(bf16[32,36,290]{2,1,0:T(8,128)(2,1)} %bitcast.6), calls=%async_computation | async-start | bytes 1966080 | tf_op jit(solution)/shard_map/all_to_all | solution.py:155
  29.6 26.3 %collective-permute-start.3 = (bf16[256,1152]{1,0:T(8,128)(2,1)S(1)}, bf16[256,1152]{1,0:T(8,128)(2,1)}, u32[]{:S(2)}, u32[]{:S(2)}) collective-permute-start(bf16[256,1152]{1,0:T(8,128)(2,1)S(1)} %bitcast.129), channel_id=1, source_target_pairs={{0,16},{4,20},{8,24},{12,28},{16,0},{20,4},{24,8},{28,12},{1,17},{... | collective-permute-start | bytes 1769480 | tf_op jit(solution)/shard_map/ppermute | solution.py:33
  38.1 26.4 %collective-permute-start.2 = (bf16[256,1152]{1,0:T(8,128)(2,1)S(1)}, bf16[256,1152]{1,0:T(8,128)(2,1)S(1)}, u32[]{:S(2)}, u32[]{:S(2)}) collective-permute-start(bf16[256,1152]{1,0:T(8,128)(2,1)S(1)} %collective-permute-done.1), channel_id=1, source_target_pairs={{0,4},{4,0},{8,12},{12,8},{16,20},{20,16},{24,28},{28,24},{1,5},{5... | collective-permute-start | bytes 1769480 | tf_op jit(solution)/shard_map/ppermute | solution.py:33
  38.4 23.5 %collective-permute-start.5 = (bf16[128,1152]{1,0:T(8,128)(2,1)S(1)}, bf16[128,1152]{1,0:T(8,128)(2,1)S(1)}, u32[]{:S(2)}, u32[]{:S(2)}) collective-permute-start(bf16[128,1152]{1,0:T(8,128)(2,1)S(1)} %slice.354), channel_id=1, source_target_pairs={{0,16},{4,20},{8,24},{12,28},{16,0},{20,4},{24,8},{28,12},{1,17},{... | collective-permute-start | bytes 884744 | tf_op jit(solution)/shard_map/ppermute | solution.py:33
  72.1 28.6 %all-to-all-start.1 = ((bf16[32,36,288]{2,1,0:T(8,128)(2,1)}), bf16[32,36,288]{2,1,0:T(8,128)(2,1)S(1)}, u32[]{:S(2)}, u32[]{:S(2)}) async-start(bf16[32,36,288]{2,1,0:T(8,128)(2,1)} %bitcast.132), calls=%async_computation.1 | async-start | bytes 1966080 | tf_op jit(solution)/shard_map/all_to_all | solution.py:155
  77.0 191.6 %all-gather.6.cloned.1.call-start = ((), (), s32[]{:S(2)}) async-start(), calls=%async_computation.8 | async-start | bytes 2211840 | tf_op jit(solution)/shard_map/all_gather | solution.py:756
  125.1 153.5 %all-gather.4.cloned.1.call-start = ((), (), s32[]{:S(2)}) async-start(), calls=%async_computation.6 | async-start | bytes 5898240 | tf_op jit(solution)/shard_map/all_gather | solution.py:760
  171.1 26.0 %collective-permute-start.17 = (bf16[256,1152]{1,0:T(8,128)(2,1)}, bf16[256,1152]{1,0:T(8,128)(2,1)}, u32[]{:S(2)}, u32[]{:S(2)}) collective-permute-start(bf16[256,1152]{1,0:T(8,128)(2,1)} %get-tuple-element.287), channel_id=1, source_target_pairs={{0,4},{4,0},{8,12},{12,8},{16,20},{20,16},{24,28},{28,24},{1,5},{5... | collective-permute-start | bytes 1769480 | tf_op jit(solution)/shard_map/ppermute | solution.py:33
  173.4 23.7 %collective-permute-start.19 = (bf16[128,1152]{1,0:T(8,128)(2,1)}, bf16[128,1152]{1,0:T(8,128)(2,1)}, u32[]{:S(2)}, u32[]{:S(2)}) collective-permute-start(bf16[128,1152]{1,0:T(8,128)(2,1)} %slice.477), channel_id=1, source_target_pairs={{0,8},{4,12},{8,0},{12,4},{16,24},{20,28},{24,16},{28,20},{1,9},{5... | collective-permute-start | bytes 884744 | tf_op jit(solution)/shard_map/ppermute | solution.py:33
  174.7 22.5 %collective-permute-start.26 = (bf16[128,1152]{1,0:T(8,128)(2,1)}, bf16[128,1152]{1,0:T(8,128)(2,1)}, u32[]{:S(2)}, u32[]{:S(2)}) collective-permute-start(bf16[128,1152]{1,0:T(8,128)(2,1)} %slice.476), channel_id=1, source_target_pairs={{0,16},{4,20},{8,24},{12,28},{16,0},{20,4},{24,8},{28,12},{1,17},{... | collective-permute-start | bytes 884744 | tf_op jit(solution)/shard_map/ppermute | solution.py:33
  185.7 19.8 %collective-permute-start.22 = (bf16[128,1152]{1,0:T(8,128)(2,1)}, bf16[128,1152]{1,0:T(8,128)(2,1)}, u32[]{:S(2)}, u32[]{:S(2)}) collective-permute-start(bf16[128,1152]{1,0:T(8,128)(2,1)} %fusion.12), channel_id=1, source_target_pairs={{0,8},{4,12},{8,0},{12,4},{16,24},{20,28},{24,16},{28,20},{1,9},{5... | collective-permute-start | bytes 884744 | tf_op jit(solution)/shard_map/ppermute | solution.py:33
  187.0 18.5 %collective-permute-start.25 = (bf16[128,1152]{1,0:T(8,128)(2,1)}, bf16[128,1152]{1,0:T(8,128)(2,1)}, u32[]{:S(2)}, u32[]{:S(2)}) collective-permute-start(bf16[128,1152]{1,0:T(8,128)(2,1)} %fusion.11), channel_id=1, source_target_pairs={{0,16},{4,20},{8,24},{12,28},{16,0},{20,4},{24,8},{28,12},{1,17},{... | collective-permute-start | bytes 884744 | tf_op jit(solution)/shard_map/ppermute | solution.py:33
  193.6 77.8 %all-to-all-start.2 = ((bf16[32,36,770]{2,1,0:T(8,128)(2,1)}), bf16[32,36,770]{2,1,0:T(8,128)(2,1)}, u32[]{:S(2)}, u32[]{:S(2)}) async-start(bf16[32,36,770]{2,1,0:T(8,128)(2,1)} %bitcast.130), calls=%async_computation.2 | async-start | bytes 4587520 | tf_op jit(solution)/shard_map/all_to_all | solution.py:155
  208.9 42.7 %collective-permute-start.28 = (bf16[256,1152]{1,0:T(8,128)(2,1)S(1)}, bf16[256,1152]{1,0:T(8,128)(2,1)S(1)}, u32[]{:S(2)}, u32[]{:S(2)}) collective-permute-start(bf16[256,1152]{1,0:T(8,128)(2,1)S(1)} %get-tuple-element.270), channel_id=1, source_target_pairs={{0,8},{4,12},{8,0},{12,4},{16,24},{20,28},{24,16},{28,20},{1,9},{5... | collective-permute-start | bytes 1769480 | tf_op jit(solution)/shard_map/ppermute | solution.py:33
  214.6 39.0 %collective-permute-start.30 = (bf16[256,1152]{1,0:T(8,128)(2,1)S(1)}, bf16[256,1152]{1,0:T(8,128)(2,1)S(1)}, u32[]{:S(2)}, u32[]{:S(2)}) collective-permute-start(bf16[256,1152]{1,0:T(8,128)(2,1)S(1)} %get-tuple-element.270), channel_id=1, source_target_pairs={{0,16},{4,20},{8,24},{12,28},{16,0},{20,4},{24,8},{28,12},{1,17},{... | collective-permute-start | bytes 1769480 | tf_op jit(solution)/shard_map/ppermute | solution.py:33
  214.6 39.4 %collective-permute-start.27 = (bf16[256,1152]{1,0:T(8,128)(2,1)S(1)}, bf16[256,1152]{1,0:T(8,128)(2,1)S(1)}, u32[]{:S(2)}, u32[]{:S(2)}) collective-permute-start(bf16[256,1152]{1,0:T(8,128)(2,1)S(1)} %get-tuple-element.270), channel_id=1, source_target_pairs={{0,4},{4,0},{8,12},{12,8},{16,20},{20,16},{24,28},{28,24},{1,5},{5... | collective-permute-start | bytes 1769480 | tf_op jit(solution)/shard_map/ppermute | solution.py:33
  316.7 26.5 %collective-permute-start.36 = (bf16[256,1152]{1,0:T(8,128)(2,1)}, bf16[256,1152]{1,0:T(8,128)(2,1)S(1)}, u32[]{:S(2)}, u32[]{:S(2)}) collective-permute-start(bf16[256,1152]{1,0:T(8,128)(2,1)} %get-tuple-element.286), channel_id=1, source_target_pairs={{0,4},{4,0},{8,12},{12,8},{16,20},{20,16},{24,28},{28,24},{1,5},{5... | collective-permute-start | bytes 1769480 | tf_op jit(solution)/shard_map/ppermute | solution.py:33
  391.5 95.4 %all-to-all-start.3 = ((bf16[32,36,770]{2,1,0:T(8,128)(2,1)}), bf16[32,36,770]{2,1,0:T(8,128)(2,1)}, u32[]{:S(2)}, u32[]{:S(2)}) async-start(bf16[32,36,770]{2,1,0:T(8,128)(2,1)} %reshape.237), calls=%async_computation.4 | async-start | bytes 4587520 | tf_op jit(solution)/shard_map/all_to_all | solution.py:155
  395.0 209.4 %reduce-scatter.2.cloned.1.call-start = ((), (), s32[]{:S(2)}) async-start(), calls=%async_computation.7 | async-start | bytes 5308416 | tf_op jit(solution)/shard_map/reduce_scatter | solution.py:787
  395.1 66.3 %collective-permute-start.57 = (bf16[2,96,1152]{2,1,0:T(8,128)(2,1)}, bf16[2,96,1152]{2,1,0:T(8,128)(2,1)}, u32[]{:S(2)}, u32[]{:S(2)}) collective-permute-start(bf16[2,96,1152]{2,1,0:T(8,128)(2,1)} %get-tuple-element.144), channel_id=1, source_target_pairs={{0,3},{1,0},{2,1},{3,2},{4,7},{5,4},{6,5},{7,6},{8,11},{9,8},{10,9... | collective-permute-start | bytes 1327112 | tf_op jit(solution)/shard_map/ppermute | solution.py:38
  398.7 88.2 %collective-permute-start.56 = (bf16[2,96,1152]{2,1,0:T(8,128)(2,1)}, bf16[2,96,1152]{2,1,0:T(8,128)(2,1)}, u32[]{:S(2)}, u32[]{:S(2)}) collective-permute-start(bf16[2,96,1152]{2,1,0:T(8,128)(2,1)} %get-tuple-element.143), channel_id=1, source_target_pairs={{0,2},{1,3},{2,0},{3,1},{4,6},{5,7},{6,4},{7,5},{8,10},{9,11},{10,... | collective-permute-start | bytes 1327112 | tf_op jit(solution)/shard_map/ppermute | solution.py:38
  398.7 88.2 %collective-permute-start.55 = (bf16[2,96,1152]{2,1,0:T(8,128)(2,1)}, bf16[2,96,1152]{2,1,0:T(8,128)(2,1)}, u32[]{:S(2)}, u32[]{:S(2)}) collective-permute-start(bf16[2,96,1152]{2,1,0:T(8,128)(2,1)} %get-tuple-element.142), channel_id=1, source_target_pairs={{0,1},{1,2},{2,3},{3,0},{4,5},{5,6},{6,7},{7,4},{8,9},{9,10},{10,1... | collective-permute-start | bytes 1327112 | tf_op jit(solution)/shard_map/ppermute | solution.py:38
  510.9 24.0 %collective-permute-start.65 = (bf16[72,1152]{1,0:T(8,128)(2,1)}, bf16[72,1152]{1,0:T(8,128)(2,1)S(1)}, u32[]{:S(2)}, u32[]{:S(2)}) collective-permute-start(bf16[72,1152]{1,0:T(8,128)(2,1)} %get-tuple-element.168), channel_id=1, source_target_pairs={{0,3},{1,0},{2,1},{3,2},{4,7},{5,4},{6,5},{7,6},{8,11},{9,8},{10,9... | collective-permute-start | bytes 497672 | tf_op jit(solution)/shard_map/ppermute | solution.py:38
  510.9 23.9 %collective-permute-start.64 = (bf16[72,1152]{1,0:T(8,128)(2,1)S(1)}, bf16[72,1152]{1,0:T(8,128)(2,1)S(1)}, u32[]{:S(2)}, u32[]{:S(2)}) collective-permute-start(bf16[72,1152]{1,0:T(8,128)(2,1)S(1)} %copy-done.62), channel_id=1, source_target_pairs={{0,2},{1,3},{2,0},{3,1},{4,6},{5,7},{6,4},{7,5},{8,10},{9,11},{10,... | collective-permute-start | bytes 497672 | tf_op jit(solution)/shard_map/ppermute | solution.py:38
  511.0 23.9 %collective-permute-start.63 = (bf16[72,1152]{1,0:T(8,128)(2,1)S(1)}, bf16[72,1152]{1,0:T(8,128)(2,1)S(1)}, u32[]{:S(2)}, u32[]{:S(2)}) collective-permute-start(bf16[72,1152]{1,0:T(8,128)(2,1)S(1)} %copy-done.61), channel_id=1, source_target_pairs={{0,1},{1,2},{2,3},{3,0},{4,5},{5,6},{6,7},{7,4},{8,9},{9,10},{10,1... | collective-permute-start | bytes 497672 | tf_op jit(solution)/shard_map/ppermute | solution.py:38
  540.8 51.7 %all-to-all-start.4 = ((bf16[32,36,576]{2,1,0:T(8,128)(2,1)}), bf16[32,36,576]{2,1,0:T(8,128)(2,1)}, u32[]{:S(2)}, u32[]{:S(2)}) async-start(bf16[32,36,576]{2,1,0:T(8,128)(2,1)} %reshape.241), calls=%async_computation.5 | async-start | bytes 3276800 | tf_op jit(solution)/shard_map/all_to_all | solution.py:155
  547.1 33.2 %collective-permute-start.66 = (bf16[256,1152]{1,0:T(8,128)(2,1)}, bf16[256,1152]{1,0:T(8,128)(2,1)S(1)}, u32[]{:S(2)}, u32[]{:S(2)}) collective-permute-start(bf16[256,1152]{1,0:T(8,128)(2,1)} %get-tuple-element.279), channel_id=1, source_target_pairs={{0,4},{4,0},{8,12},{12,8},{16,20},{20,16},{24,28},{28,24},{1,5},{5... | collective-permute-start | bytes 1769480 | tf_op jit(solution)/shard_map/ppermute | solution.py:33
  553.9 23.3 %collective-permute-start.73 = (bf16[128,1152]{1,0:T(8,128)(2,1)S(1)}, bf16[128,1152]{1,0:T(8,128)(2,1)S(1)}, u32[]{:S(2)}, u32[]{:S(2)}) collective-permute-start(bf16[128,1152]{1,0:T(8,128)(2,1)S(1)} %get-tuple-element.302), channel_id=1, source_target_pairs={{0,8},{4,12},{8,0},{12,4},{16,24},{20,28},{24,16},{28,20},{1,9},{5... | collective-permute-start | bytes 884744 | tf_op jit(solution)/shard_map/ppermute | solution.py:33
  558.0 20.7 %collective-permute-start.70 = (bf16[128,1152]{1,0:T(8,128)(2,1)S(1)}, bf16[128,1152]{1,0:T(8,128)(2,1)S(1)}, u32[]{:S(2)}, u32[]{:S(2)}) collective-permute-start(bf16[128,1152]{1,0:T(8,128)(2,1)S(1)} %get-tuple-element.303), channel_id=1, source_target_pairs={{0,16},{4,20},{8,24},{12,28},{16,0},{20,4},{24,8},{28,12},{1,17},{... | collective-permute-start | bytes 884744 | tf_op jit(solution)/shard_map/ppermute | solution.py:33
  559.5 25.6 %collective-permute-start.68 = (bf16[128,1152]{1,0:T(8,128)(2,1)S(1)}, bf16[128,1152]{1,0:T(8,128)(2,1)S(1)}, u32[]{:S(2)}, u32[]{:S(2)}) collective-permute-start(bf16[128,1152]{1,0:T(8,128)(2,1)S(1)} %slice.473), channel_id=1, source_target_pairs={{0,8},{4,12},{8,0},{12,4},{16,24},{20,28},{24,16},{28,20},{1,9},{5... | collective-permute-start | bytes 884744 | tf_op jit(solution)/shard_map/ppermute | solution.py:33
  560.2 27.2 %collective-permute-start.75 = (bf16[128,1152]{1,0:T(8,128)(2,1)S(1)}, bf16[128,1152]{1,0:T(8,128)(2,1)S(1)}, u32[]{:S(2)}, u32[]{:S(2)}) collective-permute-start(bf16[128,1152]{1,0:T(8,128)(2,1)S(1)} %slice.472), channel_id=1, source_target_pairs={{0,16},{4,20},{8,24},{12,28},{16,0},{20,4},{24,8},{28,12},{1,17},{... | collective-permute-start | bytes 884744 | tf_op jit(solution)/shard_map/ppermute | solution.py:33
  (127 other events, 992.6 us)
Sparse Core Ops, SparseCore 0:
  125.2 38.7 all-gather.5
  166.4 82.6 all-gather.3
  508.1 68.2 reduce-scatter.1

commit v3 on v2

--- a/solution.py
+++ b/solution.py
@@ -16,7 +16,7 @@
 EXPERTS = 2
 EPSILON = 1e-05
 TIME_BLOCK = 128
-VMEM = 40 * 2**20
+VMEM = 60 * 2**20
 LANES = 128
 LN2 = math.log(2.0)
 
@@ -42,10 +42,14 @@
     return lax.dynamic_index_in_dim(x, i, axis, False)
 
 
+def blocks_of(x):
+    return [[b] for b in jnp.split(x, lax.axis_size("wide"), axis=0)]
+
+
 def gather_wide(block, meanwhile=None):
     if not relative():
         made = meanwhile(block) if meanwhile else ()
-        return lax.all_gather(block, "wide", axis=0, tiled=True), made
+        return blocks_of(lax.all_gather(block, "wide", axis=0, tiled=True)), made
     half = block.shape[0] // 2
     mate = swap(block, 1)
     a, b = swap(block, 2), swap(block, 4)
@@ -54,31 +58,31 @@
         made = meanwhile(block)
         a, b, made = lax.optimization_barrier((a, b, made))
     c0, c1 = swap(a[:half], 4), swap(b[half:], 2)
-    out = jnp.concatenate(
-        [block, mate, a, swap(a, 1), b, swap(b, 1), c0, c1, swap(c0, 1), swap(c1, 1)], axis=0
-    )
+    out = [[block], [mate], [a], [swap(a, 1)], [b], [swap(b, 1)], [c0, c1], [swap(c0, 1), swap(c1, 1)]]
     return out, made
 
 
-def scatter_wide(partial):
+def scatter_wide(parts, beside=(), early=()):
     if not relative():
-        return lax.psum_scatter(partial, "wide", scatter_dimension=0, tiled=True).astype(f32)
-    rows = partial.shape[0] // 8
-    half = rows // 2
-    parts = partial.reshape(8, rows, partial.shape[1])
+        whole = jnp.concatenate(parts, axis=0)
+        total = lax.psum_scatter(whole, "wide", scatter_dimension=0, tiled=True).astype(f32)
+        return total, beside(total) if callable(beside) else beside, early
+    half = parts[0].shape[0] // 2
 
     def summed(q):
         return parts[2 * q].astype(f32) + swap(parts[2 * q + 1], 1).astype(f32)
 
     far = summed(3).astype(bf16)
     r0, r1 = swap(far[:half], 2), swap(far[half:], 4)
+    r0, r1, early = lax.optimization_barrier((r0, r1, early))
     sx, sy = summed(1), summed(2)
     x0, y1 = swap(sx[:half].astype(bf16), 2), swap(sy[half:].astype(bf16), 4)
     x1 = swap((sx[half:] + r1.astype(f32)).astype(bf16), 2)
     y0 = swap((sy[:half] + r0.astype(f32)).astype(bf16), 4)
+    x1, y0, beside = lax.optimization_barrier((x1, y0, beside(r0) if callable(beside) else beside))
     x = jnp.concatenate([x0, x1], axis=0).astype(f32)
     y = jnp.concatenate([y0, y1], axis=0).astype(f32)
-    return summed(0) + x + y
+    return summed(0) + x + y, beside, early
 
 
 def reduce_wide(partial, meanwhile):
@@ -113,10 +117,38 @@
     return jnp.pad(x, pads)
 
 
-def gather_channels(x, splits, total):
+def ordered_rows(pieces, group, cols):
     n, z = lax.axis_size("narrow"), lax.axis_index("narrow")
-    rows, cols = x.shape
-    pieces = [x] + [turn(x, k) for k in range(1, n)]
+    rows, width = pieces[0].shape
+    order = jnp.stack([(z - k) % n * group for k in range(n)]).astype(jnp.int32)
+
+    def kernel(order_ref, *refs):
+        out = refs[n]
+        r = lax.broadcasted_iota(jnp.int32, (n * rows, rows), 0)
+        j = lax.broadcasted_iota(jnp.int32, (n * rows, rows), 1)
+        spot = j
+        for i in range(1, rows // group):
+            spot = spot + jnp.where(j >= i * group, (n - 1) * group, 0)
+        value = jnp.zeros((n * rows, width), f32)
+        for k in range(n):
+            spots = jnp.where(r == spot + order_ref[k], 1.0, 0.0).astype(bf16)
+            value = value + jnp.dot(spots, refs[k][...], preferred_element_type=f32)
+        out[...] = jnp.zeros(out.shape, bf16)
+        out[:, :width] = value.astype(bf16)
+
+    vmem = pl.BlockSpec(memory_space=pltpu.VMEM)
+    return pl.pallas_call(
+        kernel,
+        in_specs=[pl.BlockSpec(memory_space=pltpu.SMEM)] + [vmem] * n,
+        out_specs=vmem,
+        out_shape=jax.ShapeDtypeStruct((n * rows, cols), bf16),
+        compiler_params=pltpu.CompilerParams(vmem_limit_bytes=VMEM),
+    )(order, *pieces)
+
+
+def gather_channels(pieces, splits, total):
+    n, z = lax.axis_size("narrow"), lax.axis_index("narrow")
+    rows, cols = pieces[0].shape
     order = jnp.stack([(z - k) % n * rows for k in range(n)]).astype(jnp.int32)
 
     def kernel(order_ref, *refs):
@@ -142,6 +174,10 @@
     )(order, *pieces)
 
 
+def turns(x):
+    return [x] + [turn(x, k) for k in range(1, lax.axis_size("narrow"))]
+
+
 def turned(pieces):
     return [pieces[0]] + [turn(pieces[k], k) for k in range(1, len(pieces))]
 
@@ -163,10 +199,9 @@
     return got.reshape(wide * narrow * rows, cols)
 
 
-def scatter_rows(grad, rows):
-    wide, narrow = lax.axis_size("wide"), lax.axis_size("narrow")
-    got = exchange(grad.reshape(wide * narrow, rows, grad.shape[1]))
-    return got.reshape(wide, narrow, rows, grad.shape[1])
+def scatter_rows(grad):
+    got = exchange(grad)
+    return got.reshape(lax.axis_size("wide"), lax.axis_size("narrow"), *grad.shape[1:])
 
 
 def summed_rows(got):
@@ -193,8 +228,10 @@
     return jnp.maximum(v, 0.0) + jnp.log1p(jnp.exp(-jnp.abs(v)))
 
 
-def call(kernel, grid, flip, ins, outs, scratch, flops, exps=0):
+def call(kernel, grid, flip, ins, outs, scratch, flops, exps=0, aliases={}):
     def spec(block, where):
+        if block is None:
+            return pl.BlockSpec(memory_space=pltpu.HBM)
         if where is None:
             zeros = (0,) * len(block)
             return pl.BlockSpec(block, lambda i, s: zeros)
@@ -212,22 +249,76 @@
             scratch_shapes=scratch,
         ),
         out_shape=[jax.ShapeDtypeStruct(o[0], o[1]) for o in outs],
+        input_output_aliases=aliases,
         compiler_params=pltpu.CompilerParams(vmem_limit_bytes=VMEM),
-        cost_estimate=pl.CostEstimate(flops=flops, bytes_accessed=size, transcendentals=exps),
+        cost_estimate=pl.CostEstimate(flops=flops // 64, bytes_accessed=size // 64, transcendentals=0),
     )(flip, *[a for a, _, _ in ins])
 
 
+def fetch_blocks(groups, held, sems, shift):
+    for k, group in enumerate(groups):
+        at = 0
+        for ref in group:
+            n = ref.shape[0]
+            pltpu.make_async_copy(ref, held.at[k ^ shift, pl.ds(at, n)], sems.at[k ^ shift]).start()
+            at += n
+
+
+def wait_block(held, sems, i):
+    pltpu.make_async_copy(held.at[i], held.at[i], sems.at[i]).wait()
+
+
+def send_rows(value, stage, sems, outs, step, steps, block, at):
+    slot = step % 2
+    n = value.shape[0]
+
+    def sent(k):
+        return pltpu.make_async_copy(stage.at[k], stage.at[k], sems.at[k])
+
+    @pl.when(step >= 2)
+    def _():
+        sent(slot).wait()
+
+    stage[slot] = value
+    for k, out in enumerate(outs):
+
+        @pl.when(block == k)
+        def _(out=out):
+            pltpu.make_async_copy(stage.at[slot], out.at[pl.ds(at, n)], sems.at[slot]).start()
+
+    @pl.when(step == steps - 1)
+    def _():
+        sent(0).wait()
+        sent(1).wait()
+
+
+def taken(refs, lengths):
+    out, at = [], 0
+    for n in lengths:
+        out.append(refs[at : at + n])
+        at += n
+    return out, refs[at:]
+
+
 def front(flip, tokens, gain, weight_x, taps, shift, weight_sel):
-    length, wid = tokens.shape[0], weight_x.shape[1]
+    wid = weight_x.shape[1]
     blocks = lax.axis_size("wide")
-    rows = length // blocks
-
-    def kernel(s_ref, tok, gain_r, wx, taps_r, shift_r, wsel, normed, proj, conv, act, part, pad):
-        @pl.when(pl.program_id(0) == 0)
+    rows = tokens[0][0].shape[0]
+    length = rows * blocks
+    counts = [len(g) for g in tokens]
+
+    def kernel(s_ref, *refs):
+        groups, refs = taken(refs, counts)
+        gain_r, wx, taps_r, shift_r, wsel, normed, proj, conv, act, part, pad, held, sems = refs
+        i = pl.program_id(0)
+
+        @pl.when(i == 0)
         def _():
+            fetch_blocks(groups, held, sems, s_ref[0])
             pad[:8, :] = jnp.zeros((8, wid), f32)
 
-        values = tok[...].astype(f32)
+        wait_block(held, sems, i)
+        values = held[i].astype(f32)
         inverse = lax.rsqrt(jnp.mean(values * values, axis=-1, keepdims=True) + EPSILON)
         low = (values * inverse * gain_r[...]).astype(bf16)
         normed[...] = low
@@ -251,7 +342,7 @@
         blocks,
         flip,
         [
-            (tokens, (rows, D), rel),
+            *[(part, None, None) for group in tokens for part in group],
             (gain, (1, D), None),
             (weight_x, (D, wid), None),
             (taps, (CONV, wid), None),
@@ -265,7 +356,11 @@
             ((length, wid), bf16, (rows, wid), here),
             ((length, LANES), bf16, (rows, LANES), here),
         ],
-        [pltpu.VMEM((rows + 8, wid), f32)],
+        [
+            pltpu.VMEM((rows + 8, wid), f32),
+            pltpu.VMEM((blocks, rows, D), bf16),
+            pltpu.SemaphoreType.DMA((blocks,)),
+        ],
         2 * length * wid * (D + LANES),
     )
 
@@ -294,14 +389,20 @@
 OUT_AT = DT_RANK + NS
 
 
-def middle(flip, sel, act, proj_z, weight_step, shift, skip, a2, weight_out):
+def middle(flip, sel, act, normed, weight_z, weight_step, shift, skip, a2, weight_out):
     length, wid = act.shape
     blocks = length // TIME_BLOCK
     per = blocks // lax.axis_size("wide")
 
+    wide = lax.axis_size("wide")
+
     def kernel(
-        s_ref, sel_r, act_r, z_r, wstep, shift_r, skip_r, a_r, wout, lin_o, kept, end, mixed, gated_o, part, state, dt_s, u_s, y_s
+        s_ref, sel_r, act_r, n_r, wz, wstep, shift_r, skip_r, a_r, wout, z_o, lin_o, kept, end, mixed, gated_o, *refs
     ):
+        (parts,), refs = taken(refs, [wide])
+        state, dt_s, u_s, y_s, stage, sems = refs
+        i = pl.program_id(0)
+
         @pl.when(pl.program_id(0) == 0)
         def _():
             state[...] = jnp.zeros_like(state)
@@ -329,10 +430,12 @@
         end[...] = h
         out = y_s[...] + skip_r[...] * act_r[...].astype(f32)
         mixed[...] = out
-        z = z_r[...]
+        z = mm(n_r[...], wz[...])
+        z_o[...] = z
         gated = (out * z * sigmoid(z)).astype(bf16)
         gated_o[...] = gated
-        part[...] = mm(gated, wout[...]).astype(bf16)
+        value = mm(gated, wout[...]).astype(bf16)
+        send_rows(value, stage, sems, parts, i, blocks, (i // per) ^ s_ref[0], i % per * TIME_BLOCK)
 
     here = lambda i, s: i
     rel = lambda i, s: ((i // per) ^ s) * per + i % per
@@ -344,7 +447,8 @@
         [
             (sel, (TIME_BLOCK, LANES), here),
             (act, row, here),
-            (proj_z, row, rel),
+            (normed, (TIME_BLOCK, D), rel),
+            (weight_z, (D, wid), None),
             (weight_step, (wid, LANES), None),
             (shift, (1, wid), None),
             (skip, (1, wid), None),
@@ -353,31 +457,44 @@
         ],
         [
             ((length, wid), f32, row, here),
+            ((length, wid), f32, row, here),
             ((length, NS, wid), f32, (TIME_BLOCK, NS, wid), here),
             ((NS, wid), f32, (NS, wid), None),
             ((length, wid), f32, row, here),
-            ((length, wid), bf16, row, rel),
-            ((length, D), bf16, (TIME_BLOCK, D), rel),
-        ],
-        [pltpu.VMEM((NS, wid), f32)] + [pltpu.VMEM(row, f32)] * 3,
-        length * wid * (8 * NS + 2 * D + 2 * LANES),
+            ((length, wid), bf16, row, here),
+            *[((length // wide, D), bf16, None, None)] * wide,
+        ],
+        [pltpu.VMEM((NS, wid), f32)]
+        + [pltpu.VMEM(row, f32)] * 3
+        + [pltpu.VMEM((2, TIME_BLOCK, D), bf16), pltpu.SemaphoreType.DMA((2,))],
+        length * wid * (8 * NS + 4 * D + 2 * LANES),
         length * NS * wid,
     )
 
 
-def experts(span, normed, cot, up, down, ff):
-    length = normed.shape[0]
-    blocks = lax.axis_size("wide")
-    rows = length // blocks
+def experts(span, base, normed, cot, up, down, ff, whole):
+    rows = normed[0].shape[0]
+    length = rows * lax.axis_size("wide")
+    blocks = len(normed)
     cols = up.shape[1]
 
-    def kernel(s_ref, n_r, cot_r, up_r, down_r, out_part, back_part, hid_o, both_o, dex_o):
+    def kernel(s_ref, *refs):
+        (n_refs, (cot_r, up_r, down_r), _, backs, outs), refs = taken(
+            refs, [blocks, 3, len(whole), blocks, blocks]
+        )
+        n_o, hid_o, both_o, dex_o = refs
         i = pl.program_id(0)
-        position = (i ^ s_ref[0]) * rows + lax.broadcasted_iota(jnp.int32, (rows, 1), 0)
+        for k, ref in enumerate(n_refs):
+
+            @pl.when(i == k)
+            def _(ref=ref):
+                n_o[...] = ref[...]
+
+        position = ((i + base) ^ s_ref[0]) * rows + lax.broadcasted_iota(jnp.int32, (rows, 1), 0)
         cot_b = cot_r[...]
         second = cot_b[:, D : D + 1] > 0.5
         upstream = jnp.where(position < s_ref[1], cot_b[:, :D], jnp.zeros((), bf16))
-        raised = mm(n_r[...], up_r[...])
+        raised = mm(n_o[...], up_r[...])
         first_l, second_l = raised[:, EXPERTS * ff : EXPERTS * ff + 1], raised[:, EXPERTS * ff + 1 : EXPERTS * ff + 2]
         lead = jnp.where(second, second_l - first_l, first_l - second_l)
         gate = sigmoid(lead)
@@ -392,7 +509,13 @@
             [jnp.where(second, 0.0, hid_f), jnp.where(second, hid_f, 0.0)], axis=1
         ).astype(bf16)
         hid_o[...] = both
-        out_part[...] = (gate * mm(both, down_r[...])).astype(bf16)
+        value = (gate * mm(both, down_r[...])).astype(bf16)
+        for k, ref in enumerate(outs):
+
+            @pl.when(i == k)
+            def _(ref=ref, value=value):
+                ref[...] = value
+
         dex_o[...] = (gate * upstream.astype(f32)).astype(bf16)
         lowered = mm_t(upstream, down_r[...])
         d_hid = jnp.where(second, lowered[:, ff:], lowered[:, :ff])
@@ -406,30 +529,40 @@
             [jnp.where(second, 0.0, d_pre), jnp.where(second, d_pre, 0.0), d_logits], axis=1
         ).astype(bf16)
         both_o[...] = d_both
-        back_part[...] = mm_t(d_both, up_r[...]).astype(bf16)
-
-    here = lambda i, s: i
-    return call(
+        value = mm_t(d_both, up_r[...]).astype(bf16)
+        for k, ref in enumerate(backs):
+
+            @pl.when(i == k)
+            def _(ref=ref):
+                ref[...] = value
+
+    here = lambda i, s: i + base
+    place = lambda i, s: (i + base) ^ s
+    first = 1 + blocks + 3
+    made = call(
         kernel,
         blocks,
         span,
         [
-            (normed, (rows, D), here),
-            (cot, (rows, D + LANES), lambda i, s: i ^ s),
+            *[(n, (rows, D), None) for n in normed],
+            (cot, (rows, D + LANES), place),
             (up, up.shape, None),
             (down, down.shape, None),
+            *[(x, None, None) for x in whole],
         ],
         [
-            ((length, D), bf16, (rows, D), lambda i, s: i ^ s),
+            *[((rows, D), bf16, (rows, D), None)] * (2 * blocks),
             ((length, D), bf16, (rows, D), here),
             ((length, EXPERTS * ff), bf16, (rows, EXPERTS * ff), here),
             ((length, cols), bf16, (rows, cols), here),
             ((length, D), bf16, (rows, D), here),
         ],
         [],
-        4 * length * D * (cols + EXPERTS * ff),
-        3 * length * ff,
-    )
+        4 * blocks * rows * D * (cols + EXPERTS * ff),
+        3 * blocks * rows * ff,
+        {first + k: 2 * blocks + k for k in range(len(whole))},
+    )
+    return made[:blocks], made[blocks : 2 * blocks], made[2 * blocks :]
 
 
 def back(flip, d_mix, weight_out, sel, act, proj_z, lin, mixed, kept, end, weight_step, skip, a2):
@@ -437,13 +570,20 @@
     blocks = length // TIME_BLOCK
     per = blocks // lax.axis_size("wide")
 
-    def kernel(
-        s_ref, mix_r, wout, sel_r, act_r, z_r, lin_r, mixed_r, kept_r, end_r, wstep, skip_r, a_r,
-        dz_o, part, dact_o, gstep_o, da_o, dskip_o, dbias_o,
-        lam_s, next_s, pb_s, pc_s, dt_s, u_s, dy_s, s1_s, s2_s, turned_s,
-    ):
+    counts = [len(g) for g in d_mix]
+
+    def kernel(s_ref, *refs):
+        mix_groups, refs = taken(refs, counts)
+        (
+            wout, sel_r, act_r, z_r, lin_r, mixed_r, kept_r, end_r, wstep, skip_r, a_r,
+            mix_o, dz_o, part, dact_o, gstep_o, da_o, dskip_o, dbias_o,
+            lam_s, next_s, pb_s, pc_s, dt_s, u_s, dy_s, s1_s, s2_s, turned_s, held, sems,
+        ) = refs
+        place = blocks - 1 - pl.program_id(0)
+
         @pl.when(pl.program_id(0) == 0)
         def _():
+            fetch_blocks(mix_groups, held, sems, s_ref[0])
             lam_s[...] = jnp.zeros_like(lam_s)
             next_s[...] = end_r[...]
             da_o[...] = jnp.zeros_like(da_o)
@@ -451,7 +591,13 @@
                 ref[...] = jnp.zeros_like(ref)
             turned_s[...] = jnp.zeros_like(turned_s)
 
-        d_gated = mm_t(mix_r[...], wout[...])
+        @pl.when(pl.program_id(0) % per == 0)
+        def _():
+            wait_block(held, sems, place // per)
+
+        mix = held[place // per, pl.ds(pl.multiple_of(place % per * TIME_BLOCK, TIME_BLOCK), TIME_BLOCK)]
+        mix_o[...] = mix
+        d_gated = mm_t(mix, wout[...])
         z = z_r[...]
         s = sigmoid(z)
         dz_o[...] = (d_gated * mixed_r[...] * (s * (1.0 + z * (1.0 - s)))).astype(bf16)
@@ -521,11 +667,11 @@
         blocks,
         flip,
         [
-            (d_mix, (TIME_BLOCK, D), rel),
+            *[(part, None, None) for group in d_mix for part in group],
             (weight_out, (wid, D), None),
             (sel, (TIME_BLOCK, LANES), here),
             (act, row, here),
-            (proj_z, row, rel),
+            (proj_z, row, here),
             (lin, row, here),
             (mixed, row, here),
             (kept, (TIME_BLOCK, NS, wid), here),
@@ -535,6 +681,7 @@
             (a2, (NS, wid), None),
         ],
         [
+            ((length, D), bf16, (TIME_BLOCK, D), here),
             ((length, wid), bf16, row, rel),
             ((length, LANES), bf16, (TIME_BLOCK, LANES), here),
             ((length, wid), f32, row, here),
@@ -546,7 +693,11 @@
         [pltpu.VMEM((NS, wid), f32)] * 2
         + [pltpu.VMEM((TIME_BLOCK, NS, LANES), f32)] * 2
         + [pltpu.VMEM(row, f32)] * 5
-        + [pltpu.VMEM((LANES, TIME_BLOCK), f32)],
+        + [pltpu.VMEM((LANES, TIME_BLOCK), f32)]
+        + [
+            pltpu.VMEM((lax.axis_size("wide"), length // lax.axis_size("wide"), D), bf16),
+            pltpu.SemaphoreType.DMA((lax.axis_size("wide"),)),
+        ],
         length * wid * (20 * NS + 2 * D + 2 * LANES),
         length * NS * wid,
     )
@@ -554,17 +705,20 @@
 
 def tail(
     flip, d_sel, d_act, conv, proj, d_z, normed, act, weight_x, weight_z, weight_sel, taps,
-    grad_step, grad_flat, chans,
+    grad_step, grad_flat, grad_z, grad_out, beyond, chans,
 ):
     length, wid = act.shape
-    blocks = lax.axis_size("wide")
+    blocks, count = lax.axis_size("wide"), lax.axis_size("narrow")
     rows = length // blocks
+    group, c_rows = D // (blocks * count), chans // count
 
     def kernel(
         s_ref, sel_r, dact_r, conv_r, proj_r, dz_r, n_r, act_r, wx, wz, wsel, taps_r, gstep_r, flat_r,
-        part, *refs,
+        gz_r, gout_r, *refs,
     ):
-        gx_o, pack_o, ext, gx, gsel, flat = refs
+        (parts, packs), refs = taken(refs, [blocks, count])
+        gx_o, ext, gx, gsel, flat, held, stage, sems = refs
+        i = pl.program_id(0)
 
         @pl.when(pl.program_id(0) == 0)
         def _():
@@ -587,29 +741,45 @@
             flat[k : k + 1, :] += jnp.sum(moved * x, axis=0, keepdims=True)
         ext[rows:, :] = d_conv[:8, :]
         d_x = d_x.astype(bf16)
-        part[...] = (mm_t(d_x, wx[...]) + mm_t(dz_r[...], wz[...])).astype(bf16)
+        value = (mm_t(d_x, wx[...]) + mm_t(dz_r[...], wz[...])).astype(bf16)
+        send_rows(value, stage, sems, parts, i, blocks, (blocks - 1 - i) ^ s_ref[0], 0)
         gx[...] += t_mm(n_r[...], d_x)
         gsel[...] += t_mm(act_r[...], low)
 
         @pl.when(pl.program_id(0) == blocks - 1)
         def _():
-            gx_o[...] = gx[:, :chans].astype(bf16)
+            for k in range(blocks * count):
+                x = gx[k * group : (k + 1) * group, :chans]
+                gx_o[k] = jnp.concatenate([x, gz_r[k].astype(f32)], axis=1).astype(bf16)
             tall = jnp.concatenate(
                 [jnp.zeros((DT_RANK, wid), f32), flat[...], jnp.zeros((LANES - DT_RANK - FLAT, wid), f32)], axis=0
             )
             lane = lax.broadcasted_iota(jnp.int32, (wid, LANES), 1)
             left = jnp.where(lane < DT_RANK, gstep_r[...], tall.T)
-            pack = jnp.concatenate([left, gsel[...]], axis=1).astype(bf16)
-            pack_o[...] = pack[:chans]
+            held[:, :LANES] = left
+            held[:, LANES:] = gsel[...]
+            for k, out in enumerate(packs):
+                if c_rows % 8 == 0:
+                    at = pl.multiple_of(s_ref[1 + k] * c_rows, 8)
+                    out[:, :D] = gout_r[pl.ds(at, c_rows), :].astype(bf16)
+                    out[:, D:] = held[pl.ds(at, c_rows), :].astype(bf16)
+                    continue
+                for p in range(count):
+
+                    @pl.when(s_ref[1 + k] == p)
+                    def _(out=out, at=p * c_rows):
+                        out[:, :D] = gout_r[at : at + c_rows, :].astype(bf16)
+                        out[:, D:] = held[at : at + c_rows, :].astype(bf16)
 
     here = lambda i, s: blocks - 1 - i
     rel = lambda i, s: (blocks - 1 - i) ^ s
     row = (rows, wid)
-    pack = (chans, 2 * LANES)
+    pack = (c_rows, D + 2 * LANES)
+    sent = (blocks * count, group, 2 * chans)
     return call(
         kernel,
         blocks,
-        flip,
+        jnp.concatenate([flip, beyond]),
         [
             (d_sel, (rows, LANES), here),
             (d_act, row, here),
@@ -624,19 +794,25 @@
             (taps, (CONV, wid), None),
             (grad_step, (wid, LANES), None),
             (grad_flat, (FLAT, wid), None),
-        ],
-        [((length, D), bf16, (rows, D), rel), ((D, chans), bf16, (D, chans), None), (pack, bf16, pack, None)],
+            (grad_z, grad_z.shape, None),
+            (grad_out, (wid, D), None),
+        ],
+        [*[((rows, D), bf16, None, None)] * blocks, *[(pack, bf16, pack, None)] * count, (sent, bf16, sent, None)],
         [
             pltpu.VMEM((rows + 8, wid), f32),
             pltpu.VMEM((D, wid), f32),
             pltpu.VMEM((wid, LANES), f32),
             pltpu.VMEM((FLAT, wid), f32),
+            pltpu.VMEM((wid, 2 * LANES), f32),
+            pltpu.VMEM((2, rows, D), bf16),
+            pltpu.SemaphoreType.DMA((2,)),
         ],
         2 * length * wid * (3 * D + 2 * LANES),
     )
 
 
-def row_grad(flip, a, b, cols):
+def row_grad(flip, a, b, cols, group, along):
+    narrow = lax.axis_size("narrow")
     length, total = a.shape
     n = b.shape[1]
     blocks = lax.axis_size("wide")
@@ -651,7 +827,9 @@
 
         @pl.when(pl.program_id(0) == blocks - 1)
         def _():
-            out[...] = acc[:, :cols].astype(bf16)
+            for k in range(total // group):
+                at = k % narrow * blocks + k // narrow if along else k
+                out[at] = acc[k * group : (k + 1) * group, :cols].astype(bf16)
 
     here = lambda i, s: i
     return call(
@@ -659,10 +837,29 @@
         blocks,
         flip,
         [(a, (rows, total), here), (b, (rows, n), here)],
-        [((total, cols), bf16, (total, cols), None)],
+        [((total // group, group, cols), bf16, (total // group, group, cols), None)],
         [pltpu.VMEM((total, n), f32)],
         2 * length * total * n,
     )[0]
+
+
+def joined(got):
+    wide, narrow, rows, cols = got.shape
+    half = cols // 2
+
+    def kernel(got_r, out):
+        parts = [sum(got_r[w, k].astype(f32) for k in range(narrow)) for w in range(wide)]
+        out[:, : wide * half] = jnp.concatenate([p[:, :half] for p in parts], axis=1)
+        out[:, wide * half :] = jnp.concatenate([p[:, half:] for p in parts], axis=1)
+
+    vmem = pl.BlockSpec(memory_space=pltpu.VMEM)
+    return pl.pallas_call(
+        kernel,
+        in_specs=[vmem],
+        out_specs=vmem,
+        out_shape=jax.ShapeDtypeStruct((rows, wide * cols), f32),
+        compiler_params=pltpu.CompilerParams(vmem_limit_bytes=VMEM),
+    )(got)
 
 
 def norm_backward(values, inverse, gain_vec, upstream):
@@ -705,16 +902,10 @@
     span = jnp.stack([flip, lengths[0]]).astype(jnp.int32)
 
     tokens_own = tokens[0].astype(f32)
-    tokens_all, _ = gather_wide(tokens[0])
 
     in_parts = in_weight.reshape(d_rows, 2, wide, chans).transpose(1, 2, 0, 3)
     gains = jnp.stack([mixer_gain, expert_gain], axis=1)
     gains = jnp.broadcast_to(gains[None], (wide, d_rows, 2))
-    x_full = gather_rows(jnp.concatenate([in_parts[0], gains], axis=2))
-    weight_x = pad_to(x_full[:, :chans], 1, wid)
-    gains = x_full[:, chans:].T.astype(f32)
-    gain_one, gain_two = gains[:1], gains[1:]
-    weight_z = pad_to(gather_rows(after(in_parts[1], x_full)), 1, wid)
     zero_col = jnp.zeros((c_rows, 1), bf16)
     channel_pack = jnp.concatenate(
         [
@@ -731,8 +922,24 @@
     )
     pack_cols = channel_pack.shape[1]
     wide_cols = -(-pack_cols // LANES) * LANES
-    channel_pack = jnp.concatenate([out_weight, pad_to(channel_pack, 1, wide_cols)], axis=1)
-    weight_out, packed = gather_channels(channel_pack, (D, wide_cols), wid)
+    channel_pack = pad_to(channel_pack, 1, wide_cols)
+    x_parts = jnp.concatenate([in_parts[0], gains], axis=2)
+    tokens_all, channel_pack = gather_wide(tokens[0], lambda block: turns(channel_pack))
+    x_full = gather_rows(after(x_parts, channel_pack))
+    x_full, tokens_all = lax.optimization_barrier((x_full, tokens_all))
+    weight_x = pad_to(x_full[:, :chans], 1, wid)
+    gains = x_full[:, chans:].T.astype(f32)
+    gain_one, gain_two = gains[:1], gains[1:]
+    up_parts = up_weight.reshape(EXPERTS, d_rows, wide, ff).transpose(2, 1, 0, 3)
+    up_parts = up_parts.reshape(wide, d_rows, both)
+    router_parts = jnp.broadcast_to(router_weight[None], (wide, d_rows, EXPERTS))
+    up_parts = jnp.concatenate([up_parts, router_parts, in_parts[1]], axis=2)
+    up_parts = lax.all_to_all(after(up_parts, x_full), "wide", 0, 0)
+    up_parts = up_parts.reshape(wide * d_rows, both + EXPERTS + chans)
+    route_cols = jnp.broadcast_to(routes[0].astype(bf16)[:, None], (rows, LANES))
+    cot_ext = jnp.concatenate([cotangent[0], route_cols], axis=1)
+    cot_all = lax.all_gather(after(cot_ext, tokens_all), "wide", axis=0, tiled=True)
+    (packed,) = gather_channels(channel_pack, (wide_cols,), wid)
     flat = packed[:, :FLAT].T.astype(f32)
     taps = flat[:CONV]
     conv_shift, step_shift, skip = (flat[CONV + k : CONV + k + 1] for k in range(3))
@@ -744,94 +951,136 @@
     normed, proj_x, conv_sum, conv_act, sel_part = front(
         flip[None], tokens_all, gain_one, weight_x, taps, conv_shift, weight_sel
     )
-    sel_part, weight_z = lax.optimization_barrier((sel_part, weight_z))
-    selected, proj_z = reduce_wide(sel_part, lambda low: mm(after(normed, low), weight_z))
+    out_pieces = turns(after(out_weight, x_full))
+    sel_part, up_parts, out_pieces = lax.optimization_barrier((sel_part, up_parts, out_pieces))
+    z_pieces = turns(up_parts[:, both + EXPERTS :])
+    up_parts = up_parts[:, : both + EXPERTS]
+    selected, z_pieces = reduce_wide(sel_part, lambda low: z_pieces)
+    weight_z = ordered_rows(z_pieces, d_rows, wid)
 
     up_cols = -(-(both + EXPERTS) // LANES) * LANES
-    up_parts = up_weight.reshape(EXPERTS, d_rows, wide, ff).transpose(2, 1, 0, 3)
-    up_parts = up_parts.reshape(wide, d_rows, both)
-    router_parts = jnp.broadcast_to(router_weight[None], (wide, d_rows, EXPERTS))
-    up_parts = jnp.concatenate([up_parts, router_parts], axis=2)
-    up_full = gather_rows(after(up_parts, selected))
-    down_full = lax.all_gather(after(down_weight, selected), "narrow")
-    down_full = down_full.transpose(1, 0, 2, 3).reshape(both, D)
-    route_cols = jnp.broadcast_to(routes[0].astype(bf16)[:, None], (rows, LANES))
-    cot_ext = jnp.concatenate([cotangent[0], route_cols], axis=1)
-    cot_all = lax.all_gather(after(cot_ext, selected), "wide", axis=0, tiled=True)
+    up_pieces = turns(after(up_parts, selected, out_pieces))
     valid_own = (w * rows + jnp.arange(rows))[:, None] < lengths[0]
     upstream = jnp.where(valid_own, cotangent[0].astype(f32), 0.0)
 
-    step_lin, kept, end, mixed, gated, mix_part = middle(
-        flip[None], selected, conv_act, proj_z, weight_step, step_shift, skip, a2, weight_out
-    )
-    up_full = pad_to(up_full, 1, up_cols)
-    hidden_one = tokens_own + scatter_wide(mix_part)
+    (weight_out,) = gather_channels(out_pieces, (D,), wid)
+    proj_z, step_lin, kept, end, mixed, gated, *mix_part = middle(
+        flip[None], selected, conv_act, normed, weight_z, weight_step, step_shift, skip, a2, weight_out
+    )
+    mix_part, up_pieces = lax.optimization_barrier((mix_part, up_pieces))
+    down_full = lax.all_gather(after(down_weight, cot_all, *up_pieces), "narrow")
+    up_full = ordered_rows(up_pieces, d_rows, up_cols)
+    down_full = down_full.transpose(1, 0, 2, 3).reshape(both, D)
+    mixer_sum, up_full, _ = scatter_wide(mix_part, up_full)
+    hidden_one = tokens_own + mixer_sum
     inverse_two = lax.rsqrt(jnp.mean(hidden_one * hidden_one, axis=-1, keepdims=True) + EPSILON)
-    normed_two, _ = gather_wide((hidden_one * inverse_two * gain_two).astype(bf16))
-    out_part, back_part, hidden_both, d_both, d_expert = experts(
-        span, normed_two, cot_all, up_full, down_full, ff
-    )
-
-    d_normed_two = scatter_wide(back_part)
+    own = (hidden_one * inverse_two * gain_two).astype(bf16)
+
+    def run(base, blocks, whole):
+        return experts(span, base, blocks, cot_all, up_full, down_full, ff, whole)
+
+    if relative():
+        mate, a, b = swap(own, 1), swap(own, 2), swap(own, 4)
+        back_own, out_own, whole = run(0, [own, mate], [])
+        a, b, whole = lax.optimization_barrier((a, b, whole))
+        far = swap(after(own, a, b), 6)
+        back_near, out_near, whole = run(2, [a, swap(a, 1), b, swap(b, 1)], whole)
+        far, back_near = lax.optimization_barrier((far, back_near))
+        pair = lambda parts: parts[0].astype(f32) + swap(parts[1], 1).astype(f32)
+        from_x = swap(pair(back_near[:2]).astype(bf16), 2)
+        from_y = swap(pair(back_near[2:]).astype(bf16), 4)
+        d_normed_two = pair(back_own)
+        back_far, out_far, whole = run(6, [far, swap(far, 1)], whole)
+        far_low = pair(back_far).astype(bf16)
+        from_far = swap(far_low, 6)
+        d_normed_two = d_normed_two + from_x.astype(f32) + from_y.astype(f32) + from_far.astype(f32)
+        out_parts, whole = lax.optimization_barrier(([*out_own, *out_near, *out_far], whole, far_low))[:2]
+        out_sums = [pair(out_parts[2 * q : 2 * q + 2]).astype(bf16) for q in range(4)]
+    else:
+        whole, parts, out_sums = [], [], []
+        blocks = [group[0] for group in gather_wide(own)[0]]
+        for k in range(0, wide, 2):
+            made, out, whole = run(k, blocks[k : k + 2], whole)
+            parts += made
+            out_sums += out
+        d_normed_two, _, _ = scatter_wide(parts)
+    normed_two, hidden_both, d_both, d_expert = whole
+
     grad_down = t_mm(hidden_both, d_expert).astype(bf16)
-    grad_down = split_narrow(grad_down.reshape(EXPERTS, narrow, f_rows, D), 1)
-    d_normed_two = after(d_normed_two, grad_down)
+    grad_down = grad_down.reshape(EXPERTS, narrow, f_rows, D).transpose(1, 0, 2, 3)
+    d_normed_two, grad_down, out_sums = lax.optimization_barrier((d_normed_two, grad_down, out_sums))
+    grad_down = lax.psum_scatter(grad_down, "narrow", scatter_dimension=0)
     d_hidden_one = upstream + norm_backward(hidden_one, inverse_two, gain_two, d_normed_two)
     d_low = d_hidden_one.astype(bf16)
     d_mix, grad_up = gather_wide(
         d_low,
-        lambda low: row_grad(flip[None], normed_two, after(d_both, low), both + EXPERTS),
-    )
-    grad_up = scatter_rows(after(grad_up, d_mix), d_rows)
-    grad_down = turned([after(p, d_mix) for p in grad_down])
-    expert_sum = lax.psum_scatter(after(out_part, d_mix), "wide", scatter_dimension=0, tiled=True)
-
-    d_z, d_sel_part, d_act, grad_step, d_a, grad_skip, grad_step_bias = back(
+        lambda low: row_grad(flip[None], normed_two, after(d_both, low), both + EXPERTS, d_rows, True),
+    )
+    d_mix, grad_down = lax.optimization_barrier((d_mix, grad_down))
+    grad_up = lax.psum_scatter(
+        after(grad_up, d_mix).reshape(narrow, wide, d_rows, both + EXPERTS), "narrow", scatter_dimension=0
+    )
+    if relative():
+        sent = after(out_sums, d_mix)
+        out_got = [swap(sent[q], 2 * q) for q in (1, 2, 3)]
+    else:
+        out_got = []
+
+    d_mix_all, d_z, d_sel_part, d_act, grad_step, d_a, grad_skip, grad_step_bias = back(
         flip[None], d_mix, weight_out, selected, conv_act, proj_z, step_lin, mixed, kept, end,
         weight_step, skip, a2,
     )
-    d_sel_part, grad_up, grad_down = lax.optimization_barrier((d_sel_part, grad_up, grad_down))
+
+    d_sel_part, out_got = lax.optimization_barrier((d_sel_part, out_got))
 
     def meanwhile(low):
-        grad_out = t_mm(after(gated, low), d_mix).astype(bf16)[:chans].reshape(narrow, c_rows, D)
-        return split_narrow(grad_out, 0), row_grad(flip[None], after(normed, low), d_z, chans)
+        grad_out = t_mm(after(gated, low), d_mix_all)
+        return grad_out, row_grad(flip[None], after(normed, low), d_z, chans, d_rows, False)
 
     d_sel, (grad_out, grad_z) = reduce_wide(d_sel_part, meanwhile)
-    grad_out = turned([after(p, d_sel) for p in grad_out])
+    z = lax.axis_index("narrow")
+    beyond = jnp.stack([(z + k) % narrow for k in range(narrow)]).astype(jnp.int32)
     grad_flat = jnp.concatenate(
         [jnp.zeros((CONV + 1, wid), f32), grad_step_bias, grad_skip, jnp.zeros((1, wid), f32), d_a * a_neg],
         axis=0,
     )
-    in_part, grad_x, grad_pack = tail(
+    grad_up = lax.all_to_all(after(grad_up, d_sel), "wide", 0, 0)
+    made = tail(
         flip[None], d_sel, d_act, conv_sum, proj_x, d_z, normed, conv_act, weight_x, weight_z,
-        weight_sel, taps, grad_step, grad_flat, chans,
-    )
-    grad_in = scatter_rows(jnp.concatenate([grad_x, grad_z], axis=1), d_rows)
-    in_part, grad_out = lax.optimization_barrier((in_part, grad_out))
-    channel_grads = turned(split_narrow(grad_pack.reshape(narrow, c_rows, 2 * LANES), 0))
-    d_normed = scatter_wide(in_part)
-    d_normed, grad_in, channel_grads, grad_out = lax.optimization_barrier(
-        (d_normed, grad_in, channel_grads, grad_out)
-    )
+        weight_sel, taps, grad_step, grad_flat, grad_z, grad_out, beyond, chans,
+    )
+    in_part, channel_grads, grad_in = made[:wide], made[wide:-1], made[-1]
+    in_part, grad_up = lax.optimization_barrier((in_part, grad_up))
+    grad_in = scatter_rows(grad_in)
+
+    def beside(hop):
+        up, down = lax.optimization_barrier((grad_up, grad_down, hop))[:2]
+        up = up.astype(f32)
+        router = jnp.sum(up[:, :, both:], axis=0)
+        up = up[:, :, :both].reshape(wide, d_rows, EXPERTS, ff)
+        up = up.transpose(2, 1, 0, 3).reshape(EXPERTS, d_rows, FF)
+        gain = (
+            jnp.sum(up_weight.astype(f32) * up, axis=(0, 2))
+            + jnp.sum(router_weight.astype(f32) * router, axis=1)
+        ) / expert_gain.astype(f32)
+        if relative():
+            out = sum(p.astype(f32) for p in lax.optimization_barrier(([out_sums[0], *out_got], hop))[0])
+        else:
+            out, _, _ = scatter_wide(out_sums)
+        return up, router, gain, down.astype(f32), out, turned(channel_grads)
+
+    d_normed, made, _ = scatter_wide(in_part, beside)
+    channel_grads = made[-1]
+    made = made[:-1]
+    grad_up, grad_router, grad_gain_two, grad_down, expert_sum = made
+    d_normed, grad_in = lax.optimization_barrier((d_normed, grad_in))
     channel_grads = sum(p.astype(f32) for p in channel_grads)
-    grad_out = sum(p.astype(f32) for p in grad_out)
+    grad_out, channel_grads = channel_grads[:, :D], channel_grads[:, D:]
     inverse_one = lax.rsqrt(jnp.mean(tokens_own * tokens_own, axis=-1, keepdims=True) + EPSILON)
     token_grad = d_hidden_one + norm_backward(tokens_own, inverse_one, gain_one, d_normed)
-    output = (hidden_one + after(expert_sum, in_part).astype(f32)).astype(bf16)
-
-    grad_up, grad_down, _ = lax.optimization_barrier((grad_up, grad_down, in_part))
-    grad_up = summed_rows(grad_up)
-    grad_down = sum(p.astype(f32) for p in grad_down)
-    grad_router = jnp.sum(grad_up[:, :, both:], axis=0)
-    grad_up = grad_up[:, :, :both].reshape(wide, d_rows, EXPERTS, ff)
-    grad_up = grad_up.transpose(2, 1, 0, 3).reshape(EXPERTS, d_rows, FF)
-    grad_gain_two = (
-        jnp.sum(up_weight.astype(f32) * grad_up, axis=(0, 2))
-        + jnp.sum(router_weight.astype(f32) * grad_router, axis=1)
-    ) / expert_gain.astype(f32)
-
-    grad_in = summed_rows(grad_in).reshape(wide, d_rows, 2, chans)
-    grad_in = grad_in.transpose(1, 2, 0, 3).reshape(d_rows, 2 * DI)
+    output = (hidden_one + expert_sum).astype(bf16)
+
+    grad_in = joined(grad_in)
     grad_gain_one = jnp.sum(in_weight.astype(f32) * grad_in, axis=1) / mixer_gain.astype(f32)
     flat_grads = channel_grads[:, DT_RANK : DT_RANK + FLAT].T
     return (

time: 622 us -> 557 us (0.90)
  local copies, waits for them, and re-layouts: 129 us -> 47.5 us
  Pallas kernels: 149 us -> 212 us
  waiting for transfers between devices: 176 us -> 127 us
  other arithmetic: 35.9 us -> 42.4 us
    ppermute x67 -> x69, waiting for transfers between devices: 148 us -> 65.8 us  [swap(): return lax.ppermute(x, 'wide', [(i, i ^ k) for i in range(n)])]
    unnamed x176 -> x173, local copies, waits for them, and re-layouts: 65.9 us -> 13.2 us
    pallas_call x7 -> x9, Pallas kernels: 147 us -> 192 us  [call(): pl.pallas_call(kernel, grid_spec=pltpu.PrefetchScalarGridSpec(num_scalar_...]
    pallas_call x0 -> x3, Pallas kernels: none -> 14.7 us  [the longest x2 12.1 us: ordered_rows(): pl.pallas_call(kernel, in_specs=[pl.BlockSpec(memory_space=pltpu.SMEM)] +...]
    all_gather x2, waiting for transfers between devices: 0.01 us -> 14.4 us  [the longest x1 14.4 us: local(): lax.all_gather(after(down_weight, cot_all, *up_pieces), 'narrow')]
    all_to_all x5 -> x2, starting transfers between devices: 21 us -> 7.46 us  [exchange(): return lax.all_to_all(x, ('wide', 'narrow'), 0, 0)]
    convert_element_type x0 -> x13, other arithmetic: none -> 13.1 us  [the longest x4 3.89 us: local(): out_sums = [pair(out_parts[2 * q:2 * q + 2]).astype(bf16) for q in range(4)]]
    slice x6, local copies, waits for them, and re-layouts: 12.6 us -> 3.63 us  [the longest x1 1.06 us: beside(): up = up[:, :, :both].reshape(wide, d_rows, EXPERTS, ff)]
  transfers between devices with their start and end apart: 87 -> 92, of which waited for: 33 -> 31; matrix products, arithmetic and copies ran while one was open for 19% -> 16% of each run, Pallas kernels for 20% -> 38%
where the time goes in v3:
time: 557 us; the launch traced here: 548 us
  Pallas kernels  212 us (38%)
  waiting for transfers between devices  127 us (23%)
  starting transfers between devices  91.3 us (16%)
  local copies, waits for them, and re-layouts  47.5 us (9%)
  other arithmetic  42.4 us (8%)
  between operations  16 us (3%)
  matrix products  12.5 us (2%)
    pallas_call x9, Pallas kernels, call(): pl.pallas_call(kernel, grid_spec=pltpu.PrefetchScalarGridSpec(num_scalar_...  192 us
    ppermute x69, waiting for transfers between devices, swap(): return lax.ppermute(x, 'wide', [(i, i ^ k) for i in range(n)])  65.8 us
    ppermute x69, starting transfers between devices, swap(): return lax.ppermute(x, 'wide', [(i, i ^ k) for i in range(n)])  51.6 us
    ppermute x15, waiting for transfers between devices, turn(): return lax.ppermute(x, 'narrow', [(i, (i + k) % n) for i in range(n)])  33.5 us
    ppermute x15, starting transfers between devices, turn(): return lax.ppermute(x, 'narrow', [(i, (i + k) % n) for i in range(n)])  24.8 us
    all_gather x1, waiting for transfers between devices, local(): lax.all_gather(after(down_weight, cot_all, *up_pieces), 'narrow')  14.4 us
    unnamed x173, local copies, waits for them, and re-layouts  13.2 us
    dot_general x2, matrix products, t_mm(): lax.dot_general(a, b, (((0,), (0,)), ((), ())), preferred_element_type=f32)  12.5 us
  transfers between devices with their start and end apart: 92, of which 31 were waited for; matrix products, arithmetic and copies ran while one was open for 16% of the time, Pallas kernels for 38%

profile of v3, /device:TPU:0, one launch (start us, length us, event | category | flops | bytes accessed | tf_op | source)
XLA Modules:
  0.0 548.4 jit_solution(16758812154444902342)
XLA Ops:
  7.2 3.0 collective-permute-start.1
  17.3 3.7 collective-permute-start.4
  27.8 3.5 all-to-all-start
  37.2 11.8 %collective-permute-done.9.refs_7_ = bf16[128,1152]{1,0:T(8,128)(2,1)} collective-permute-done((bf16[128,1152]{1,0:T(8,128)(2,1)S(1)}, bf16[128,1152]{1,0:T(8,128)(2,1)}, u32[]{:S(2)}, u32[]{:S(2)}) %collective-permute-start.9) | collective-permute-done | bytes 294944 | tf_op jit(solution)/shard_map/ppermute | solution.py:33
  50.7 4.4 all-to-all-done
  63.1 3.2 collective-permute-start.14
  69.0 3.5 all-to-all-start.1
  74.2 11.7 %shard_map.298 = (bf16[2048,1152]{1,0:T(8,128)(2,1)}, f32[2048,384]{1,0:T(8,128)}, f32[2048,384]{1,0:T(8,128)}, bf16[2048,384]{1,0:T(8,128)(2,1)}, bf16[2048,128]{1,0:T(8,128)(2,1)}) custom-call(s32[1]{0:T(128)} %bitcast.1.s_ref, bf16[256,1152]{1,0:T(8,128)(2,1)} %bitcast.95, bf16[256,1152]{1,0:T(8,128)(2,1)} %collective-permute-done.5.refs_1_, ...), custom_call_target="tpu_custom_call" | custom-call | flops 31457280 | bytes 294080 | tf_op jit(solution)/shard_map/pallas_call | solution.py:242
  88.3 4.4 collective-permute-start.21
  98.9 14.0 %collective-permute-done.20.refs_2_ = bf16[288,288]{1,0:T(8,128)(2,1)S(1)} collective-permute-done((bf16[288,288]{1,0:T(8,128)(2,1)S(1)}, bf16[288,288]{1,0:T(8,128)(2,1)S(1)}, u32[]{:S(2)}, u32[]{:S(2)}) %collective-permute-start.20) | collective-permute-done | bytes 165920 | tf_op jit(solution)/shard_map/ppermute | solution.py:38
  123.5 3.1 shard_map.300.wout.refs_10_
  126.6 4.5 shard_map.299.wz
  131.1 32.9 %shard_map.301 = (f32[2048,384]{1,0:T(8,128)}, f32[2048,384]{1,0:T(8,128)}, f32[2048,16,384]{2,1,0:T(8,128)}, f32[16,384]{1,0:T(8,128)}, f32[2048,384]{1,0:T(8,1...) custom-call(s32[1]{0:T(128)} %bitcast.1.s_ref, ...), custom_call_target="tpu_custom_call" | custom-call | flops 61341696 | bytes 1168688 | tf_op jit(solution)/shard_map/pallas_call | solution.py:242
  172.1 5.9 %collective-permute-done.31 = bf16[128,1152]{1,0:T(8,128)(2,1)} collective-permute-done((bf16[128,1152]{1,0:T(8,128)(2,1)S(1)}, bf16[128,1152]{1,0:T(8,128)(2,1)}, u32[]{:S(2)}, u32[]{:S(2)}) %collective-permute-start.31) | collective-permute-done | bytes 294944 | tf_op jit(solution)/shard_map/ppermute | solution.py:33
  187.6 7.6 %shard_map.302.refs_3_.refs_5_ = bf16[1152,896]{1,0:T(8,128)(2,1)} custom-call(s32[4]{0:T(128)} %pad_add_fusion.1.order_ref, bf16[288,770]{1,0:T(8,128)(2,1)} %copy-done.9, bf16[288,770]{1,0:T(8,128)(2,1)} %copy-done.46, bf16[288,770]{1,0:T(8,128)(2,1)} %copy-done.45, bf16[288,770]{1,0:T(8,128)(2,1)} %copy-done.44), custom_call_target="tpu_custom_call" | custom-call | tf_op jit(solution)/shard_map/pallas_call | solution.py:140
  203.7 14.4 %all-gather.6.cloned.1.call-done = bf16[8,96,1152]{2,1,0:T(8,128)(2,1)} async-done(((bf16[2,96,1152]{2,1,0:T(8,128)(2,1)}), bf16[8,96,1152]{2,1,0:T(8,128)(2,1)}) %all-gather.6.cloned.1.call-update) | async-done | bytes 1769488 | tf_op jit(solution)/shard_map/all_gather | solution.py:971
  221.0 13.1 %shard_map.303 = (bf16[256,1152]{1,0:T(8,128)(2,1)}, bf16[256,1152]{1,0:T(8,128)(2,1)}, bf16[256,1152]{1,0:T(8,128)(2,1)}, bf16[256,1152]{1,0:T(8,128)(2,1)}, bf...) custom-call(s32[2]{0:T(128)} %pad_add_fusion.2.s_ref, ...), custom_call_target="tpu_custom_call" | custom-call | flops 61341696 | bytes 451072 | tf_op jit(solution)/shard_map/pallas_call | solution.py:242
  237.2 21.6 %shard_map.304 = (bf16[256,1152]{1,0:T(8,128)(2,1)}, bf16[256,1152]{1,0:T(8,128)(2,1)}, bf16[256,1152]{1,0:T(8,128)(2,1)}, bf16[256,1152]{1,0:T(8,128)(2,1)}, bf...) custom-call(s32[2]{0:T(128)} %pad_add_fusion.2.s_ref, ...), custom_call_target="tpu_custom_call", output_to_operand_aliasing={{8}: (8, {}), {9}: (9, {}), {10}: (10, {}), {11}: (11, {})} | custom-call | flops 122683392 | bytes 760320 | tf_op jit(solution)/shard_map/pallas_call | solution.py:242
  261.8 13.1 %shard_map.305 = (bf16[256,1152]{1,0:T(8,128)(2,1)}, bf16[256,1152]{1,0:T(8,128)(2,1)}, bf16[256,1152]{1,0:T(8,128)(2,1)}, bf16[256,1152]{1,0:T(8,128)(2,1)}, bf...) custom-call(s32[2]{0:T(128)} %pad_add_fusion.2.s_ref, ...), custom_call_target="tpu_custom_call", output_to_operand_aliasing={{4}: (6, {}), {5}: (7, {}), {6}: (8, {}), {7}: (9, {})} | custom-call | flops 61341696 | bytes 705024 | tf_op jit(solution)/shard_map/pallas_call | solution.py:242
  282.8 6.3 %convolution_convert_fusion = bf16[768,1152]{1,0:T(8,128)(2,1)S(1)} fusion(bf16[2048,768]{1,0:T(8,128)(2,1)} %get-tuple-element.332, bf16[2048,1152]{1,0:T(8,128)(2,1)S(1)} %copy-done), kind=kOutput, calls=%fused_computation | convolution fusion | flops 3624763392 | bytes 9633792 | tf_op jit(solution)/shard_map/dot_general | solution.py:220
  295.6 13.9 %collective-permute-done.49 = bf16[256,1152]{1,0:T(8,128)(2,1)S(1)} collective-permute-done((bf16[256,1152]{1,0:T(8,128)(2,1)S(1)}, bf16[256,1152]{1,0:T(8,128)(2,1)S(1)}, u32[]{:S(2)}, u32[]{:S(2)}) %collective-permute-start.49) | collective-permute-done | bytes 589856 | tf_op jit(solution)/shard_map/ppermute | solution.py:33
  314.5 11.5 %shard_map.306 = bf16[32,36,770]{2,1,0:T(8,128)(2,1)} custom-call(s32[1]{0:T(128)} %bitcast.1.s_ref, bf16[2048,1152]{1,0:T(8,128)(2,1)} %get-tuple-element.343.a_r, bf16[2048,896]{1,0:T(8,128)(2,1)} %get-tuple-element.345.b_r), custom_call_target="tpu_custom_call" | custom-call | flops 66060288 | bytes 158792 | tf_op jit(solution)/shard_map/pallas_call | solution.py:242
  331.3 4.6 collective-permute-done.60.refs_7_
  340.0 6.7 %reduce-scatter.3.cloned.1.call-done = bf16[1,2,96,1152]{3,2,1,0:T(8,128)(2,1)} async-done(((bf16[4,2,96,1152]{3,2,1,0:T(8,128)(2,1)}), bf16[1,2,96,1152]{3,2,1,0:T(8,128)(2,1)}) %reduce-scatter.3.cloned.1.call-update) | async-done | bytes 442384 | tf_op jit(solution)/shard_map/reduce_scatter | solution.py:1012
  350.3 57.2 %shard_map.307 = (bf16[2048,1152]{1,0:T(8,128)(2,1)}, bf16[2048,384]{1,0:T(8,128)(2,1)}, bf16[2048,128]{1,0:T(8,128)(2,1)}, f32[2048,384]{1,0:T(8,128)}, f32[384...) custom-call(s32[1]{0:T(128)} %bitcast.1.s_ref, ...), custom_call_target="tpu_custom_call" | custom-call | flops 35389440 | bytes 1215688 | tf_op jit(solution)/shard_map/pallas_call | solution.py:242
  416.2 6.3 %fusion.20.gout_r = f32[384,1152]{1,0:T(8,128)} fusion(bf16[2048,384]{1,0:T(8,128)(2,1)} %get-tuple-element.374, bf16[2048,1152]{1,0:T(8,128)(2,1)} %get-tuple-element.375), kind=kOutput, calls=%fused_computation.100 | convolution fusion | flops 1811939328 | bytes 8060928 | tf_op jit(solution)/shard_map/dot_general | solution.py:220
  422.5 8.4 %shard_map.308.gz_r = bf16[32,36,288]{2,1,0:T(8,128)(2,1)} custom-call(s32[1]{0:T(128)} %bitcast.1.s_ref, bf16[2048,1152]{1,0:T(8,128)(2,1)} %get-tuple-element.376.n_r.a_r, bf16[2048,384]{1,0:T(8,128)(2,1)} %get-tuple-element.377.b_r.dz_r), custom_call_target="tpu_custom_call" | custom-call | flops 28311552 | bytes 108672 | tf_op jit(solution)/shard_map/pallas_call | solution.py:242
  435.5 3.5 all-to-all-start.2
  440.9 22.8 %shard_map.309 = (bf16[256,1152]{1,0:T(8,128)(2,1)}, bf16[256,1152]{1,0:T(8,128)(2,1)}, bf16[256,1152]{1,0:T(8,128)(2,1)}, bf16[256,1152]{1,0:T(8,128)(2,1)}, bf...) custom-call(s32[5]{0:T(128)} %concatenate.42.s_ref, ...), custom_call_target="tpu_custom_call" | custom-call | flops 91226112 | bytes 456608 | tf_op jit(solution)/shard_map/pallas_call | solution.py:242
  465.1 4.0 all-to-all-start.3
  480.7 11.2 %collective-permute-done.74 = bf16[128,1152]{1,0:T(8,128)(2,1)S(1)} collective-permute-done((bf16[128,1152]{1,0:T(8,128)(2,1)S(1)}, bf16[128,1152]{1,0:T(8,128)(2,1)S(1)}, u32[]{:S(2)}, u32[]{:S(2)}) %collective-permute-start.74) | collective-permute-done | bytes 294944 | tf_op jit(solution)/shard_map/ppermute | solution.py:33
  505.8 15.6 %collective-permute-done.79 = bf16[72,1408]{1,0:T(8,128)(2,1)} collective-permute-done((bf16[72,1408]{1,0:T(8,128)(2,1)}, bf16[72,1408]{1,0:T(8,128)(2,1)}, u32[]{:S(2)}, u32[]{:S(2)}) %collective-permute-start.79) | collective-permute-done | bytes 202784 | tf_op jit(solution)/shard_map/ppermute | solution.py:38
  (463 shorter events, 180.8 us)
Async XLA Ops:
  7.2 19.5 %collective-permute-start.1 = (bf16[256,1152]{1,0:T(8,128)(2,1)}, bf16[256,1152]{1,0:T(8,128)(2,1)}, u32[]{:S(2)}, u32[]{:S(2)}) collective-permute-start(bf16[256,1152]{1,0:T(8,128)(2,1)} %bitcast.93), channel_id=1, source_target_pairs={{0,16},{4,20},{8,24},{12,28},{16,0},{20,4},{24,8},{28,12},{1,17},{... | collective-permute-start | bytes 1769480 | tf_op jit(solution)/shard_map/ppermute | solution.py:33
  27.8 27.2 %all-to-all-start = ((bf16[32,36,290]{2,1,0:T(8,128)(2,1)}), bf16[32,36,290]{2,1,0:T(8,128)(2,1)S(1)}, u32[]{:S(2)}, u32[]{:S(2)}) async-start(bf16[32,36,290]{2,1,0:T(8,128)(2,1)} %bitcast.12), calls=%async_computation | async-start | bytes 1966080 | tf_op jit(solution)/shard_map/all_to_all | solution.py:191
  31.3 147.6 %all-gather.4.cloned.1.call-start = ((), (), s32[]{:S(2)}) async-start(), calls=%async_computation.6 | async-start | bytes 5898240 | tf_op jit(solution)/shard_map/all_gather | solution.py:941
  63.1 24.8 %collective-permute-start.14 = (bf16[72,1152]{1,0:T(8,128)(2,1)S(1)}, bf16[72,1152]{1,0:T(8,128)(2,1)}, u32[]{:S(2)}, u32[]{:S(2)}) collective-permute-start(bf16[72,1152]{1,0:T(8,128)(2,1)S(1)} %copy-done.62), channel_id=1, source_target_pairs={{0,3},{1,0},{2,1},{3,2},{4,7},{5,4},{6,5},{7,6},{8,11},{9,8},{10,9... | collective-permute-start | bytes 497672 | tf_op jit(solution)/shard_map/ppermute | solution.py:38
  66.3 21.7 %collective-permute-start.13 = (bf16[72,1152]{1,0:T(8,128)(2,1)S(1)}, bf16[72,1152]{1,0:T(8,128)(2,1)}, u32[]{:S(2)}, u32[]{:S(2)}) collective-permute-start(bf16[72,1152]{1,0:T(8,128)(2,1)S(1)} %copy-done.62), channel_id=1, source_target_pairs={{0,2},{1,3},{2,0},{3,1},{4,6},{5,7},{6,4},{7,5},{8,10},{9,11},{10,... | collective-permute-start | bytes 497672 | tf_op jit(solution)/shard_map/ppermute | solution.py:38
  67.7 20.3 %collective-permute-start.12 = (bf16[72,1152]{1,0:T(8,128)(2,1)S(1)}, bf16[72,1152]{1,0:T(8,128)(2,1)}, u32[]{:S(2)}, u32[]{:S(2)}) collective-permute-start(bf16[72,1152]{1,0:T(8,128)(2,1)S(1)} %copy-done.62), channel_id=1, source_target_pairs={{0,1},{1,2},{2,3},{3,0},{4,5},{5,6},{6,7},{7,4},{8,9},{9,10},{10,1... | collective-permute-start | bytes 497672 | tf_op jit(solution)/shard_map/ppermute | solution.py:38
  72.5 145.6 %all-gather.6.cloned.1.call-start = ((), (), s32[]{:S(2)}) async-start(), calls=%async_computation.9 | async-start | bytes 2211840 | tf_op jit(solution)/shard_map/all_gather | solution.py:971
  92.7 20.2 %collective-permute-start.18 = (bf16[1024,128]{1,0:T(8,128)(2,1)S(1)}, bf16[1024,128]{1,0:T(8,128)(2,1)S(1)}, u32[]{:S(2)}, u32[]{:S(2)}) collective-permute-start(bf16[1024,128]{1,0:T(8,128)(2,1)S(1)} %fusion.11), channel_id=1, source_target_pairs={{0,24},{4,28},{8,16},{12,20},{16,8},{20,12},{24,0},{28,4},{1,25},{... | collective-permute-start | bytes 786440 | tf_op jit(solution)/shard_map/ppermute | solution.py:33
  116.4 47.7 %collective-permute-start.25 = (bf16[288,770]{1,0:T(8,128)(2,1)S(1)}, bf16[288,770]{1,0:T(8,128)(2,1)S(1)}, u32[]{:S(2)}, u32[]{:S(2)}) collective-permute-start(bf16[288,770]{1,0:T(8,128)(2,1)S(1)} %slice.153.refs_0_), channel_id=1, source_target_pairs={{0,3},{1,0},{2,1},{3,2},{4,7},{5,4},{6,5},{7,6},{8,11},{9,8},{10,9... | collective-permute-start | bytes 1330568 | tf_op jit(solution)/shard_map/ppermute | solution.py:38
  117.3 46.9 %collective-permute-start.24 = (bf16[288,770]{1,0:T(8,128)(2,1)S(1)}, bf16[288,770]{1,0:T(8,128)(2,1)S(1)}, u32[]{:S(2)}, u32[]{:S(2)}) collective-permute-start(bf16[288,770]{1,0:T(8,128)(2,1)S(1)} %slice.153.refs_0_), channel_id=1, source_target_pairs={{0,2},{1,3},{2,0},{3,1},{4,6},{5,7},{6,4},{7,5},{8,10},{9,11},{10,... | collective-permute-start | bytes 1330568 | tf_op jit(solution)/shard_map/ppermute | solution.py:38
  119.0 45.2 %collective-permute-start.23 = (bf16[288,770]{1,0:T(8,128)(2,1)S(1)}, bf16[288,770]{1,0:T(8,128)(2,1)S(1)}, u32[]{:S(2)}, u32[]{:S(2)}) collective-permute-start(bf16[288,770]{1,0:T(8,128)(2,1)S(1)} %slice.153.refs_0_), channel_id=1, source_target_pairs={{0,1},{1,2},{2,3},{3,0},{4,5},{5,6},{6,7},{7,4},{8,9},{9,10},{10,1... | collective-permute-start | bytes 1330568 | tf_op jit(solution)/shard_map/ppermute | solution.py:38
  165.3 29.9 %collective-permute-start.26 = (bf16[256,1152]{1,0:T(8,128)(2,1)}, bf16[256,1152]{1,0:T(8,128)(2,1)S(1)}, u32[]{:S(2)}, u32[]{:S(2)}) collective-permute-start(bf16[256,1152]{1,0:T(8,128)(2,1)} %get-tuple-element.274), channel_id=1, source_target_pairs={{0,4},{4,0},{8,12},{12,8},{16,20},{20,16},{24,28},{28,24},{1,5},{5... | collective-permute-start | bytes 1769480 | tf_op jit(solution)/shard_map/ppermute | solution.py:33
  178.9 167.7 %reduce-scatter.3.cloned.1.call-start = ((), (), s32[]{:S(2)}) async-start(), calls=%async_computation.7 | async-start | bytes 2211840 | tf_op jit(solution)/shard_map/reduce_scatter | solution.py:1012
  201.4 19.6 %collective-permute-start.36 = (bf16[256,1152]{1,0:T(8,128)(2,1)S(1)}, bf16[256,1152]{1,0:T(8,128)(2,1)}, u32[]{:S(2)}, u32[]{:S(2)}) collective-permute-start(bf16[256,1152]{1,0:T(8,128)(2,1)S(1)} %multiply_convert_fusion.refs_0_), channel_id=1, source_target_pairs={{0,4},{4,0},{8,12},{12,8},{16,20},{20,16},{24,28},{28,24},{1,5},{5... | collective-permute-start | bytes 1769480 | tf_op jit(solution)/shard_map/ppermute | solution.py:33
  201.4 32.8 %collective-permute-start.39 = (bf16[256,1152]{1,0:T(8,128)(2,1)S(1)}, bf16[256,1152]{1,0:T(8,128)(2,1)S(1)}, u32[]{:S(2)}, u32[]{:S(2)}) collective-permute-start(bf16[256,1152]{1,0:T(8,128)(2,1)S(1)} %multiply_convert_fusion.refs_0_), channel_id=1, source_target_pairs={{0,16},{4,20},{8,24},{12,28},{16,0},{20,4},{24,8},{28,12},{1,17},{... | collective-permute-start | bytes 1769480 | tf_op jit(solution)/shard_map/ppermute | solution.py:33
  202.1 32.1 %collective-permute-start.38 = (bf16[256,1152]{1,0:T(8,128)(2,1)S(1)}, bf16[256,1152]{1,0:T(8,128)(2,1)}, u32[]{:S(2)}, u32[]{:S(2)}) collective-permute-start(bf16[256,1152]{1,0:T(8,128)(2,1)S(1)} %multiply_convert_fusion.refs_0_), channel_id=1, source_target_pairs={{0,8},{4,12},{8,0},{12,4},{16,24},{20,28},{24,16},{28,20},{1,9},{5... | collective-permute-start | bytes 1769480 | tf_op jit(solution)/shard_map/ppermute | solution.py:33
  234.8 24.1 %collective-permute-start.40 = (bf16[256,1152]{1,0:T(8,128)(2,1)}, bf16[256,1152]{1,0:T(8,128)(2,1)S(1)}, u32[]{:S(2)}, u32[]{:S(2)}) collective-permute-start(bf16[256,1152]{1,0:T(8,128)(2,1)} %copy-done.6), channel_id=1, source_target_pairs={{0,24},{4,28},{8,16},{12,20},{16,8},{20,12},{24,0},{28,4},{1,25},{... | collective-permute-start | bytes 1769480 | tf_op jit(solution)/shard_map/ppermute | solution.py:33
  259.6 36.0 %collective-permute-start.37 = (bf16[256,1152]{1,0:T(8,128)(2,1)}, bf16[256,1152]{1,0:T(8,128)(2,1)}, u32[]{:S(2)}, u32[]{:S(2)}) collective-permute-start(bf16[256,1152]{1,0:T(8,128)(2,1)} %get-tuple-element.293), channel_id=1, source_target_pairs={{0,4},{4,0},{8,12},{12,8},{16,20},{20,16},{24,28},{28,24},{1,5},{5... | collective-permute-start | bytes 1769480 | tf_op jit(solution)/shard_map/ppermute | solution.py:33
  276.7 18.9 %collective-permute-start.44 = (bf16[256,1152]{1,0:T(8,128)(2,1)S(1)}, bf16[256,1152]{1,0:T(8,128)(2,1)S(1)}, u32[]{:S(2)}, u32[]{:S(2)}) collective-permute-start(bf16[256,1152]{1,0:T(8,128)(2,1)S(1)} %add_convert_fusion.8), channel_id=1, source_target_pairs={{0,8},{4,12},{8,0},{12,4},{16,24},{20,28},{24,16},{28,20},{1,9},{5... | collective-permute-start | bytes 1769480 | tf_op jit(solution)/shard_map/ppermute | solution.py:33
  310.9 124.5 %reduce-scatter.5.cloned.1.call-start = ((), (), s32[]{:S(2)}) async-start(), calls=%async_computation.8 | async-start | bytes 2867200 | tf_op jit(solution)/shard_map/reduce_scatter | solution.py:1020
  314.5 22.3 %collective-permute-start.54 = (bf16[256,1152]{1,0:T(8,128)(2,1)}, bf16[256,1152]{1,0:T(8,128)(2,1)S(1)}, u32[]{:S(2)}, u32[]{:S(2)}) collective-permute-start(bf16[256,1152]{1,0:T(8,128)(2,1)} %get-tuple-element.349.refs_0_), channel_id=1, source_target_pairs={{0,4},{4,0},{8,12},{12,8},{16,20},{20,16},{24,28},{28,24},{1,5},{5... | collective-permute-start | bytes 1769480 | tf_op jit(solution)/shard_map/ppermute | solution.py:33
  346.7 60.8 %collective-permute-start.63 = (bf16[256,1152]{1,0:T(8,128)(2,1)}, bf16[256,1152]{1,0:T(8,128)(2,1)S(1)}, u32[]{:S(2)}, u32[]{:S(2)}) collective-permute-start(bf16[256,1152]{1,0:T(8,128)(2,1)} %add_convert_fusion.4), channel_id=1, source_target_pairs={{0,8},{4,12},{8,0},{12,4},{16,24},{20,28},{24,16},{28,20},{1,9},{5... | collective-permute-start | bytes 1769480 | tf_op jit(solution)/shard_map/ppermute | solution.py:33
  348.3 59.3 %collective-permute-start.64 = (bf16[256,1152]{1,0:T(8,128)(2,1)}, bf16[256,1152]{1,0:T(8,128)(2,1)S(1)}, u32[]{:S(2)}, u32[]{:S(2)}) collective-permute-start(bf16[256,1152]{1,0:T(8,128)(2,1)} %add_convert_fusion.3), channel_id=1, source_target_pairs={{0,16},{4,20},{8,24},{12,28},{16,0},{20,4},{24,8},{28,12},{1,17},{... | collective-permute-start | bytes 1769480 | tf_op jit(solution)/shard_map/ppermute | solution.py:33
  349.7 57.8 %collective-permute-start.65 = (bf16[256,1152]{1,0:T(8,128)(2,1)}, bf16[256,1152]{1,0:T(8,128)(2,1)S(1)}, u32[]{:S(2)}, u32[]{:S(2)}) collective-permute-start(bf16[256,1152]{1,0:T(8,128)(2,1)} %add_convert_fusion.2), channel_id=1, source_target_pairs={{0,24},{4,28},{8,16},{12,20},{16,8},{20,12},{24,0},{28,4},{1,25},{... | collective-permute-start | bytes 1769480 | tf_op jit(solution)/shard_map/ppermute | solution.py:33
  435.5 28.3 %all-to-all-start.2 = ((bf16[8,36,770]{2,1,0:T(8,128)(2,1)}), bf16[8,36,770]{2,1,0:T(8,128)(2,1)S(1)}, u32[]{:S(2)}, u32[]{:S(2)}) async-start(bf16[8,36,770]{2,1,0:T(8,128)(2,1)} %bitcast.114), calls=%async_computation.4 | async-start | bytes 1146880 | tf_op jit(solution)/shard_map/all_to_all | solution.py:1047
  465.1 67.8 %all-to-all-start.3 = ((bf16[32,36,576]{2,1,0:T(8,128)(2,1)}), bf16[32,36,576]{2,1,0:T(8,128)(2,1)}, u32[]{:S(2)}, u32[]{:S(2)}) async-start(bf16[32,36,576]{2,1,0:T(8,128)(2,1)} %get-tuple-element.429), calls=%async_computation.5 | async-start | bytes 3276800 | tf_op jit(solution)/shard_map/all_to_all | solution.py:191
  469.0 36.7 %collective-permute-start.78 = (bf16[72,1408]{1,0:T(8,128)(2,1)}, bf16[72,1408]{1,0:T(8,128)(2,1)}, u32[]{:S(2)}, u32[]{:S(2)}) collective-permute-start(bf16[72,1408]{1,0:T(8,128)(2,1)} %get-tuple-element.421), channel_id=1, source_target_pairs={{0,1},{1,2},{2,3},{3,0},{4,5},{5,6},{6,7},{7,4},{8,9},{9,10},{10,1... | collective-permute-start | bytes 608264 | tf_op jit(solution)/shard_map/ppermute | solution.py:38
  470.8 50.6 %collective-permute-start.79 = (bf16[72,1408]{1,0:T(8,128)(2,1)}, bf16[72,1408]{1,0:T(8,128)(2,1)}, u32[]{:S(2)}, u32[]{:S(2)}) collective-permute-start(bf16[72,1408]{1,0:T(8,128)(2,1)} %get-tuple-element.422), channel_id=1, source_target_pairs={{0,2},{1,3},{2,0},{3,1},{4,6},{5,7},{6,4},{7,5},{8,10},{9,11},{10,... | collective-permute-start | bytes 608264 | tf_op jit(solution)/shard_map/ppermute | solution.py:38
  473.2 49.7 %collective-permute-start.80 = (bf16[72,1408]{1,0:T(8,128)(2,1)}, bf16[72,1408]{1,0:T(8,128)(2,1)}, u32[]{:S(2)}, u32[]{:S(2)}) collective-permute-start(bf16[72,1408]{1,0:T(8,128)(2,1)} %get-tuple-element.423), channel_id=1, source_target_pairs={{0,3},{1,0},{2,1},{3,2},{4,7},{5,4},{6,5},{7,6},{8,11},{9,8},{10,9... | collective-permute-start | bytes 608264 | tf_op jit(solution)/shard_map/ppermute | solution.py:38
  495.6 28.8 %collective-permute-start.75 = (bf16[128,1152]{1,0:T(8,128)(2,1)}, bf16[128,1152]{1,0:T(8,128)(2,1)S(1)}, u32[]{:S(2)}, u32[]{:S(2)}) collective-permute-start(bf16[128,1152]{1,0:T(8,128)(2,1)} %fusion.8), channel_id=1, source_target_pairs={{0,8},{4,12},{8,0},{12,4},{16,24},{20,28},{24,16},{28,20},{1,9},{5... | collective-permute-start | bytes 884744 | tf_op jit(solution)/shard_map/ppermute | solution.py:33
  497.7 26.7 %collective-permute-start.77 = (bf16[128,1152]{1,0:T(8,128)(2,1)}, bf16[128,1152]{1,0:T(8,128)(2,1)}, u32[]{:S(2)}, u32[]{:S(2)}) collective-permute-start(bf16[128,1152]{1,0:T(8,128)(2,1)} %fusion.7), channel_id=1, source_target_pairs={{0,16},{4,20},{8,24},{12,28},{16,0},{20,4},{24,8},{28,12},{1,17},{... | collective-permute-start | bytes 884744 | tf_op jit(solution)/shard_map/ppermute | solution.py:33
  505.7 22.1 %collective-permute-start.81 = (bf16[256,1152]{1,0:T(8,128)(2,1)S(1)}, bf16[256,1152]{1,0:T(8,128)(2,1)S(1)}, u32[]{:S(2)}, u32[]{:S(2)}) collective-permute-start(bf16[256,1152]{1,0:T(8,128)(2,1)S(1)} %copy-done.77), channel_id=1, source_target_pairs={{0,4},{4,0},{8,12},{12,8},{16,20},{20,16},{24,28},{28,24},{1,5},{5... | collective-permute-start | bytes 1769480 | tf_op jit(solution)/shard_map/ppermute | solution.py:33
  (142 other events, 1192.9 us)
Sparse Core Ops, SparseCore 0:
  55.6 45.1 all-gather.3
  179.1 39.0 all-gather.5
  311.1 35.5 reduce-scatter.2
  349.0 46.0 reduce-scatter.4

commit v4 on v3

--- a/solution.py
+++ b/solution.py
@@ -62,11 +62,11 @@
     return out, made
 
 
-def scatter_wide(parts, beside=(), early=()):
+def scatter_wide(parts, beside=(), eager=False):
     if not relative():
         whole = jnp.concatenate(parts, axis=0)
         total = lax.psum_scatter(whole, "wide", scatter_dimension=0, tiled=True).astype(f32)
-        return total, beside(total) if callable(beside) else beside, early
+        return total, beside(total) if callable(beside) else beside
     half = parts[0].shape[0] // 2
 
     def summed(q):
@@ -74,15 +74,16 @@
 
     far = summed(3).astype(bf16)
     r0, r1 = swap(far[:half], 2), swap(far[half:], 4)
-    r0, r1, early = lax.optimization_barrier((r0, r1, early))
     sx, sy = summed(1), summed(2)
     x0, y1 = swap(sx[:half].astype(bf16), 2), swap(sy[half:].astype(bf16), 4)
+    if eager:
+        r0, r1, x0, y1 = lax.optimization_barrier((r0, r1, x0, y1))
     x1 = swap((sx[half:] + r1.astype(f32)).astype(bf16), 2)
     y0 = swap((sy[:half] + r0.astype(f32)).astype(bf16), 4)
     x1, y0, beside = lax.optimization_barrier((x1, y0, beside(r0) if callable(beside) else beside))
     x = jnp.concatenate([x0, x1], axis=0).astype(f32)
     y = jnp.concatenate([y0, y1], axis=0).astype(f32)
-    return summed(0) + x + y, beside, early
+    return summed(0) + x + y, beside
 
 
 def reduce_wide(partial, meanwhile):
@@ -472,25 +473,30 @@
     )
 
 
-def experts(span, base, normed, cot, up, down, ff, whole):
-    rows = normed[0].shape[0]
-    length = rows * lax.axis_size("wide")
-    blocks = len(normed)
+def experts(span, normed, cot, up, down, ff):
+    rows = sum(p.shape[0] for p in normed[0])
+    blocks = lax.axis_size("wide")
+    length = rows * blocks
     cols = up.shape[1]
+    share = down.shape[2]
+    counts = [len(g) for g in normed]
 
     def kernel(s_ref, *refs):
-        (n_refs, (cot_r, up_r, down_r), _, backs, outs), refs = taken(
-            refs, [blocks, 3, len(whole), blocks, blocks]
-        )
-        n_o, hid_o, both_o, dex_o = refs
+        groups, refs = taken(refs, counts)
+        ((cot_r, up_r, down_r), backs, outs), refs = taken(refs, [3, blocks, blocks])
+        n_o, hid_o, both_o, dex_o, down_s, held, sems, stage, stage_sems, stage_2, stage_2_sems = refs
         i = pl.program_id(0)
-        for k, ref in enumerate(n_refs):
-
-            @pl.when(i == k)
-            def _(ref=ref):
-                n_o[...] = ref[...]
-
-        position = ((i + base) ^ s_ref[0]) * rows + lax.broadcasted_iota(jnp.int32, (rows, 1), 0)
+
+        @pl.when(i == 0)
+        def _():
+            fetch_blocks(groups, held, sems, 0)
+            for k in range(down.shape[0]):
+                for e in range(EXPERTS):
+                    down_s[e * ff + k * share : e * ff + (k + 1) * share, :] = down_r[k, e]
+
+        wait_block(held, sems, i)
+        n_o[...] = held[i]
+        position = (i ^ s_ref[0]) * rows + lax.broadcasted_iota(jnp.int32, (rows, 1), 0)
         cot_b = cot_r[...]
         second = cot_b[:, D : D + 1] > 0.5
         upstream = jnp.where(position < s_ref[1], cot_b[:, :D], jnp.zeros((), bf16))
@@ -509,15 +515,10 @@
             [jnp.where(second, 0.0, hid_f), jnp.where(second, hid_f, 0.0)], axis=1
         ).astype(bf16)
         hid_o[...] = both
-        value = (gate * mm(both, down_r[...])).astype(bf16)
-        for k, ref in enumerate(outs):
-
-            @pl.when(i == k)
-            def _(ref=ref, value=value):
-                ref[...] = value
-
+        value = (gate * mm(both, down_s[...])).astype(bf16)
+        send_rows(value, stage_2, stage_2_sems, outs, i, blocks, i, 0)
         dex_o[...] = (gate * upstream.astype(f32)).astype(bf16)
-        lowered = mm_t(upstream, down_r[...])
+        lowered = mm_t(upstream, down_s[...])
         d_hid = jnp.where(second, lowered[:, ff:], lowered[:, :ff])
         d_gate = jnp.sum(hid_f * d_hid, axis=-1, keepdims=True)
         d_pre = gate * d_hid * slope
@@ -530,37 +531,37 @@
         ).astype(bf16)
         both_o[...] = d_both
         value = mm_t(d_both, up_r[...]).astype(bf16)
-        for k, ref in enumerate(backs):
-
-            @pl.when(i == k)
-            def _(ref=ref):
-                ref[...] = value
-
-    here = lambda i, s: i + base
-    place = lambda i, s: (i + base) ^ s
-    first = 1 + blocks + 3
+        send_rows(value, stage, stage_sems, backs, i, blocks, i, 0)
+
+    here = lambda i, s: i
     made = call(
         kernel,
         blocks,
         span,
         [
-            *[(n, (rows, D), None) for n in normed],
-            (cot, (rows, D + LANES), place),
+            *[(part, None, None) for group in normed for part in group],
+            (cot, (rows, D + LANES), lambda i, s: i ^ s),
             (up, up.shape, None),
             (down, down.shape, None),
-            *[(x, None, None) for x in whole],
-        ],
-        [
-            *[((rows, D), bf16, (rows, D), None)] * (2 * blocks),
+        ],
+        [
+            *[((rows, D), bf16, None, None)] * (2 * blocks),
             ((length, D), bf16, (rows, D), here),
             ((length, EXPERTS * ff), bf16, (rows, EXPERTS * ff), here),
             ((length, cols), bf16, (rows, cols), here),
             ((length, D), bf16, (rows, D), here),
         ],
-        [],
-        4 * blocks * rows * D * (cols + EXPERTS * ff),
-        3 * blocks * rows * ff,
-        {first + k: 2 * blocks + k for k in range(len(whole))},
+        [
+            pltpu.VMEM((EXPERTS * ff, D), bf16),
+            pltpu.VMEM((blocks, rows, D), bf16),
+            pltpu.SemaphoreType.DMA((blocks,)),
+            pltpu.VMEM((2, rows, D), bf16),
+            pltpu.SemaphoreType.DMA((2,)),
+            pltpu.VMEM((2, rows, D), bf16),
+            pltpu.SemaphoreType.DMA((2,)),
+        ],
+        4 * length * D * (cols + EXPERTS * ff),
+        3 * length * ff,
     )
     return made[:blocks], made[blocks : 2 * blocks], made[2 * blocks :]
 
@@ -970,45 +971,25 @@
     mix_part, up_pieces = lax.optimization_barrier((mix_part, up_pieces))
     down_full = lax.all_gather(after(down_weight, cot_all, *up_pieces), "narrow")
     up_full = ordered_rows(up_pieces, d_rows, up_cols)
-    down_full = down_full.transpose(1, 0, 2, 3).reshape(both, D)
-    mixer_sum, up_full, _ = scatter_wide(mix_part, up_full)
+    mixer_sum, up_full = scatter_wide(mix_part, up_full, True)
     hidden_one = tokens_own + mixer_sum
     inverse_two = lax.rsqrt(jnp.mean(hidden_one * hidden_one, axis=-1, keepdims=True) + EPSILON)
     own = (hidden_one * inverse_two * gain_two).astype(bf16)
 
-    def run(base, blocks, whole):
-        return experts(span, base, blocks, cot_all, up_full, down_full, ff, whole)
-
-    if relative():
-        mate, a, b = swap(own, 1), swap(own, 2), swap(own, 4)
-        back_own, out_own, whole = run(0, [own, mate], [])
-        a, b, whole = lax.optimization_barrier((a, b, whole))
-        far = swap(after(own, a, b), 6)
-        back_near, out_near, whole = run(2, [a, swap(a, 1), b, swap(b, 1)], whole)
-        far, back_near = lax.optimization_barrier((far, back_near))
-        pair = lambda parts: parts[0].astype(f32) + swap(parts[1], 1).astype(f32)
-        from_x = swap(pair(back_near[:2]).astype(bf16), 2)
-        from_y = swap(pair(back_near[2:]).astype(bf16), 4)
-        d_normed_two = pair(back_own)
-        back_far, out_far, whole = run(6, [far, swap(far, 1)], whole)
-        far_low = pair(back_far).astype(bf16)
-        from_far = swap(far_low, 6)
-        d_normed_two = d_normed_two + from_x.astype(f32) + from_y.astype(f32) + from_far.astype(f32)
-        out_parts, whole = lax.optimization_barrier(([*out_own, *out_near, *out_far], whole, far_low))[:2]
-        out_sums = [pair(out_parts[2 * q : 2 * q + 2]).astype(bf16) for q in range(4)]
-    else:
-        whole, parts, out_sums = [], [], []
-        blocks = [group[0] for group in gather_wide(own)[0]]
-        for k in range(0, wide, 2):
-            made, out, whole = run(k, blocks[k : k + 2], whole)
-            parts += made
-            out_sums += out
-        d_normed_two, _, _ = scatter_wide(parts)
-    normed_two, hidden_both, d_both, d_expert = whole
-
-    grad_down = t_mm(hidden_both, d_expert).astype(bf16)
-    grad_down = grad_down.reshape(EXPERTS, narrow, f_rows, D).transpose(1, 0, 2, 3)
-    d_normed_two, grad_down, out_sums = lax.optimization_barrier((d_normed_two, grad_down, out_sums))
+    pieces, _ = gather_wide(own)
+    back_parts, out_parts, made = experts(span, pieces, cot_all, up_full, down_full, ff)
+    normed_two, hidden_both, d_both, d_expert = made
+
+    def beside(hop):
+        hidden, outs = lax.optimization_barrier((hidden_both, out_parts, hop))[:2]
+        grad = t_mm(hidden, d_expert).astype(bf16)
+        grad = grad.reshape(EXPERTS, narrow, f_rows, D).transpose(1, 0, 2, 3)
+        if not relative():
+            return grad, outs
+        pair = lambda q: outs[2 * q].astype(f32) + swap(outs[2 * q + 1], 1).astype(f32)
+        return grad, [pair(q).astype(bf16) for q in range(4)]
+
+    d_normed_two, (grad_down, out_sums) = scatter_wide(back_parts, beside, True)
     grad_down = lax.psum_scatter(grad_down, "narrow", scatter_dimension=0)
     d_hidden_one = upstream + norm_backward(hidden_one, inverse_two, gain_two, d_normed_two)
     d_low = d_hidden_one.astype(bf16)
@@ -1016,7 +997,6 @@
         d_low,
         lambda low: row_grad(flip[None], normed_two, after(d_both, low), both + EXPERTS, d_rows, True),
     )
-    d_mix, grad_down = lax.optimization_barrier((d_mix, grad_down))
     grad_up = lax.psum_scatter(
         after(grad_up, d_mix).reshape(narrow, wide, d_rows, both + EXPERTS), "narrow", scatter_dimension=0
     )
@@ -1066,10 +1046,10 @@
         if relative():
             out = sum(p.astype(f32) for p in lax.optimization_barrier(([out_sums[0], *out_got], hop))[0])
         else:
-            out, _, _ = scatter_wide(out_sums)
+            out, _ = scatter_wide(out_sums)
         return up, router, gain, down.astype(f32), out, turned(channel_grads)
 
-    d_normed, made, _ = scatter_wide(in_part, beside)
+    d_normed, made = scatter_wide(in_part, beside)
     channel_grads = made[-1]
     made = made[:-1]
     grad_up, grad_router, grad_gain_two, grad_down, expert_sum = made

time: 557 us -> 541 us (0.971)
  waiting for transfers between devices: 127 us -> 113 us
  Pallas kernels: 212 us -> 201 us
    ppermute x69 -> x74, waiting for transfers between devices: 65.8 us -> 87.2 us  [swap(): return lax.ppermute(x, 'wide', [(i, i ^ k) for i in range(n)])]
    ppermute x15, waiting for transfers between devices: 33.5 us -> 16.4 us  [turn(): return lax.ppermute(x, 'narrow', [(i, (i + k) % n) for i in range(n)])]
    all_gather x1, waiting for transfers between devices: 14.4 us -> 0.01 us  [local(): lax.all_gather(after(down_weight, cot_all, *up_pieces), 'narrow')]
    pallas_call x9 -> x7, Pallas kernels: 192 us -> 182 us  [call(): pl.pallas_call(kernel, grid_spec=pltpu.PrefetchScalarGridSpec(num_scalar_...]
    reduce_scatter x1, waiting for transfers between devices: 6.72 us -> 0.01 us  [local(): grad_down = lax.psum_scatter(grad_down, 'narrow', scatter_dimension=0)]
    unnamed x173 -> x203, local copies, waits for them, and re-layouts: 13.2 us -> 18.4 us
    ppermute x69 -> x74, starting transfers between devices: 51.6 us -> 53.4 us  [swap(): return lax.ppermute(x, 'wide', [(i, i ^ k) for i in range(n)])]
  transfers between devices with their start and end apart: 92 -> 97, of which waited for: 31 -> 32; matrix products, arithmetic and copies ran while one was open for 16% -> 16% of each run, Pallas kernels for 38% -> 30%
where the time goes in v4:
time: 541 us; the launch traced here: 533 us
  Pallas kernels  201 us (37%)
  waiting for transfers between devices  113 us (21%)
  starting transfers between devices  90.1 us (17%)
  local copies, waits for them, and re-layouts  52.1 us (10%)
  other arithmetic  46.4 us (9%)
  between operations  16.2 us (3%)
  matrix products  13.9 us (3%)
    pallas_call x7, Pallas kernels, call(): pl.pallas_call(kernel, grid_spec=pltpu.PrefetchScalarGridSpec(num_scalar_...  182 us
    ppermute x74, waiting for transfers between devices, swap(): return lax.ppermute(x, 'wide', [(i, i ^ k) for i in range(n)])  87.2 us
    ppermute x74, starting transfers between devices, swap(): return lax.ppermute(x, 'wide', [(i, i ^ k) for i in range(n)])  53.4 us
    ppermute x15, starting transfers between devices, turn(): return lax.ppermute(x, 'narrow', [(i, (i + k) % n) for i in range(n)])  20.9 us
    unnamed x203, local copies, waits for them, and re-layouts  18.4 us
    ppermute x15, waiting for transfers between devices, turn(): return lax.ppermute(x, 'narrow', [(i, (i + k) % n) for i in range(n)])  16.4 us
    dot_general x2, matrix products, t_mm(): lax.dot_general(a, b, (((0,), (0,)), ((), ())), preferred_element_type=f32)  13.9 us
    pallas_call x2, Pallas kernels, ordered_rows(): pl.pallas_call(kernel, in_specs=[pl.BlockSpec(memory_space=pltpu.SMEM)] +...  12.2 us
  transfers between devices with their start and end apart: 97, of which 32 were waited for; matrix products, arithmetic and copies ran while one was open for 16% of the time, Pallas kernels for 30%

profile of v4, /device:TPU:0, one launch (start us, length us, event | category | flops | bytes accessed | tf_op | source)
XLA Modules:
  0.0 533.4 jit_solution(14629312502505093156)
XLA Ops:
  27.3 4.0 all-to-all-start
  37.2 11.3 %collective-permute-done.8.refs_6_ = bf16[128,1152]{1,0:T(8,128)(2,1)} collective-permute-done((bf16[128,1152]{1,0:T(8,128)(2,1)S(1)}, bf16[128,1152]{1,0:T(8,128)(2,1)}, u32[]{:S(2)}, u32[]{:S(2)}) %collective-permute-start.8) | collective-permute-done | bytes 294944 | tf_op jit(solution)/shard_map/ppermute | solution.py:33
  50.2 4.9 all-to-all-done
  63.5 3.1 collective-permute-start.12
  71.0 3.5 all-to-all-start.1
  75.2 11.7 %shard_map.298 = (bf16[2048,1152]{1,0:T(8,128)(2,1)}, f32[2048,384]{1,0:T(8,128)}, f32[2048,384]{1,0:T(8,128)}, bf16[2048,384]{1,0:T(8,128)(2,1)}, bf16[2048,128]{1,0:T(8,128)(2,1)}) custom-call(s32[1]{0:T(128)} %bitcast.1.s_ref, bf16[256,1152]{1,0:T(8,128)(2,1)} %bitcast.89, bf16[256,1152]{1,0:T(8,128)(2,1)} %collective-permute-done.5.refs_1_, ...), custom_call_target="tpu_custom_call" | custom-call | flops 31457280 | bytes 294080 | tf_op jit(solution)/shard_map/pallas_call | solution.py:243
  86.9 4.8 all-to-all-done.1
  97.3 5.2 collective-permute-done.19.refs_1_
  102.5 9.1 %collective-permute-done.20.refs_2_ = bf16[288,288]{1,0:T(8,128)(2,1)S(1)} collective-permute-done((bf16[288,288]{1,0:T(8,128)(2,1)S(1)}, bf16[288,288]{1,0:T(8,128)(2,1)S(1)}, u32[]{:S(2)}, u32[]{:S(2)}) %collective-permute-start.20) | collective-permute-done | bytes 165920 | tf_op jit(solution)/shard_map/ppermute | solution.py:38
  117.0 3.1 collective-permute-start.23
  124.7 3.1 shard_map.300.wout.refs_10_
  127.8 4.5 shard_map.299.wz
  132.3 32.9 %shard_map.301 = (f32[2048,384]{1,0:T(8,128)}, f32[2048,384]{1,0:T(8,128)}, f32[2048,16,384]{2,1,0:T(8,128)}, f32[16,384]{1,0:T(8,128)}, f32[2048,384]{1,0:T(8,1...) custom-call(s32[1]{0:T(128)} %bitcast.1.s_ref, ...), custom_call_target="tpu_custom_call" | custom-call | flops 61341696 | bytes 1168688 | tf_op jit(solution)/shard_map/pallas_call | solution.py:243
  174.2 5.3 collective-permute-done.28
  179.6 5.4 %collective-permute-done.31 = bf16[128,1152]{1,0:T(8,128)(2,1)S(1)} collective-permute-done((bf16[128,1152]{1,0:T(8,128)(2,1)S(1)}, bf16[128,1152]{1,0:T(8,128)(2,1)S(1)}, u32[]{:S(2)}, u32[]{:S(2)}) %collective-permute-start.31) | collective-permute-done | bytes 294944 | tf_op jit(solution)/shard_map/ppermute | solution.py:33
  190.1 7.7 %shard_map.302.refs_11_ = bf16[1152,896]{1,0:T(8,128)(2,1)} custom-call(s32[4]{0:T(128)} %pad_add_fusion.1.order_ref, bf16[288,770]{1,0:T(8,128)(2,1)} %copy-done.16, bf16[288,770]{1,0:T(8,128)(2,1)} %copy-done.50, bf16[288,770]{1,0:T(8,128)(2,1)} %copy-done.51, bf16[288,770]{1,0:T(8,128)(2,1)} %copy-done.52), custom_call_target="tpu_custom_call" | custom-call | tf_op jit(solution)/shard_map/pallas_call | solution.py:141
  203.3 12.0 %collective-permute-done.37.refs_2_ = bf16[256,1152]{1,0:T(8,128)(2,1)S(1)} collective-permute-done((bf16[256,1152]{1,0:T(8,128)(2,1)S(1)}, bf16[256,1152]{1,0:T(8,128)(2,1)S(1)}, u32[]{:S(2)}, u32[]{:S(2)}) %collective-permute-start.37) | collective-permute-done | bytes 589856 | tf_op jit(solution)/shard_map/ppermute | solution.py:33
  218.0 4.1 collective-permute-done.41.refs_6_
  222.1 4.2 collective-permute-done.42.refs_7_
  229.9 37.3 %shard_map.303 = (bf16[256,1152]{1,0:T(8,128)(2,1)}, bf16[256,1152]{1,0:T(8,128)(2,1)}, bf16[256,1152]{1,0:T(8,128)(2,1)}, bf16[256,1152]{1,0:T(8,128)(2,1)}, bf...) custom-call(s32[2]{0:T(128)} %pad_add_fusion.2.s_ref, ...), custom_call_target="tpu_custom_call" | custom-call | flops 245366784 | bytes 616960 | tf_op jit(solution)/shard_map/pallas_call | solution.py:243
  282.8 4.9 collective-permute-done.50
  292.9 7.6 %convolution_convert_fusion = bf16[768,1152]{1,0:T(8,128)(2,1)S(1)} fusion(bf16[2048,768]{1,0:T(8,128)(2,1)} %get-tuple-element.285, bf16[2048,1152]{1,0:T(8,128)(2,1)} %get-tuple-element.286), kind=kOutput, calls=%fused_computation | convolution fusion | flops 3624763392 | bytes 9633792 | tf_op jit(solution)/shard_map/dot_general | solution.py:221
  313.8 11.2 %shard_map.304 = bf16[32,36,770]{2,1,0:T(8,128)(2,1)} custom-call(s32[1]{0:T(128)} %bitcast.1.s_ref, bf16[2048,1152]{1,0:T(8,128)(2,1)} %get-tuple-element.298.a_r, bf16[2048,896]{1,0:T(8,128)(2,1)} %get-tuple-element.300.b_r), custom_call_target="tpu_custom_call" | custom-call | flops 66060288 | bytes 158792 | tf_op jit(solution)/shard_map/pallas_call | solution.py:243
  330.9 6.8 %collective-permute-done.64.refs_6_ = bf16[128,1152]{1,0:T(8,128)(2,1)S(1)} collective-permute-done((bf16[128,1152]{1,0:T(8,128)(2,1)S(1)}, bf16[128,1152]{1,0:T(8,128)(2,1)S(1)}, u32[]{:S(2)}, u32[]{:S(2)}) %collective-permute-start.64) | collective-permute-done | bytes 294944 | tf_op jit(solution)/shard_map/ppermute | solution.py:33
  345.2 57.2 %shard_map.305 = (bf16[2048,1152]{1,0:T(8,128)(2,1)}, bf16[2048,384]{1,0:T(8,128)(2,1)}, bf16[2048,128]{1,0:T(8,128)(2,1)}, f32[2048,384]{1,0:T(8,128)}, f32[384...) custom-call(s32[1]{0:T(128)} %bitcast.1.s_ref, bf16[256,1152]{1,0:T(8,128)(2,1)} %copy-done.15, ...), custom_call_target="tpu_custom_call" | custom-call | flops 35389440 | bytes 1215688 | tf_op jit(solution)/shard_map/pallas_call | solution.py:243
  411.0 6.3 %fusion.23.gout_r = f32[384,1152]{1,0:T(8,128)} fusion(bf16[2048,384]{1,0:T(8,128)(2,1)} %get-tuple-element.318, bf16[2048,1152]{1,0:T(8,128)(2,1)} %get-tuple-element.319), kind=kOutput, calls=%fused_computation.107 | convolution fusion | flops 1811939328 | bytes 8060928 | tf_op jit(solution)/shard_map/dot_general | solution.py:221
  417.3 8.4 %shard_map.306.gz_r = bf16[32,36,288]{2,1,0:T(8,128)(2,1)} custom-call(s32[1]{0:T(128)} %bitcast.1.s_ref, bf16[2048,1152]{1,0:T(8,128)(2,1)} %get-tuple-element.320.n_r.a_r, bf16[2048,384]{1,0:T(8,128)(2,1)} %get-tuple-element.321.b_r.dz_r), custom_call_target="tpu_custom_call" | custom-call | flops 28311552 | bytes 108672 | tf_op jit(solution)/shard_map/pallas_call | solution.py:243
  430.1 3.5 all-to-all-start.2
  435.6 22.8 %shard_map.307 = (bf16[256,1152]{1,0:T(8,128)(2,1)}, bf16[256,1152]{1,0:T(8,128)(2,1)}, bf16[256,1152]{1,0:T(8,128)(2,1)}, bf16[256,1152]{1,0:T(8,128)(2,1)}, bf...) custom-call(s32[5]{0:T(128)} %concatenate.48.s_ref, ...), custom_call_target="tpu_custom_call" | custom-call | flops 91226112 | bytes 456608 | tf_op jit(solution)/shard_map/pallas_call | solution.py:243
  463.6 4.6 all-to-all-start.3
  477.0 9.4 %collective-permute-done.81 = bf16[128,1152]{1,0:T(8,128)(2,1)} collective-permute-done((bf16[128,1152]{1,0:T(8,128)(2,1)S(1)}, bf16[128,1152]{1,0:T(8,128)(2,1)}, u32[]{:S(2)}, u32[]{:S(2)}) %collective-permute-start.81) | collective-permute-done | bytes 294944 | tf_op jit(solution)/shard_map/ppermute | solution.py:33
  509.3 5.6 %collective-permute-done.87 = bf16[128,1152]{1,0:T(8,128)(2,1)S(1)} collective-permute-done((bf16[128,1152]{1,0:T(8,128)(2,1)S(1)}, bf16[128,1152]{1,0:T(8,128)(2,1)S(1)}, u32[]{:S(2)}, u32[]{:S(2)}) %collective-permute-start.87) | collective-permute-done | bytes 294944 | tf_op jit(solution)/shard_map/ppermute | solution.py:33
  (506 shorter events, 191.6 us)
Async XLA Ops:
  7.2 19.0 %collective-permute-start = (bf16[256,1152]{1,0:T(8,128)(2,1)}, bf16[256,1152]{1,0:T(8,128)(2,1)}, u32[]{:S(2)}, u32[]{:S(2)}) collective-permute-start(bf16[256,1152]{1,0:T(8,128)(2,1)} %bitcast.87), channel_id=1, source_target_pairs={{0,8},{4,12},{8,0},{12,4},{16,24},{20,28},{24,16},{28,20},{1,9},{5... | collective-permute-start | bytes 1769480 | tf_op jit(solution)/shard_map/ppermute | solution.py:33
  27.3 27.7 %all-to-all-start = ((bf16[32,36,290]{2,1,0:T(8,128)(2,1)}), bf16[32,36,290]{2,1,0:T(8,128)(2,1)S(1)}, u32[]{:S(2)}, u32[]{:S(2)}) async-start(bf16[32,36,290]{2,1,0:T(8,128)(2,1)} %bitcast.12), calls=%async_computation | async-start | bytes 1966080 | tf_op jit(solution)/shard_map/all_to_all | solution.py:192
  31.3 156.2 %all-gather.4.cloned.1.call-start = ((), (), s32[]{:S(2)}) async-start(), calls=%async_computation.6 | async-start | bytes 5898240 | tf_op jit(solution)/shard_map/all_gather | solution.py:942
  36.7 18.7 %collective-permute-start.5 = (bf16[256,1152]{1,0:T(8,128)(2,1)S(1)}, bf16[256,1152]{1,0:T(8,128)(2,1)}, u32[]{:S(2)}, u32[]{:S(2)}) collective-permute-start(bf16[256,1152]{1,0:T(8,128)(2,1)S(1)} %bitcast.90), channel_id=1, source_target_pairs={{0,4},{4,0},{8,12},{12,8},{16,20},{20,16},{24,28},{28,24},{1,5},{5... | collective-permute-start | bytes 1769480 | tf_op jit(solution)/shard_map/ppermute | solution.py:33
  36.7 18.7 %collective-permute-start.6 = (bf16[256,1152]{1,0:T(8,128)(2,1)}, bf16[256,1152]{1,0:T(8,128)(2,1)}, u32[]{:S(2)}, u32[]{:S(2)}) collective-permute-start(bf16[256,1152]{1,0:T(8,128)(2,1)} %collective-permute-done.refs_2_), channel_id=1, source_target_pairs={{0,4},{4,0},{8,12},{12,8},{16,20},{20,16},{24,28},{28,24},{1,5},{5... | collective-permute-start | bytes 1769480 | tf_op jit(solution)/shard_map/ppermute | solution.py:33
  37.2 18.2 %collective-permute-start.7 = (bf16[256,1152]{1,0:T(8,128)(2,1)}, bf16[256,1152]{1,0:T(8,128)(2,1)}, u32[]{:S(2)}, u32[]{:S(2)}) collective-permute-start(bf16[256,1152]{1,0:T(8,128)(2,1)} %collective-permute-done.1.refs_4_), channel_id=1, source_target_pairs={{0,4},{4,0},{8,12},{12,8},{16,20},{20,16},{24,28},{28,24},{1,5},{5... | collective-permute-start | bytes 1769480 | tf_op jit(solution)/shard_map/ppermute | solution.py:33
  63.5 28.5 %collective-permute-start.12 = (bf16[72,1152]{1,0:T(8,128)(2,1)}, bf16[72,1152]{1,0:T(8,128)(2,1)}, u32[]{:S(2)}, u32[]{:S(2)}) collective-permute-start(bf16[72,1152]{1,0:T(8,128)(2,1)} %refs_0_), channel_id=1, source_target_pairs={{0,1},{1,2},{2,3},{3,0},{4,5},{5,6},{6,7},{7,4},{8,9},{9,10},{10,1... | collective-permute-start | bytes 497672 | tf_op jit(solution)/shard_map/ppermute | solution.py:38
  66.6 25.4 %collective-permute-start.13 = (bf16[72,1152]{1,0:T(8,128)(2,1)}, bf16[72,1152]{1,0:T(8,128)(2,1)}, u32[]{:S(2)}, u32[]{:S(2)}) collective-permute-start(bf16[72,1152]{1,0:T(8,128)(2,1)} %refs_0_), channel_id=1, source_target_pairs={{0,2},{1,3},{2,0},{3,1},{4,6},{5,7},{6,4},{7,5},{8,10},{9,11},{10,... | collective-permute-start | bytes 497672 | tf_op jit(solution)/shard_map/ppermute | solution.py:38
  67.3 24.7 %collective-permute-start.14 = (bf16[72,1152]{1,0:T(8,128)(2,1)}, bf16[72,1152]{1,0:T(8,128)(2,1)}, u32[]{:S(2)}, u32[]{:S(2)}) collective-permute-start(bf16[72,1152]{1,0:T(8,128)(2,1)} %refs_0_), channel_id=1, source_target_pairs={{0,3},{1,0},{2,1},{3,2},{4,7},{5,4},{6,5},{7,6},{8,11},{9,8},{10,9... | collective-permute-start | bytes 497672 | tf_op jit(solution)/shard_map/ppermute | solution.py:38
  71.0 20.7 %all-to-all-start.1 = ((bf16[8,36,1058]{2,1,0:T(8,128)(2,1)}), bf16[8,36,1058]{2,1,0:T(8,128)(2,1)S(1)}, u32[]{:S(2)}, u32[]{:S(2)}) async-start(bf16[8,36,1058]{2,1,0:T(8,128)(2,1)} %copy.99), calls=%async_computation.1 | async-start | bytes 1474560 | tf_op jit(solution)/shard_map/all_to_all | solution.py:938
  74.6 155.3 %all-gather.6.cloned.1.call-start = ((), (), s32[]{:S(2)}) async-start(), calls=%async_computation.9 | async-start | bytes 2211840 | tf_op jit(solution)/shard_map/all_gather | solution.py:972
  93.7 19.9 %collective-permute-start.16 = (bf16[1024,128]{1,0:T(8,128)(2,1)S(1)}, bf16[1024,128]{1,0:T(8,128)(2,1)S(1)}, u32[]{:S(2)}, u32[]{:S(2)}) collective-permute-start(bf16[1024,128]{1,0:T(8,128)(2,1)S(1)} %fusion.13), channel_id=1, source_target_pairs={{0,8},{4,12},{8,0},{12,4},{16,24},{20,28},{24,16},{28,20},{1,9},{5... | collective-permute-start | bytes 786440 | tf_op jit(solution)/shard_map/ppermute | solution.py:33
  93.8 19.8 %collective-permute-start.17 = (bf16[1024,128]{1,0:T(8,128)(2,1)S(1)}, bf16[1024,128]{1,0:T(8,128)(2,1)S(1)}, u32[]{:S(2)}, u32[]{:S(2)}) collective-permute-start(bf16[1024,128]{1,0:T(8,128)(2,1)S(1)} %fusion.13), channel_id=1, source_target_pairs={{0,16},{4,20},{8,24},{12,28},{16,0},{20,4},{24,8},{28,12},{1,17},{... | collective-permute-start | bytes 786440 | tf_op jit(solution)/shard_map/ppermute | solution.py:33
  94.9 19.4 %collective-permute-start.18 = (bf16[1024,128]{1,0:T(8,128)(2,1)S(1)}, bf16[1024,128]{1,0:T(8,128)(2,1)S(1)}, u32[]{:S(2)}, u32[]{:S(2)}) collective-permute-start(bf16[1024,128]{1,0:T(8,128)(2,1)S(1)} %fusion.13), channel_id=1, source_target_pairs={{0,24},{4,28},{8,16},{12,20},{16,8},{20,12},{24,0},{28,4},{1,25},{... | collective-permute-start | bytes 786440 | tf_op jit(solution)/shard_map/ppermute | solution.py:33
  117.0 48.3 %collective-permute-start.23 = (bf16[288,770]{1,0:T(8,128)(2,1)S(1)}, bf16[288,770]{1,0:T(8,128)(2,1)S(1)}, u32[]{:S(2)}, u32[]{:S(2)}) collective-permute-start(bf16[288,770]{1,0:T(8,128)(2,1)S(1)} %slice.179.refs_0_), channel_id=1, source_target_pairs={{0,1},{1,2},{2,3},{3,0},{4,5},{5,6},{6,7},{7,4},{8,9},{9,10},{10,1... | collective-permute-start | bytes 1330568 | tf_op jit(solution)/shard_map/ppermute | solution.py:38
  120.1 45.2 %collective-permute-start.24 = (bf16[288,770]{1,0:T(8,128)(2,1)S(1)}, bf16[288,770]{1,0:T(8,128)(2,1)S(1)}, u32[]{:S(2)}, u32[]{:S(2)}) collective-permute-start(bf16[288,770]{1,0:T(8,128)(2,1)S(1)} %slice.179.refs_0_), channel_id=1, source_target_pairs={{0,2},{1,3},{2,0},{3,1},{4,6},{5,7},{6,4},{7,5},{8,10},{9,11},{10,... | collective-permute-start | bytes 1330568 | tf_op jit(solution)/shard_map/ppermute | solution.py:38
  120.4 44.9 %collective-permute-start.25 = (bf16[288,770]{1,0:T(8,128)(2,1)S(1)}, bf16[288,770]{1,0:T(8,128)(2,1)S(1)}, u32[]{:S(2)}, u32[]{:S(2)}) collective-permute-start(bf16[288,770]{1,0:T(8,128)(2,1)S(1)} %slice.179.refs_0_), channel_id=1, source_target_pairs={{0,3},{1,0},{2,1},{3,2},{4,7},{5,4},{6,5},{7,6},{8,11},{9,8},{10,9... | collective-permute-start | bytes 1330568 | tf_op jit(solution)/shard_map/ppermute | solution.py:38
  174.2 24.4 %collective-permute-start.26 = (bf16[256,1152]{1,0:T(8,128)(2,1)}, bf16[256,1152]{1,0:T(8,128)(2,1)S(1)}, u32[]{:S(2)}, u32[]{:S(2)}) collective-permute-start(bf16[256,1152]{1,0:T(8,128)(2,1)} %get-tuple-element.245), channel_id=1, source_target_pairs={{0,4},{4,0},{8,12},{12,8},{16,20},{20,16},{24,28},{28,24},{1,5},{5... | collective-permute-start | bytes 1769480 | tf_op jit(solution)/shard_map/ppermute | solution.py:33
  187.6 242.5 %reduce-scatter.3.cloned.1.call-start = ((), (), s32[]{:S(2)}) async-start(), calls=%async_computation.7 | async-start | bytes 2867200 | tf_op jit(solution)/shard_map/reduce_scatter | solution.py:1000
  203.3 24.2 %collective-permute-start.36 = (bf16[256,1152]{1,0:T(8,128)(2,1)S(1)}, bf16[256,1152]{1,0:T(8,128)(2,1)S(1)}, u32[]{:S(2)}, u32[]{:S(2)}) collective-permute-start(bf16[256,1152]{1,0:T(8,128)(2,1)S(1)} %multiply_convert_fusion.refs_0_), channel_id=1, source_target_pairs={{0,4},{4,0},{8,12},{12,8},{16,20},{20,16},{24,28},{28,24},{1,5},{5... | collective-permute-start | bytes 1769480 | tf_op jit(solution)/shard_map/ppermute | solution.py:33
  279.2 27.4 %collective-permute-start.45 = (bf16[256,1152]{1,0:T(8,128)(2,1)}, bf16[256,1152]{1,0:T(8,128)(2,1)}, u32[]{:S(2)}, u32[]{:S(2)}) collective-permute-start(bf16[256,1152]{1,0:T(8,128)(2,1)} %get-tuple-element.266), channel_id=1, source_target_pairs={{0,4},{4,0},{8,12},{12,8},{16,20},{20,16},{24,28},{28,24},{1,5},{5... | collective-permute-start | bytes 1769480 | tf_op jit(solution)/shard_map/ppermute | solution.py:33
  313.8 24.6 %collective-permute-start.59 = (bf16[256,1152]{1,0:T(8,128)(2,1)S(1)}, bf16[256,1152]{1,0:T(8,128)(2,1)}, u32[]{:S(2)}, u32[]{:S(2)}) collective-permute-start(bf16[256,1152]{1,0:T(8,128)(2,1)S(1)} %get-tuple-element.453.refs_0_), channel_id=1, source_target_pairs={{0,4},{4,0},{8,12},{12,8},{16,20},{20,16},{24,28},{28,24},{1,5},{5... | collective-permute-start | bytes 1769480 | tf_op jit(solution)/shard_map/ppermute | solution.py:33
  341.6 135.4 %reduce-scatter.5.cloned.1.call-start = ((), (), s32[]{:S(2)}) async-start(), calls=%async_computation.8 | async-start | bytes 2211840 | tf_op jit(solution)/shard_map/reduce_scatter | solution.py:993
  341.6 60.7 %collective-permute-start.68 = (bf16[256,1152]{1,0:T(8,128)(2,1)}, bf16[256,1152]{1,0:T(8,128)(2,1)S(1)}, u32[]{:S(2)}, u32[]{:S(2)}) collective-permute-start(bf16[256,1152]{1,0:T(8,128)(2,1)} %add_convert_fusion.4), channel_id=1, source_target_pairs={{0,8},{4,12},{8,0},{12,4},{16,24},{20,28},{24,16},{28,20},{1,9},{5... | collective-permute-start | bytes 1769480 | tf_op jit(solution)/shard_map/ppermute | solution.py:33
  342.9 59.5 %collective-permute-start.69 = (bf16[256,1152]{1,0:T(8,128)(2,1)}, bf16[256,1152]{1,0:T(8,128)(2,1)S(1)}, u32[]{:S(2)}, u32[]{:S(2)}) collective-permute-start(bf16[256,1152]{1,0:T(8,128)(2,1)} %add_convert_fusion.3), channel_id=1, source_target_pairs={{0,16},{4,20},{8,24},{12,28},{16,0},{20,4},{24,8},{28,12},{1,17},{... | collective-permute-start | bytes 1769480 | tf_op jit(solution)/shard_map/ppermute | solution.py:33
  343.6 58.8 %collective-permute-start.70 = (bf16[256,1152]{1,0:T(8,128)(2,1)}, bf16[256,1152]{1,0:T(8,128)(2,1)}, u32[]{:S(2)}, u32[]{:S(2)}) collective-permute-start(bf16[256,1152]{1,0:T(8,128)(2,1)} %add_convert_fusion.2), channel_id=1, source_target_pairs={{0,24},{4,28},{8,16},{12,20},{16,8},{20,12},{24,0},{28,4},{1,25},{... | collective-permute-start | bytes 1769480 | tf_op jit(solution)/shard_map/ppermute | solution.py:33
  407.5 18.2 %collective-permute-start.72 = (bf16[1024,128]{1,0:T(8,128)(2,1)}, bf16[1024,128]{1,0:T(8,128)(2,1)S(1)}, u32[]{:S(2)}, u32[]{:S(2)}) collective-permute-start(bf16[1024,128]{1,0:T(8,128)(2,1)} %fusion.14), channel_id=1, source_target_pairs={{0,8},{4,12},{8,0},{12,4},{16,24},{20,28},{24,16},{28,20},{1,9},{5... | collective-permute-start | bytes 786440 | tf_op jit(solution)/shard_map/ppermute | solution.py:33
  430.1 28.3 %all-to-all-start.2 = ((bf16[8,36,770]{2,1,0:T(8,128)(2,1)}), bf16[8,36,770]{2,1,0:T(8,128)(2,1)S(1)}, u32[]{:S(2)}, u32[]{:S(2)}) async-start(bf16[8,36,770]{2,1,0:T(8,128)(2,1)} %bitcast.108), calls=%async_computation.3 | async-start | bytes 1146880 | tf_op jit(solution)/shard_map/all_to_all | solution.py:1027
  459.6 43.9 %collective-permute-start.83 = (bf16[72,1408]{1,0:T(8,128)(2,1)}, bf16[72,1408]{1,0:T(8,128)(2,1)S(1)}, u32[]{:S(2)}, u32[]{:S(2)}) collective-permute-start(bf16[72,1408]{1,0:T(8,128)(2,1)} %get-tuple-element.363), channel_id=1, source_target_pairs={{0,1},{1,2},{2,3},{3,0},{4,5},{5,6},{6,7},{7,4},{8,9},{9,10},{10,1... | collective-permute-start | bytes 608264 | tf_op jit(solution)/shard_map/ppermute | solution.py:38
  460.0 43.5 %collective-permute-start.84 = (bf16[72,1408]{1,0:T(8,128)(2,1)}, bf16[72,1408]{1,0:T(8,128)(2,1)}, u32[]{:S(2)}, u32[]{:S(2)}) collective-permute-start(bf16[72,1408]{1,0:T(8,128)(2,1)} %get-tuple-element.364), channel_id=1, source_target_pairs={{0,2},{1,3},{2,0},{3,1},{4,6},{5,7},{6,4},{7,5},{8,10},{9,11},{10,... | collective-permute-start | bytes 608264 | tf_op jit(solution)/shard_map/ppermute | solution.py:38
  462.3 41.4 %collective-permute-start.85 = (bf16[72,1408]{1,0:T(8,128)(2,1)}, bf16[72,1408]{1,0:T(8,128)(2,1)}, u32[]{:S(2)}, u32[]{:S(2)}) collective-permute-start(bf16[72,1408]{1,0:T(8,128)(2,1)} %get-tuple-element.365), channel_id=1, source_target_pairs={{0,3},{1,0},{2,1},{3,2},{4,7},{5,4},{6,5},{7,6},{8,11},{9,8},{10,9... | collective-permute-start | bytes 608264 | tf_op jit(solution)/shard_map/ppermute | solution.py:38
  463.6 54.2 %all-to-all-start.3 = ((bf16[32,36,576]{2,1,0:T(8,128)(2,1)}), bf16[32,36,576]{2,1,0:T(8,128)(2,1)}, u32[]{:S(2)}, u32[]{:S(2)}) async-start(bf16[32,36,576]{2,1,0:T(8,128)(2,1)} %get-tuple-element.371), calls=%async_computation.5 | async-start | bytes 3276800 | tf_op jit(solution)/shard_map/all_to_all | solution.py:192
  (162 other events, 1167.4 us)
Sparse Core Ops, SparseCore 0:
  55.6 48.5 all-gather.3
  187.7 38.2 all-gather.5
  341.7 45.7 reduce-scatter.2
  427.8 36.5 reduce-scatter.4

commit v5 on v4

--- a/solution.py
+++ b/solution.py
@@ -46,9 +46,10 @@
     return [[b] for b in jnp.split(x, lax.axis_size("wide"), axis=0)]
 
 
-def gather_wide(block, meanwhile=None):
+def gather_wide(block, meanwhile=None, second=None):
     if not relative():
         made = meanwhile(block) if meanwhile else ()
+        made = (made, second(block)) if second else made
         return blocks_of(lax.all_gather(block, "wide", axis=0, tiled=True)), made
     half = block.shape[0] // 2
     mate = swap(block, 1)
@@ -58,6 +59,9 @@
         made = meanwhile(block)
         a, b, made = lax.optimization_barrier((a, b, made))
     c0, c1 = swap(a[:half], 4), swap(b[half:], 2)
+    if second:
+        c0, c1, late = lax.optimization_barrier((c0, c1, second(a)))
+        made = (made, late)
     out = [[block], [mate], [a], [swap(a, 1)], [b], [swap(b, 1)], [c0, c1], [swap(c0, 1), swap(c1, 1)]]
     return out, made
 
@@ -269,28 +273,25 @@
     pltpu.make_async_copy(held.at[i], held.at[i], sems.at[i]).wait()
 
 
-def send_rows(value, stage, sems, outs, step, steps, block, at):
-    slot = step % 2
-    n = value.shape[0]
-
-    def sent(k):
-        return pltpu.make_async_copy(stage.at[k], stage.at[k], sems.at[k])
-
+def send_ready(stage, sems, step):
     @pl.when(step >= 2)
     def _():
-        sent(slot).wait()
-
-    stage[slot] = value
+        pltpu.make_async_copy(stage.at[step % 2], stage.at[step % 2], sems.at[step % 2]).wait()
+
+
+def send_rows(stage, sems, outs, step, steps, block, at):
+    slot = step % 2
     for k, out in enumerate(outs):
 
         @pl.when(block == k)
         def _(out=out):
-            pltpu.make_async_copy(stage.at[slot], out.at[pl.ds(at, n)], sems.at[slot]).start()
+            part = out.at[pl.ds(at, stage.shape[1])]
+            pltpu.make_async_copy(stage.at[slot], part, sems.at[slot]).start()
 
     @pl.when(step == steps - 1)
     def _():
-        sent(0).wait()
-        sent(1).wait()
+        for k in range(2):
+            pltpu.make_async_copy(stage.at[k], stage.at[k], sems.at[k]).wait()
 
 
 def taken(refs, lengths):
@@ -404,7 +405,9 @@
         state, dt_s, u_s, y_s, stage, sems = refs
         i = pl.program_id(0)
 
-        @pl.when(pl.program_id(0) == 0)
+        send_ready(stage, sems, i)
+
+        @pl.when(i == 0)
         def _():
             state[...] = jnp.zeros_like(state)
 
@@ -435,8 +438,8 @@
         z_o[...] = z
         gated = (out * z * sigmoid(z)).astype(bf16)
         gated_o[...] = gated
-        value = mm(gated, wout[...]).astype(bf16)
-        send_rows(value, stage, sems, parts, i, blocks, (i // per) ^ s_ref[0], i % per * TIME_BLOCK)
+        stage[i % 2] = mm(gated, wout[...]).astype(bf16)
+        send_rows(stage, sems, parts, i, blocks, (i // per) ^ s_ref[0], i % per * TIME_BLOCK)
 
     here = lambda i, s: i
     rel = lambda i, s: ((i // per) ^ s) * per + i % per
@@ -493,6 +496,16 @@
             for k in range(down.shape[0]):
                 for e in range(EXPERTS):
                     down_s[e * ff + k * share : e * ff + (k + 1) * share, :] = down_r[k, e]
+
+        slot = i % 2
+
+        def sent(k):
+            for buffer, sem in ((stage, stage_sems), (stage_2, stage_2_sems)):
+                pltpu.make_async_copy(buffer.at[k], buffer.at[k], sem.at[k]).wait()
+
+        @pl.when(i >= 2)
+        def _():
+            sent(slot)
 
         wait_block(held, sems, i)
         n_o[...] = held[i]
@@ -515,8 +528,7 @@
             [jnp.where(second, 0.0, hid_f), jnp.where(second, hid_f, 0.0)], axis=1
         ).astype(bf16)
         hid_o[...] = both
-        value = (gate * mm(both, down_s[...])).astype(bf16)
-        send_rows(value, stage_2, stage_2_sems, outs, i, blocks, i, 0)
+        stage_2[slot] = (gate * mm(both, down_s[...])).astype(bf16)
         dex_o[...] = (gate * upstream.astype(f32)).astype(bf16)
         lowered = mm_t(upstream, down_s[...])
         d_hid = jnp.where(second, lowered[:, ff:], lowered[:, :ff])
@@ -530,8 +542,18 @@
             [jnp.where(second, 0.0, d_pre), jnp.where(second, d_pre, 0.0), d_logits], axis=1
         ).astype(bf16)
         both_o[...] = d_both
-        value = mm_t(d_both, up_r[...]).astype(bf16)
-        send_rows(value, stage, stage_sems, backs, i, blocks, i, 0)
+        stage[slot] = mm_t(d_both, up_r[...]).astype(bf16)
+        for k in range(blocks):
+
+            @pl.when(i == k)
+            def _(k=k):
+                for buffer, sem, out in ((stage, stage_sems, backs[k]), (stage_2, stage_2_sems, outs[k])):
+                    pltpu.make_async_copy(buffer.at[k % 2], out, sem.at[k % 2]).start()
+
+        @pl.when(i == blocks - 1)
+        def _():
+            sent(0)
+            sent(1)
 
     here = lambda i, s: i
     made = call(
@@ -721,6 +743,8 @@
         gx_o, ext, gx, gsel, flat, held, stage, sems = refs
         i = pl.program_id(0)
 
+        send_ready(stage, sems, i)
+
         @pl.when(pl.program_id(0) == 0)
         def _():
             ext[rows:, :] = jnp.zeros((8, wid), f32)
@@ -742,10 +766,10 @@
             flat[k : k + 1, :] += jnp.sum(moved * x, axis=0, keepdims=True)
         ext[rows:, :] = d_conv[:8, :]
         d_x = d_x.astype(bf16)
-        value = (mm_t(d_x, wx[...]) + mm_t(dz_r[...], wz[...])).astype(bf16)
-        send_rows(value, stage, sems, parts, i, blocks, (blocks - 1 - i) ^ s_ref[0], 0)
+        stage[i % 2] = (mm_t(d_x, wx[...]) + mm_t(dz_r[...], wz[...])).astype(bf16)
         gx[...] += t_mm(n_r[...], d_x)
         gsel[...] += t_mm(act_r[...], low)
+        send_rows(stage, sems, parts, i, blocks, (blocks - 1 - i) ^ s_ref[0], 0)
 
         @pl.when(pl.program_id(0) == blocks - 1)
         def _():
@@ -956,7 +980,9 @@
     sel_part, up_parts, out_pieces = lax.optimization_barrier((sel_part, up_parts, out_pieces))
     z_pieces = turns(up_parts[:, both + EXPERTS :])
     up_parts = up_parts[:, : both + EXPERTS]
-    selected, z_pieces = reduce_wide(sel_part, lambda low: z_pieces)
+    selected, (z_pieces, weight_out) = reduce_wide(
+        sel_part, lambda low: (z_pieces, gather_channels(out_pieces, (D,), wid)[0])
+    )
     weight_z = ordered_rows(z_pieces, d_rows, wid)
 
     up_cols = -(-(both + EXPERTS) // LANES) * LANES
@@ -964,7 +990,6 @@
     valid_own = (w * rows + jnp.arange(rows))[:, None] < lengths[0]
     upstream = jnp.where(valid_own, cotangent[0].astype(f32), 0.0)
 
-    (weight_out,) = gather_channels(out_pieces, (D,), wid)
     proj_z, step_lin, kept, end, mixed, gated, *mix_part = middle(
         flip[None], selected, conv_act, normed, weight_z, weight_step, step_shift, skip, a2, weight_out
     )
@@ -981,21 +1006,26 @@
     normed_two, hidden_both, d_both, d_expert = made
 
     def beside(hop):
-        hidden, outs = lax.optimization_barrier((hidden_both, out_parts, hop))[:2]
+        hidden = after(hidden_both, hop)
         grad = t_mm(hidden, d_expert).astype(bf16)
         grad = grad.reshape(EXPERTS, narrow, f_rows, D).transpose(1, 0, 2, 3)
-        if not relative():
-            return grad, outs
-        pair = lambda q: outs[2 * q].astype(f32) + swap(outs[2 * q + 1], 1).astype(f32)
-        return grad, [pair(q).astype(bf16) for q in range(4)]
-
-    d_normed_two, (grad_down, out_sums) = scatter_wide(back_parts, beside, True)
+        return grad
+
+    d_normed_two, grad_down = scatter_wide(back_parts, beside, True)
     grad_down = lax.psum_scatter(grad_down, "narrow", scatter_dimension=0)
     d_hidden_one = upstream + norm_backward(hidden_one, inverse_two, gain_two, d_normed_two)
     d_low = d_hidden_one.astype(bf16)
-    d_mix, grad_up = gather_wide(
+    def output_sums(hop):
+        outs = after(out_parts, hop)
+        if not relative():
+            return outs
+        pair = lambda q: outs[2 * q].astype(f32) + swap(outs[2 * q + 1], 1).astype(f32)
+        return [pair(q).astype(bf16) for q in range(4)]
+
+    d_mix, (grad_up, out_sums) = gather_wide(
         d_low,
         lambda low: row_grad(flip[None], normed_two, after(d_both, low), both + EXPERTS, d_rows, True),
+        output_sums,
     )
     grad_up = lax.psum_scatter(
         after(grad_up, d_mix).reshape(narrow, wide, d_rows, both + EXPERTS), "narrow", scatter_dimension=0

time: 541 us -> 535 us (0.989)
  Pallas kernels: 201 us -> 194 us
    pallas_call x7, Pallas kernels: 182 us -> 174 us  [call(): pl.pallas_call(kernel, grid_spec=pltpu.PrefetchScalarGridSpec(num_scalar_...]
    unnamed x203 -> x191, local copies, waits for them, and re-layouts: 18.4 us -> 18.3 us
  transfers between devices with their start and end apart: 97 -> 97, of which waited for: 32 -> 34; matrix products, arithmetic and copies ran while one was open for 16% -> 17% of each run, Pallas kernels for 30% -> 30%
where the time goes in v5:
time: 535 us; the launch traced here: 526 us
  Pallas kernels  194 us (36%)
  waiting for transfers between devices  110 us (21%)
  starting transfers between devices  92.1 us (17%)
  local copies, waits for them, and re-layouts  53.1 us (10%)
  other arithmetic  46.4 us (9%)
  between operations  16.4 us (3%)
  matrix products  13.9 us (3%)
    pallas_call x7, Pallas kernels, call(): pl.pallas_call(kernel, grid_spec=pltpu.PrefetchScalarGridSpec(num_scalar_...  174 us
    ppermute x74, waiting for transfers between devices, swap(): return lax.ppermute(x, 'wide', [(i, i ^ k) for i in range(n)])  86.2 us
    ppermute x74, starting transfers between devices, swap(): return lax.ppermute(x, 'wide', [(i, i ^ k) for i in range(n)])  53.5 us
    ppermute x15, starting transfers between devices, turn(): return lax.ppermute(x, 'narrow', [(i, (i + k) % n) for i in range(n)])  22.7 us
    unnamed x191, local copies, waits for them, and re-layouts  18.3 us
    dot_general x2, matrix products, t_mm(): lax.dot_general(a, b, (((0,), (0,)), ((), ())), preferred_element_type=f32)  13.9 us
    ppermute x15, waiting for transfers between devices, turn(): return lax.ppermute(x, 'narrow', [(i, (i + k) % n) for i in range(n)])  13.3 us
    pallas_call x2, Pallas kernels, ordered_rows(): pl.pallas_call(kernel, in_specs=[pl.BlockSpec(memory_space=pltpu.SMEM)] +...  12.2 us
  transfers between devices with their start and end apart: 97, of which 34 were waited for; matrix products, arithmetic and copies ran while one was open for 17% of the time, Pallas kernels for 30%

profile of v5, /device:TPU:0, one launch (start us, length us, event | category | flops | bytes accessed | tf_op | source)
XLA Modules:
  0.0 525.7 jit_solution(12852170020320950655)
XLA Ops:
  27.3 4.0 all-to-all-start
  37.2 11.3 %collective-permute-done.8.refs_6_ = bf16[128,1152]{1,0:T(8,128)(2,1)} collective-permute-done((bf16[128,1152]{1,0:T(8,128)(2,1)S(1)}, bf16[128,1152]{1,0:T(8,128)(2,1)}, u32[]{:S(2)}, u32[]{:S(2)}) %collective-permute-start.8) | collective-permute-done | bytes 294944 | tf_op jit(solution)/shard_map/ppermute | solution.py:33
  50.2 4.9 all-to-all-done
  71.0 3.5 all-to-all-start.1
  75.2 11.7 %shard_map.298 = (bf16[2048,1152]{1,0:T(8,128)(2,1)}, f32[2048,384]{1,0:T(8,128)}, f32[2048,384]{1,0:T(8,128)}, bf16[2048,384]{1,0:T(8,128)(2,1)}, bf16[2048,128]{1,0:T(8,128)(2,1)}) custom-call(s32[1]{0:T(128)} %bitcast.1.s_ref, bf16[256,1152]{1,0:T(8,128)(2,1)} %bitcast.89, bf16[256,1152]{1,0:T(8,128)(2,1)} %collective-permute-done.5.refs_1_, ...), custom_call_target="tpu_custom_call" | custom-call | flops 31457280 | bytes 294080 | tf_op jit(solution)/shard_map/pallas_call | solution.py:247
  86.9 4.7 all-to-all-done.1
  97.2 5.2 collective-permute-done.19.refs_1_
  102.3 3.2 shard_map.299.wout.refs_10_
  105.5 5.9 %collective-permute-done.20.refs_2_ = bf16[288,288]{1,0:T(8,128)(2,1)S(1)} collective-permute-done((bf16[288,288]{1,0:T(8,128)(2,1)S(1)}, bf16[288,288]{1,0:T(8,128)(2,1)S(1)}, u32[]{:S(2)}, u32[]{:S(2)}) %collective-permute-start.20) | collective-permute-done | bytes 165920 | tf_op jit(solution)/shard_map/ppermute | solution.py:38
  116.3 3.1 collective-permute-start.23
  124.3 4.5 shard_map.300.wz
  128.8 32.7 %shard_map.301 = (f32[2048,384]{1,0:T(8,128)}, f32[2048,384]{1,0:T(8,128)}, f32[2048,16,384]{2,1,0:T(8,128)}, f32[16,384]{1,0:T(8,128)}, f32[2048,384]{1,0:T(8,1...) custom-call(s32[1]{0:T(128)} %bitcast.1.s_ref, ...), custom_call_target="tpu_custom_call" | custom-call | flops 61341696 | bytes 1168688 | tf_op jit(solution)/shard_map/pallas_call | solution.py:247
  170.4 5.3 %collective-permute-done.28 = bf16[128,1152]{1,0:T(8,128)(2,1)S(1)} collective-permute-done((bf16[128,1152]{1,0:T(8,128)(2,1)S(1)}, bf16[128,1152]{1,0:T(8,128)(2,1)S(1)}, u32[]{:S(2)}, u32[]{:S(2)}) %collective-permute-start.28) | collective-permute-done | bytes 294944 | tf_op jit(solution)/shard_map/ppermute | solution.py:33
  175.8 5.4 %collective-permute-done.31 = bf16[128,1152]{1,0:T(8,128)(2,1)S(1)} collective-permute-done((bf16[128,1152]{1,0:T(8,128)(2,1)S(1)}, bf16[128,1152]{1,0:T(8,128)(2,1)S(1)}, u32[]{:S(2)}, u32[]{:S(2)}) %collective-permute-start.31) | collective-permute-done | bytes 294944 | tf_op jit(solution)/shard_map/ppermute | solution.py:33
  186.4 7.7 %shard_map.302.refs_11_ = bf16[1152,896]{1,0:T(8,128)(2,1)} custom-call(s32[4]{0:T(128)} %pad_add_fusion.1.order_ref, bf16[288,770]{1,0:T(8,128)(2,1)} %copy-done.14, bf16[288,770]{1,0:T(8,128)(2,1)} %copy-done.46, bf16[288,770]{1,0:T(8,128)(2,1)} %copy-done.47, bf16[288,770]{1,0:T(8,128)(2,1)} %copy-done.48), custom_call_target="tpu_custom_call" | custom-call | tf_op jit(solution)/shard_map/pallas_call | solution.py:145
  199.5 12.0 %collective-permute-done.37.refs_2_ = bf16[256,1152]{1,0:T(8,128)(2,1)S(1)} collective-permute-done((bf16[256,1152]{1,0:T(8,128)(2,1)S(1)}, bf16[256,1152]{1,0:T(8,128)(2,1)S(1)}, u32[]{:S(2)}, u32[]{:S(2)}) %collective-permute-start.37) | collective-permute-done | bytes 589856 | tf_op jit(solution)/shard_map/ppermute | solution.py:33
  214.3 4.1 collective-permute-done.41.refs_6_
  218.4 4.2 collective-permute-done.42.refs_7_
  226.3 32.1 %shard_map.303 = (bf16[256,1152]{1,0:T(8,128)(2,1)}, bf16[256,1152]{1,0:T(8,128)(2,1)}, bf16[256,1152]{1,0:T(8,128)(2,1)}, bf16[256,1152]{1,0:T(8,128)(2,1)}, bf...) custom-call(s32[2]{0:T(128)} %pad_add_fusion.2.s_ref, ...), custom_call_target="tpu_custom_call" | custom-call | flops 245366784 | bytes 616960 | tf_op jit(solution)/shard_map/pallas_call | solution.py:247
  273.8 5.0 collective-permute-done.50
  283.4 7.6 %convolution_convert_fusion = bf16[768,1152]{1,0:T(8,128)(2,1)S(1)} fusion(bf16[2048,768]{1,0:T(8,128)(2,1)} %get-tuple-element.281, bf16[2048,1152]{1,0:T(8,128)(2,1)} %get-tuple-element.282), kind=kOutput, calls=%fused_computation | convolution fusion | flops 3624763392 | bytes 9633792 | tf_op jit(solution)/shard_map/dot_general | solution.py:225
  299.4 11.3 %shard_map.304 = bf16[32,36,770]{2,1,0:T(8,128)(2,1)} custom-call(s32[1]{0:T(128)} %bitcast.1.s_ref, bf16[2048,1152]{1,0:T(8,128)(2,1)} %get-tuple-element.286.a_r, bf16[2048,896]{1,0:T(8,128)(2,1)} %get-tuple-element.288.b_r), custom_call_target="tpu_custom_call" | custom-call | flops 66060288 | bytes 158792 | tf_op jit(solution)/shard_map/pallas_call | solution.py:247
  322.8 5.0 collective-permute-done.60.refs_6_
  337.3 57.1 %shard_map.305 = (bf16[2048,1152]{1,0:T(8,128)(2,1)}, bf16[2048,384]{1,0:T(8,128)(2,1)}, bf16[2048,128]{1,0:T(8,128)(2,1)}, f32[2048,384]{1,0:T(8,128)}, f32[384...) custom-call(s32[1]{0:T(128)} %bitcast.1.s_ref, ...), custom_call_target="tpu_custom_call" | custom-call | flops 35389440 | bytes 1215688 | tf_op jit(solution)/shard_map/pallas_call | solution.py:247
  403.1 6.3 %fusion.23.gout_r = f32[384,1152]{1,0:T(8,128)} fusion(bf16[2048,384]{1,0:T(8,128)(2,1)} %get-tuple-element.324, bf16[2048,1152]{1,0:T(8,128)(2,1)} %get-tuple-element.325), kind=kOutput, calls=%fused_computation.107 | convolution fusion | flops 1811939328 | bytes 8060928 | tf_op jit(solution)/shard_map/dot_general | solution.py:225
  409.4 8.4 %shard_map.306.gz_r = bf16[32,36,288]{2,1,0:T(8,128)(2,1)} custom-call(s32[1]{0:T(128)} %bitcast.1.s_ref, bf16[2048,1152]{1,0:T(8,128)(2,1)} %get-tuple-element.326.n_r.a_r, bf16[2048,384]{1,0:T(8,128)(2,1)} %get-tuple-element.327.b_r.dz_r), custom_call_target="tpu_custom_call" | custom-call | flops 28311552 | bytes 108672 | tf_op jit(solution)/shard_map/pallas_call | solution.py:247
  423.3 3.5 all-to-all-start.2
  428.8 20.4 %shard_map.307 = (bf16[256,1152]{1,0:T(8,128)(2,1)}, bf16[256,1152]{1,0:T(8,128)(2,1)}, bf16[256,1152]{1,0:T(8,128)(2,1)}, bf16[256,1152]{1,0:T(8,128)(2,1)}, bf...) custom-call(s32[5]{0:T(128)} %concatenate.48.s_ref, ...), custom_call_target="tpu_custom_call" | custom-call | flops 91226112 | bytes 456608 | tf_op jit(solution)/shard_map/pallas_call | solution.py:247
  450.4 3.2 collective-permute-start.83
  456.0 4.7 all-to-all-start.3
  469.4 7.6 %collective-permute-done.81 = bf16[128,1152]{1,0:T(8,128)(2,1)} collective-permute-done((bf16[128,1152]{1,0:T(8,128)(2,1)S(1)}, bf16[128,1152]{1,0:T(8,128)(2,1)}, u32[]{:S(2)}, u32[]{:S(2)}) %collective-permute-start.81) | collective-permute-done | bytes 294944 | tf_op jit(solution)/shard_map/ppermute | solution.py:33
  499.8 6.8 %collective-permute-done.87 = bf16[128,1152]{1,0:T(8,128)(2,1)S(1)} collective-permute-done((bf16[128,1152]{1,0:T(8,128)(2,1)S(1)}, bf16[128,1152]{1,0:T(8,128)(2,1)S(1)}, u32[]{:S(2)}, u32[]{:S(2)}) %collective-permute-start.87) | collective-permute-done | bytes 294944 | tf_op jit(solution)/shard_map/ppermute | solution.py:33
  (494 shorter events, 196.8 us)
Async XLA Ops:
  7.2 19.0 %collective-permute-start = (bf16[256,1152]{1,0:T(8,128)(2,1)}, bf16[256,1152]{1,0:T(8,128)(2,1)}, u32[]{:S(2)}, u32[]{:S(2)}) collective-permute-start(bf16[256,1152]{1,0:T(8,128)(2,1)} %bitcast.87), channel_id=1, source_target_pairs={{0,8},{4,12},{8,0},{12,4},{16,24},{20,28},{24,16},{28,20},{1,9},{5... | collective-permute-start | bytes 1769480 | tf_op jit(solution)/shard_map/ppermute | solution.py:33
  27.3 27.7 %all-to-all-start = ((bf16[32,36,290]{2,1,0:T(8,128)(2,1)}), bf16[32,36,290]{2,1,0:T(8,128)(2,1)S(1)}, u32[]{:S(2)}, u32[]{:S(2)}) async-start(bf16[32,36,290]{2,1,0:T(8,128)(2,1)} %bitcast.12), calls=%async_computation | async-start | bytes 1966080 | tf_op jit(solution)/shard_map/all_to_all | solution.py:196
  31.3 152.5 %all-gather.4.cloned.1.call-start = ((), (), s32[]{:S(2)}) async-start(), calls=%async_computation.6 | async-start | bytes 5898240 | tf_op jit(solution)/shard_map/all_gather | solution.py:966
  36.7 18.7 %collective-permute-start.5 = (bf16[256,1152]{1,0:T(8,128)(2,1)S(1)}, bf16[256,1152]{1,0:T(8,128)(2,1)}, u32[]{:S(2)}, u32[]{:S(2)}) collective-permute-start(bf16[256,1152]{1,0:T(8,128)(2,1)S(1)} %bitcast.90), channel_id=1, source_target_pairs={{0,4},{4,0},{8,12},{12,8},{16,20},{20,16},{24,28},{28,24},{1,5},{5... | collective-permute-start | bytes 1769480 | tf_op jit(solution)/shard_map/ppermute | solution.py:33
  36.7 18.7 %collective-permute-start.6 = (bf16[256,1152]{1,0:T(8,128)(2,1)}, bf16[256,1152]{1,0:T(8,128)(2,1)}, u32[]{:S(2)}, u32[]{:S(2)}) collective-permute-start(bf16[256,1152]{1,0:T(8,128)(2,1)} %collective-permute-done.refs_2_), channel_id=1, source_target_pairs={{0,4},{4,0},{8,12},{12,8},{16,20},{20,16},{24,28},{28,24},{1,5},{5... | collective-permute-start | bytes 1769480 | tf_op jit(solution)/shard_map/ppermute | solution.py:33
  37.2 18.2 %collective-permute-start.7 = (bf16[256,1152]{1,0:T(8,128)(2,1)}, bf16[256,1152]{1,0:T(8,128)(2,1)}, u32[]{:S(2)}, u32[]{:S(2)}) collective-permute-start(bf16[256,1152]{1,0:T(8,128)(2,1)} %collective-permute-done.1.refs_4_), channel_id=1, source_target_pairs={{0,4},{4,0},{8,12},{12,8},{16,20},{20,16},{24,28},{28,24},{1,5},{5... | collective-permute-start | bytes 1769480 | tf_op jit(solution)/shard_map/ppermute | solution.py:33
  63.4 28.4 %collective-permute-start.12 = (bf16[72,1152]{1,0:T(8,128)(2,1)}, bf16[72,1152]{1,0:T(8,128)(2,1)}, u32[]{:S(2)}, u32[]{:S(2)}) collective-permute-start(bf16[72,1152]{1,0:T(8,128)(2,1)} %refs_0_), channel_id=1, source_target_pairs={{0,1},{1,2},{2,3},{3,0},{4,5},{5,6},{6,7},{7,4},{8,9},{9,10},{10,1... | collective-permute-start | bytes 497672 | tf_op jit(solution)/shard_map/ppermute | solution.py:38
  66.6 25.3 %collective-permute-start.13 = (bf16[72,1152]{1,0:T(8,128)(2,1)}, bf16[72,1152]{1,0:T(8,128)(2,1)}, u32[]{:S(2)}, u32[]{:S(2)}) collective-permute-start(bf16[72,1152]{1,0:T(8,128)(2,1)} %refs_0_), channel_id=1, source_target_pairs={{0,2},{1,3},{2,0},{3,1},{4,6},{5,7},{6,4},{7,5},{8,10},{9,11},{10,... | collective-permute-start | bytes 497672 | tf_op jit(solution)/shard_map/ppermute | solution.py:38
  67.2 24.7 %collective-permute-start.14 = (bf16[72,1152]{1,0:T(8,128)(2,1)}, bf16[72,1152]{1,0:T(8,128)(2,1)}, u32[]{:S(2)}, u32[]{:S(2)}) collective-permute-start(bf16[72,1152]{1,0:T(8,128)(2,1)} %refs_0_), channel_id=1, source_target_pairs={{0,3},{1,0},{2,1},{3,2},{4,7},{5,4},{6,5},{7,6},{8,11},{9,8},{10,9... | collective-permute-start | bytes 497672 | tf_op jit(solution)/shard_map/ppermute | solution.py:38
  71.0 20.6 %all-to-all-start.1 = ((bf16[8,36,1058]{2,1,0:T(8,128)(2,1)}), bf16[8,36,1058]{2,1,0:T(8,128)(2,1)S(1)}, u32[]{:S(2)}, u32[]{:S(2)}) async-start(bf16[8,36,1058]{2,1,0:T(8,128)(2,1)} %copy.99), calls=%async_computation.1 | async-start | bytes 1474560 | tf_op jit(solution)/shard_map/all_to_all | solution.py:962
  74.5 151.7 %all-gather.6.cloned.1.call-start = ((), (), s32[]{:S(2)}) async-start(), calls=%async_computation.9 | async-start | bytes 2211840 | tf_op jit(solution)/shard_map/all_gather | solution.py:997
  93.6 20.0 %collective-permute-start.16 = (bf16[1024,128]{1,0:T(8,128)(2,1)S(1)}, bf16[1024,128]{1,0:T(8,128)(2,1)S(1)}, u32[]{:S(2)}, u32[]{:S(2)}) collective-permute-start(bf16[1024,128]{1,0:T(8,128)(2,1)S(1)} %fusion.13), channel_id=1, source_target_pairs={{0,8},{4,12},{8,0},{12,4},{16,24},{20,28},{24,16},{28,20},{1,9},{5... | collective-permute-start | bytes 786440 | tf_op jit(solution)/shard_map/ppermute | solution.py:33
  93.7 20.0 %collective-permute-start.17 = (bf16[1024,128]{1,0:T(8,128)(2,1)S(1)}, bf16[1024,128]{1,0:T(8,128)(2,1)S(1)}, u32[]{:S(2)}, u32[]{:S(2)}) collective-permute-start(bf16[1024,128]{1,0:T(8,128)(2,1)S(1)} %fusion.13), channel_id=1, source_target_pairs={{0,16},{4,20},{8,24},{12,28},{16,0},{20,4},{24,8},{28,12},{1,17},{... | collective-permute-start | bytes 786440 | tf_op jit(solution)/shard_map/ppermute | solution.py:33
  94.8 18.9 %collective-permute-start.18 = (bf16[1024,128]{1,0:T(8,128)(2,1)S(1)}, bf16[1024,128]{1,0:T(8,128)(2,1)S(1)}, u32[]{:S(2)}, u32[]{:S(2)}) collective-permute-start(bf16[1024,128]{1,0:T(8,128)(2,1)S(1)} %fusion.13), channel_id=1, source_target_pairs={{0,24},{4,28},{8,16},{12,20},{16,8},{20,12},{24,0},{28,4},{1,25},{... | collective-permute-start | bytes 786440 | tf_op jit(solution)/shard_map/ppermute | solution.py:33
  116.3 45.2 %collective-permute-start.23 = (bf16[288,770]{1,0:T(8,128)(2,1)S(1)}, bf16[288,770]{1,0:T(8,128)(2,1)S(1)}, u32[]{:S(2)}, u32[]{:S(2)}) collective-permute-start(bf16[288,770]{1,0:T(8,128)(2,1)S(1)} %slice.179.refs_0_), channel_id=1, source_target_pairs={{0,1},{1,2},{2,3},{3,0},{4,5},{5,6},{6,7},{7,4},{8,9},{9,10},{10,1... | collective-permute-start | bytes 1330568 | tf_op jit(solution)/shard_map/ppermute | solution.py:38
  119.5 42.1 %collective-permute-start.24 = (bf16[288,770]{1,0:T(8,128)(2,1)S(1)}, bf16[288,770]{1,0:T(8,128)(2,1)S(1)}, u32[]{:S(2)}, u32[]{:S(2)}) collective-permute-start(bf16[288,770]{1,0:T(8,128)(2,1)S(1)} %slice.179.refs_0_), channel_id=1, source_target_pairs={{0,2},{1,3},{2,0},{3,1},{4,6},{5,7},{6,4},{7,5},{8,10},{9,11},{10,... | collective-permute-start | bytes 1330568 | tf_op jit(solution)/shard_map/ppermute | solution.py:38
  120.3 41.3 %collective-permute-start.25 = (bf16[288,770]{1,0:T(8,128)(2,1)S(1)}, bf16[288,770]{1,0:T(8,128)(2,1)S(1)}, u32[]{:S(2)}, u32[]{:S(2)}) collective-permute-start(bf16[288,770]{1,0:T(8,128)(2,1)S(1)} %slice.179.refs_0_), channel_id=1, source_target_pairs={{0,3},{1,0},{2,1},{3,2},{4,7},{5,4},{6,5},{7,6},{8,11},{9,8},{10,9... | collective-permute-start | bytes 1330568 | tf_op jit(solution)/shard_map/ppermute | solution.py:38
  170.4 24.4 %collective-permute-start.26 = (bf16[256,1152]{1,0:T(8,128)(2,1)}, bf16[256,1152]{1,0:T(8,128)(2,1)S(1)}, u32[]{:S(2)}, u32[]{:S(2)}) collective-permute-start(bf16[256,1152]{1,0:T(8,128)(2,1)} %get-tuple-element.249), channel_id=1, source_target_pairs={{0,4},{4,0},{8,12},{12,8},{16,20},{20,16},{24,28},{28,24},{1,5},{5... | collective-permute-start | bytes 1769480 | tf_op jit(solution)/shard_map/ppermute | solution.py:33
  183.9 239.4 %reduce-scatter.3.cloned.1.call-start = ((), (), s32[]{:S(2)}) async-start(), calls=%async_computation.7 | async-start | bytes 2867200 | tf_op jit(solution)/shard_map/reduce_scatter | solution.py:1030
  199.5 24.3 %collective-permute-start.36 = (bf16[256,1152]{1,0:T(8,128)(2,1)S(1)}, bf16[256,1152]{1,0:T(8,128)(2,1)S(1)}, u32[]{:S(2)}, u32[]{:S(2)}) collective-permute-start(bf16[256,1152]{1,0:T(8,128)(2,1)S(1)} %multiply_convert_fusion.refs_0_), channel_id=1, source_target_pairs={{0,4},{4,0},{8,12},{12,8},{16,20},{20,16},{24,28},{28,24},{1,5},{5... | collective-permute-start | bytes 1769480 | tf_op jit(solution)/shard_map/ppermute | solution.py:33
  270.3 22.1 %collective-permute-start.45 = (bf16[256,1152]{1,0:T(8,128)(2,1)}, bf16[256,1152]{1,0:T(8,128)(2,1)}, u32[]{:S(2)}, u32[]{:S(2)}) collective-permute-start(bf16[256,1152]{1,0:T(8,128)(2,1)} %get-tuple-element.270), channel_id=1, source_target_pairs={{0,4},{4,0},{8,12},{12,8},{16,20},{20,16},{24,28},{28,24},{1,5},{5... | collective-permute-start | bytes 1769480 | tf_op jit(solution)/shard_map/ppermute | solution.py:33
  333.7 135.8 %reduce-scatter.5.cloned.1.call-start = ((), (), s32[]{:S(2)}) async-start(), calls=%async_computation.8 | async-start | bytes 2211840 | tf_op jit(solution)/shard_map/reduce_scatter | solution.py:1015
  333.7 60.7 %collective-permute-start.68 = (bf16[256,1152]{1,0:T(8,128)(2,1)}, bf16[256,1152]{1,0:T(8,128)(2,1)S(1)}, u32[]{:S(2)}, u32[]{:S(2)}) collective-permute-start(bf16[256,1152]{1,0:T(8,128)(2,1)} %add_convert_fusion.4), channel_id=1, source_target_pairs={{0,8},{4,12},{8,0},{12,4},{16,24},{20,28},{24,16},{28,20},{1,9},{5... | collective-permute-start | bytes 1769480 | tf_op jit(solution)/shard_map/ppermute | solution.py:33
  335.1 59.3 %collective-permute-start.69 = (bf16[256,1152]{1,0:T(8,128)(2,1)}, bf16[256,1152]{1,0:T(8,128)(2,1)}, u32[]{:S(2)}, u32[]{:S(2)}) collective-permute-start(bf16[256,1152]{1,0:T(8,128)(2,1)} %add_convert_fusion.3), channel_id=1, source_target_pairs={{0,16},{4,20},{8,24},{12,28},{16,0},{20,4},{24,8},{28,12},{1,17},{... | collective-permute-start | bytes 1769480 | tf_op jit(solution)/shard_map/ppermute | solution.py:33
  335.7 58.8 %collective-permute-start.70 = (bf16[256,1152]{1,0:T(8,128)(2,1)}, bf16[256,1152]{1,0:T(8,128)(2,1)}, u32[]{:S(2)}, u32[]{:S(2)}) collective-permute-start(bf16[256,1152]{1,0:T(8,128)(2,1)} %add_convert_fusion.2), channel_id=1, source_target_pairs={{0,24},{4,28},{8,16},{12,20},{16,8},{20,12},{24,0},{28,4},{1,25},{... | collective-permute-start | bytes 1769480 | tf_op jit(solution)/shard_map/ppermute | solution.py:33
  399.6 18.2 %collective-permute-start.72 = (bf16[1024,128]{1,0:T(8,128)(2,1)}, bf16[1024,128]{1,0:T(8,128)(2,1)S(1)}, u32[]{:S(2)}, u32[]{:S(2)}) collective-permute-start(bf16[1024,128]{1,0:T(8,128)(2,1)} %fusion.14), channel_id=1, source_target_pairs={{0,8},{4,12},{8,0},{12,4},{16,24},{20,28},{24,16},{28,20},{1,9},{5... | collective-permute-start | bytes 786440 | tf_op jit(solution)/shard_map/ppermute | solution.py:33
  400.5 18.0 %collective-permute-start.74 = (bf16[1024,128]{1,0:T(8,128)(2,1)}, bf16[1024,128]{1,0:T(8,128)(2,1)}, u32[]{:S(2)}, u32[]{:S(2)}) collective-permute-start(bf16[1024,128]{1,0:T(8,128)(2,1)} %fusion.14), channel_id=1, source_target_pairs={{0,24},{4,28},{8,16},{12,20},{16,8},{20,12},{24,0},{28,4},{1,25},{... | collective-permute-start | bytes 786440 | tf_op jit(solution)/shard_map/ppermute | solution.py:33
  423.3 25.9 %all-to-all-start.2 = ((bf16[8,36,770]{2,1,0:T(8,128)(2,1)}), bf16[8,36,770]{2,1,0:T(8,128)(2,1)S(1)}, u32[]{:S(2)}, u32[]{:S(2)}) async-start(bf16[8,36,770]{2,1,0:T(8,128)(2,1)} %bitcast.108), calls=%async_computation.3 | async-start | bytes 1146880 | tf_op jit(solution)/shard_map/all_to_all | solution.py:1057
  450.4 43.4 %collective-permute-start.83 = (bf16[72,1408]{1,0:T(8,128)(2,1)}, bf16[72,1408]{1,0:T(8,128)(2,1)S(1)}, u32[]{:S(2)}, u32[]{:S(2)}) collective-permute-start(bf16[72,1408]{1,0:T(8,128)(2,1)} %get-tuple-element.369), channel_id=1, source_target_pairs={{0,1},{1,2},{2,3},{3,0},{4,5},{5,6},{6,7},{7,4},{8,9},{9,10},{10,1... | collective-permute-start | bytes 608264 | tf_op jit(solution)/shard_map/ppermute | solution.py:38
  453.6 40.2 %collective-permute-start.84 = (bf16[72,1408]{1,0:T(8,128)(2,1)}, bf16[72,1408]{1,0:T(8,128)(2,1)}, u32[]{:S(2)}, u32[]{:S(2)}) collective-permute-start(bf16[72,1408]{1,0:T(8,128)(2,1)} %get-tuple-element.370), channel_id=1, source_target_pairs={{0,2},{1,3},{2,0},{3,1},{4,6},{5,7},{6,4},{7,5},{8,10},{9,11},{10,... | collective-permute-start | bytes 608264 | tf_op jit(solution)/shard_map/ppermute | solution.py:38
  455.6 38.4 %collective-permute-start.85 = (bf16[72,1408]{1,0:T(8,128)(2,1)}, bf16[72,1408]{1,0:T(8,128)(2,1)}, u32[]{:S(2)}, u32[]{:S(2)}) collective-permute-start(bf16[72,1408]{1,0:T(8,128)(2,1)} %get-tuple-element.371), channel_id=1, source_target_pairs={{0,3},{1,0},{2,1},{3,2},{4,7},{5,4},{6,5},{7,6},{8,11},{9,8},{10,9... | collective-permute-start | bytes 608264 | tf_op jit(solution)/shard_map/ppermute | solution.py:38
  456.0 53.9 %all-to-all-start.3 = ((bf16[32,36,576]{2,1,0:T(8,128)(2,1)}), bf16[32,36,576]{2,1,0:T(8,128)(2,1)}, u32[]{:S(2)}, u32[]{:S(2)}) async-start(bf16[32,36,576]{2,1,0:T(8,128)(2,1)} %get-tuple-element.377), calls=%async_computation.5 | async-start | bytes 3276800 | tf_op jit(solution)/shard_map/all_to_all | solution.py:196
  (156 other events, 1120.9 us)
Sparse Core Ops, SparseCore 0:
  55.6 48.5 all-gather.3
  184.0 40.8 all-gather.5
  333.8 48.2 reduce-scatter.2
  419.9 41.2 reduce-scatter.4

commit v6 on v5

--- a/solution.py
+++ b/solution.py
@@ -775,7 +775,8 @@
         def _():
             for k in range(blocks * count):
                 x = gx[k * group : (k + 1) * group, :chans]
-                gx_o[k] = jnp.concatenate([x, gz_r[k].astype(f32)], axis=1).astype(bf16)
+                z = gz_r[k * group : (k + 1) * group, :chans]
+                gx_o[k] = jnp.concatenate([x, z], axis=1).astype(bf16)
             tall = jnp.concatenate(
                 [jnp.zeros((DT_RANK, wid), f32), flat[...], jnp.zeros((LANES - DT_RANK - FLAT, wid), f32)], axis=0
             )
@@ -1045,7 +1046,7 @@
 
     def meanwhile(low):
         grad_out = t_mm(after(gated, low), d_mix_all)
-        return grad_out, row_grad(flip[None], after(normed, low), d_z, chans, d_rows, False)
+        return grad_out, t_mm(after(normed, low), d_z)
 
     d_sel, (grad_out, grad_z) = reduce_wide(d_sel_part, meanwhile)
     z = lax.axis_index("narrow")

time: 535 us -> 530 us (level)
  Pallas kernels: 194 us -> 185 us
    pallas_call x7 -> x6, Pallas kernels: 174 us -> 165 us  [call(): pl.pallas_call(kernel, grid_spec=pltpu.PrefetchScalarGridSpec(num_scalar_...]
    dot_general x2 -> x3, matrix products: 13.9 us -> 17.9 us  [t_mm(): lax.dot_general(a, b, (((0,), (0,)), ((), ())), preferred_element_type=f32)]
    unnamed x191 -> x195, local copies, waits for them, and re-layouts: 18.3 us -> 17.7 us
  transfers between devices with their start and end apart: 97 -> 97, of which waited for: 34 -> 35; matrix products, arithmetic and copies ran while one was open for 17% -> 18% of each run, Pallas kernels for 30% -> 29%
where the time goes in v6:
time: 530 us; the launch traced here: 521 us
  Pallas kernels  185 us (35%)
  waiting for transfers between devices  111 us (21%)
  starting transfers between devices  92 us (17%)
  local copies, waits for them, and re-layouts  52.4 us (10%)
  other arithmetic  45.6 us (9%)
  matrix products  17.9 us (3%)
  between operations  16.4 us (3%)
    pallas_call x6, Pallas kernels, call(): pl.pallas_call(kernel, grid_spec=pltpu.PrefetchScalarGridSpec(num_scalar_...  165 us
    ppermute x74, waiting for transfers between devices, swap(): return lax.ppermute(x, 'wide', [(i, i ^ k) for i in range(n)])  88 us
    ppermute x74, starting transfers between devices, swap(): return lax.ppermute(x, 'wide', [(i, i ^ k) for i in range(n)])  52.9 us
    ppermute x15, starting transfers between devices, turn(): return lax.ppermute(x, 'narrow', [(i, (i + k) % n) for i in range(n)])  22.9 us
    dot_general x3, matrix products, t_mm(): lax.dot_general(a, b, (((0,), (0,)), ((), ())), preferred_element_type=f32)  17.9 us
    unnamed x195, local copies, waits for them, and re-layouts  17.7 us
    ppermute x15, waiting for transfers between devices, turn(): return lax.ppermute(x, 'narrow', [(i, (i + k) % n) for i in range(n)])  13.3 us
    pallas_call x2, Pallas kernels, ordered_rows(): pl.pallas_call(kernel, in_specs=[pl.BlockSpec(memory_space=pltpu.SMEM)] +...  12.2 us
  transfers between devices with their start and end apart: 97, of which 35 were waited for; matrix products, arithmetic and copies ran while one was open for 18% of the time, Pallas kernels for 29%

profile of v6, /device:TPU:0, one launch (start us, length us, event | category | flops | bytes accessed | tf_op | source)
XLA Modules:
  0.0 520.9 jit_solution(14491469078696156929)
XLA Ops:
  27.3 4.0 all-to-all-start
  37.2 11.3 %collective-permute-done.8.refs_6_ = bf16[128,1152]{1,0:T(8,128)(2,1)} collective-permute-done((bf16[128,1152]{1,0:T(8,128)(2,1)S(1)}, bf16[128,1152]{1,0:T(8,128)(2,1)}, u32[]{:S(2)}, u32[]{:S(2)}) %collective-permute-start.8) | collective-permute-done | bytes 294944 | tf_op jit(solution)/shard_map/ppermute | solution.py:33
  50.2 4.9 all-to-all-done
  71.0 3.5 all-to-all-start.1
  75.2 11.7 %shard_map.298 = (bf16[2048,1152]{1,0:T(8,128)(2,1)}, f32[2048,384]{1,0:T(8,128)}, f32[2048,384]{1,0:T(8,128)}, bf16[2048,384]{1,0:T(8,128)(2,1)}, bf16[2048,128]{1,0:T(8,128)(2,1)}) custom-call(s32[1]{0:T(128)} %bitcast.1.s_ref, bf16[256,1152]{1,0:T(8,128)(2,1)} %bitcast.91, bf16[256,1152]{1,0:T(8,128)(2,1)} %collective-permute-done.5.refs_1_, ...), custom_call_target="tpu_custom_call" | custom-call | flops 31457280 | bytes 294080 | tf_op jit(solution)/shard_map/pallas_call | solution.py:247
  86.9 4.7 all-to-all-done.1
  97.2 5.2 collective-permute-done.19.refs_1_
  102.3 3.2 shard_map.299.wout.refs_10_
  105.5 5.9 %collective-permute-done.20.refs_2_ = bf16[288,288]{1,0:T(8,128)(2,1)S(1)} collective-permute-done((bf16[288,288]{1,0:T(8,128)(2,1)S(1)}, bf16[288,288]{1,0:T(8,128)(2,1)S(1)}, u32[]{:S(2)}, u32[]{:S(2)}) %collective-permute-start.20) | collective-permute-done | bytes 165920 | tf_op jit(solution)/shard_map/ppermute | solution.py:38
  116.3 3.1 collective-permute-start.23
  124.3 4.5 shard_map.300.wz
  128.8 32.7 %shard_map.301 = (f32[2048,384]{1,0:T(8,128)}, f32[2048,384]{1,0:T(8,128)}, f32[2048,16,384]{2,1,0:T(8,128)}, f32[16,384]{1,0:T(8,128)}, f32[2048,384]{1,0:T(8,1...) custom-call(s32[1]{0:T(128)} %bitcast.1.s_ref, ...), custom_call_target="tpu_custom_call" | custom-call | flops 61341696 | bytes 1168688 | tf_op jit(solution)/shard_map/pallas_call | solution.py:247
  170.4 5.3 %collective-permute-done.28 = bf16[128,1152]{1,0:T(8,128)(2,1)S(1)} collective-permute-done((bf16[128,1152]{1,0:T(8,128)(2,1)S(1)}, bf16[128,1152]{1,0:T(8,128)(2,1)S(1)}, u32[]{:S(2)}, u32[]{:S(2)}) %collective-permute-start.28) | collective-permute-done | bytes 294944 | tf_op jit(solution)/shard_map/ppermute | solution.py:33
  175.8 5.4 %collective-permute-done.31 = bf16[128,1152]{1,0:T(8,128)(2,1)S(1)} collective-permute-done((bf16[128,1152]{1,0:T(8,128)(2,1)S(1)}, bf16[128,1152]{1,0:T(8,128)(2,1)S(1)}, u32[]{:S(2)}, u32[]{:S(2)}) %collective-permute-start.31) | collective-permute-done | bytes 294944 | tf_op jit(solution)/shard_map/ppermute | solution.py:33
  186.4 7.7 %shard_map.302.refs_11_ = bf16[1152,896]{1,0:T(8,128)(2,1)} custom-call(s32[4]{0:T(128)} %pad_add_fusion.1.order_ref, bf16[288,770]{1,0:T(8,128)(2,1)} %copy-done.14, bf16[288,770]{1,0:T(8,128)(2,1)} %copy-done.46, bf16[288,770]{1,0:T(8,128)(2,1)} %copy-done.47, bf16[288,770]{1,0:T(8,128)(2,1)} %copy-done.48), custom_call_target="tpu_custom_call" | custom-call | tf_op jit(solution)/shard_map/pallas_call | solution.py:145
  199.6 12.0 %collective-permute-done.37.refs_2_ = bf16[256,1152]{1,0:T(8,128)(2,1)S(1)} collective-permute-done((bf16[256,1152]{1,0:T(8,128)(2,1)S(1)}, bf16[256,1152]{1,0:T(8,128)(2,1)S(1)}, u32[]{:S(2)}, u32[]{:S(2)}) %collective-permute-start.37) | collective-permute-done | bytes 589856 | tf_op jit(solution)/shard_map/ppermute | solution.py:33
  214.3 4.1 collective-permute-done.41.refs_6_
  218.4 4.2 collective-permute-done.42.refs_7_
  226.3 32.1 %shard_map.303 = (bf16[256,1152]{1,0:T(8,128)(2,1)}, bf16[256,1152]{1,0:T(8,128)(2,1)}, bf16[256,1152]{1,0:T(8,128)(2,1)}, bf16[256,1152]{1,0:T(8,128)(2,1)}, bf...) custom-call(s32[2]{0:T(128)} %pad_add_fusion.2.s_ref, ...), custom_call_target="tpu_custom_call" | custom-call | flops 245366784 | bytes 616960 | tf_op jit(solution)/shard_map/pallas_call | solution.py:247
  273.8 5.1 collective-permute-done.50
  283.5 7.6 %convolution_convert_fusion = bf16[768,1152]{1,0:T(8,128)(2,1)S(1)} fusion(bf16[2048,768]{1,0:T(8,128)(2,1)} %get-tuple-element.281, bf16[2048,1152]{1,0:T(8,128)(2,1)} %get-tuple-element.282), kind=kOutput, calls=%fused_computation | convolution fusion | flops 3624763392 | bytes 9633792 | tf_op jit(solution)/shard_map/dot_general | solution.py:225
  299.4 11.3 %shard_map.304 = bf16[32,36,770]{2,1,0:T(8,128)(2,1)} custom-call(s32[1]{0:T(128)} %bitcast.1.s_ref, bf16[2048,1152]{1,0:T(8,128)(2,1)} %get-tuple-element.286.a_r, bf16[2048,896]{1,0:T(8,128)(2,1)} %get-tuple-element.288.b_r), custom_call_target="tpu_custom_call" | custom-call | flops 66060288 | bytes 158792 | tf_op jit(solution)/shard_map/pallas_call | solution.py:247
  322.8 5.0 collective-permute-done.60.refs_6_
  337.4 57.2 %shard_map.305 = (bf16[2048,1152]{1,0:T(8,128)(2,1)}, bf16[2048,384]{1,0:T(8,128)(2,1)}, bf16[2048,128]{1,0:T(8,128)(2,1)}, f32[2048,384]{1,0:T(8,128)}, f32[384...) custom-call(s32[1]{0:T(128)} %bitcast.1.s_ref, ...), custom_call_target="tpu_custom_call" | custom-call | flops 35389440 | bytes 1215688 | tf_op jit(solution)/shard_map/pallas_call | solution.py:247
  402.7 6.9 %fusion.24.gz_r = f32[1152,384]{1,0:T(8,128)} fusion(bf16[2048,1152]{1,0:T(8,128)(2,1)} %get-tuple-element.326.n_r, bf16[2048,384]{1,0:T(8,128)(2,1)} %get-tuple-element.327.dz_r), kind=kOutput, calls=%fused_computation.108 | convolution fusion | flops 1811939328 | bytes 8060928 | tf_op jit(solution)/shard_map/dot_general | solution.py:225
  409.6 3.5 fusion.23.gout_r
  418.3 3.8 all-to-all-start.2
  424.0 20.5 %shard_map.306 = (bf16[256,1152]{1,0:T(8,128)(2,1)}, bf16[256,1152]{1,0:T(8,128)(2,1)}, bf16[256,1152]{1,0:T(8,128)(2,1)}, bf16[256,1152]{1,0:T(8,128)(2,1)}, bf...) custom-call(s32[5]{0:T(128)} %concatenate.48.s_ref, ...), custom_call_target="tpu_custom_call" | custom-call | flops 91226112 | bytes 473888 | tf_op jit(solution)/shard_map/pallas_call | solution.py:247
  445.8 3.4 collective-permute-start.83
  451.5 4.7 all-to-all-start.3
  465.0 8.4 %collective-permute-done.81 = bf16[128,1152]{1,0:T(8,128)(2,1)} collective-permute-done((bf16[128,1152]{1,0:T(8,128)(2,1)S(1)}, bf16[128,1152]{1,0:T(8,128)(2,1)}, u32[]{:S(2)}, u32[]{:S(2)}) %collective-permute-start.81) | collective-permute-done | bytes 294944 | tf_op jit(solution)/shard_map/ppermute | solution.py:33
  496.9 5.6 %collective-permute-done.87 = bf16[128,1152]{1,0:T(8,128)(2,1)S(1)} collective-permute-done((bf16[128,1152]{1,0:T(8,128)(2,1)S(1)}, bf16[128,1152]{1,0:T(8,128)(2,1)S(1)}, u32[]{:S(2)}, u32[]{:S(2)}) %collective-permute-start.87) | collective-permute-done | bytes 294944 | tf_op jit(solution)/shard_map/ppermute | solution.py:33
  (499 shorter events, 196.0 us)
Async XLA Ops:
  7.2 19.0 %collective-permute-start = (bf16[256,1152]{1,0:T(8,128)(2,1)}, bf16[256,1152]{1,0:T(8,128)(2,1)}, u32[]{:S(2)}, u32[]{:S(2)}) collective-permute-start(bf16[256,1152]{1,0:T(8,128)(2,1)} %bitcast.89), channel_id=1, source_target_pairs={{0,8},{4,12},{8,0},{12,4},{16,24},{20,28},{24,16},{28,20},{1,9},{5... | collective-permute-start | bytes 1769480 | tf_op jit(solution)/shard_map/ppermute | solution.py:33
  27.3 27.7 %all-to-all-start = ((bf16[32,36,290]{2,1,0:T(8,128)(2,1)}), bf16[32,36,290]{2,1,0:T(8,128)(2,1)S(1)}, u32[]{:S(2)}, u32[]{:S(2)}) async-start(bf16[32,36,290]{2,1,0:T(8,128)(2,1)} %bitcast.12), calls=%async_computation | async-start | bytes 1966080 | tf_op jit(solution)/shard_map/all_to_all | solution.py:196
  31.3 152.5 %all-gather.4.cloned.1.call-start = ((), (), s32[]{:S(2)}) async-start(), calls=%async_computation.6 | async-start | bytes 5898240 | tf_op jit(solution)/shard_map/all_gather | solution.py:967
  36.7 18.7 %collective-permute-start.5 = (bf16[256,1152]{1,0:T(8,128)(2,1)S(1)}, bf16[256,1152]{1,0:T(8,128)(2,1)}, u32[]{:S(2)}, u32[]{:S(2)}) collective-permute-start(bf16[256,1152]{1,0:T(8,128)(2,1)S(1)} %bitcast.92), channel_id=1, source_target_pairs={{0,4},{4,0},{8,12},{12,8},{16,20},{20,16},{24,28},{28,24},{1,5},{5... | collective-permute-start | bytes 1769480 | tf_op jit(solution)/shard_map/ppermute | solution.py:33
  36.7 18.7 %collective-permute-start.6 = (bf16[256,1152]{1,0:T(8,128)(2,1)}, bf16[256,1152]{1,0:T(8,128)(2,1)}, u32[]{:S(2)}, u32[]{:S(2)}) collective-permute-start(bf16[256,1152]{1,0:T(8,128)(2,1)} %collective-permute-done.refs_2_), channel_id=1, source_target_pairs={{0,4},{4,0},{8,12},{12,8},{16,20},{20,16},{24,28},{28,24},{1,5},{5... | collective-permute-start | bytes 1769480 | tf_op jit(solution)/shard_map/ppermute | solution.py:33
  37.2 18.2 %collective-permute-start.7 = (bf16[256,1152]{1,0:T(8,128)(2,1)}, bf16[256,1152]{1,0:T(8,128)(2,1)}, u32[]{:S(2)}, u32[]{:S(2)}) collective-permute-start(bf16[256,1152]{1,0:T(8,128)(2,1)} %collective-permute-done.1.refs_4_), channel_id=1, source_target_pairs={{0,4},{4,0},{8,12},{12,8},{16,20},{20,16},{24,28},{28,24},{1,5},{5... | collective-permute-start | bytes 1769480 | tf_op jit(solution)/shard_map/ppermute | solution.py:33
  63.4 28.4 %collective-permute-start.12 = (bf16[72,1152]{1,0:T(8,128)(2,1)}, bf16[72,1152]{1,0:T(8,128)(2,1)}, u32[]{:S(2)}, u32[]{:S(2)}) collective-permute-start(bf16[72,1152]{1,0:T(8,128)(2,1)} %refs_0_), channel_id=1, source_target_pairs={{0,1},{1,2},{2,3},{3,0},{4,5},{5,6},{6,7},{7,4},{8,9},{9,10},{10,1... | collective-permute-start | bytes 497672 | tf_op jit(solution)/shard_map/ppermute | solution.py:38
  66.6 25.3 %collective-permute-start.13 = (bf16[72,1152]{1,0:T(8,128)(2,1)}, bf16[72,1152]{1,0:T(8,128)(2,1)}, u32[]{:S(2)}, u32[]{:S(2)}) collective-permute-start(bf16[72,1152]{1,0:T(8,128)(2,1)} %refs_0_), channel_id=1, source_target_pairs={{0,2},{1,3},{2,0},{3,1},{4,6},{5,7},{6,4},{7,5},{8,10},{9,11},{10,... | collective-permute-start | bytes 497672 | tf_op jit(solution)/shard_map/ppermute | solution.py:38
  67.2 24.7 %collective-permute-start.14 = (bf16[72,1152]{1,0:T(8,128)(2,1)}, bf16[72,1152]{1,0:T(8,128)(2,1)}, u32[]{:S(2)}, u32[]{:S(2)}) collective-permute-start(bf16[72,1152]{1,0:T(8,128)(2,1)} %refs_0_), channel_id=1, source_target_pairs={{0,3},{1,0},{2,1},{3,2},{4,7},{5,4},{6,5},{7,6},{8,11},{9,8},{10,9... | collective-permute-start | bytes 497672 | tf_op jit(solution)/shard_map/ppermute | solution.py:38
  71.0 20.6 %all-to-all-start.1 = ((bf16[8,36,1058]{2,1,0:T(8,128)(2,1)}), bf16[8,36,1058]{2,1,0:T(8,128)(2,1)S(1)}, u32[]{:S(2)}, u32[]{:S(2)}) async-start(bf16[8,36,1058]{2,1,0:T(8,128)(2,1)} %copy.99), calls=%async_computation.1 | async-start | bytes 1474560 | tf_op jit(solution)/shard_map/all_to_all | solution.py:963
  74.5 151.8 %all-gather.6.cloned.1.call-start = ((), (), s32[]{:S(2)}) async-start(), calls=%async_computation.9 | async-start | bytes 2211840 | tf_op jit(solution)/shard_map/all_gather | solution.py:998
  93.6 20.0 %collective-permute-start.16 = (bf16[1024,128]{1,0:T(8,128)(2,1)S(1)}, bf16[1024,128]{1,0:T(8,128)(2,1)S(1)}, u32[]{:S(2)}, u32[]{:S(2)}) collective-permute-start(bf16[1024,128]{1,0:T(8,128)(2,1)S(1)} %fusion.13), channel_id=1, source_target_pairs={{0,8},{4,12},{8,0},{12,4},{16,24},{20,28},{24,16},{28,20},{1,9},{5... | collective-permute-start | bytes 786440 | tf_op jit(solution)/shard_map/ppermute | solution.py:33
  93.7 20.0 %collective-permute-start.17 = (bf16[1024,128]{1,0:T(8,128)(2,1)S(1)}, bf16[1024,128]{1,0:T(8,128)(2,1)S(1)}, u32[]{:S(2)}, u32[]{:S(2)}) collective-permute-start(bf16[1024,128]{1,0:T(8,128)(2,1)S(1)} %fusion.13), channel_id=1, source_target_pairs={{0,16},{4,20},{8,24},{12,28},{16,0},{20,4},{24,8},{28,12},{1,17},{... | collective-permute-start | bytes 786440 | tf_op jit(solution)/shard_map/ppermute | solution.py:33
  94.8 18.9 %collective-permute-start.18 = (bf16[1024,128]{1,0:T(8,128)(2,1)S(1)}, bf16[1024,128]{1,0:T(8,128)(2,1)S(1)}, u32[]{:S(2)}, u32[]{:S(2)}) collective-permute-start(bf16[1024,128]{1,0:T(8,128)(2,1)S(1)} %fusion.13), channel_id=1, source_target_pairs={{0,24},{4,28},{8,16},{12,20},{16,8},{20,12},{24,0},{28,4},{1,25},{... | collective-permute-start | bytes 786440 | tf_op jit(solution)/shard_map/ppermute | solution.py:33
  116.3 45.2 %collective-permute-start.23 = (bf16[288,770]{1,0:T(8,128)(2,1)S(1)}, bf16[288,770]{1,0:T(8,128)(2,1)S(1)}, u32[]{:S(2)}, u32[]{:S(2)}) collective-permute-start(bf16[288,770]{1,0:T(8,128)(2,1)S(1)} %slice.179.refs_0_), channel_id=1, source_target_pairs={{0,1},{1,2},{2,3},{3,0},{4,5},{5,6},{6,7},{7,4},{8,9},{9,10},{10,1... | collective-permute-start | bytes 1330568 | tf_op jit(solution)/shard_map/ppermute | solution.py:38
  119.5 42.1 %collective-permute-start.24 = (bf16[288,770]{1,0:T(8,128)(2,1)S(1)}, bf16[288,770]{1,0:T(8,128)(2,1)S(1)}, u32[]{:S(2)}, u32[]{:S(2)}) collective-permute-start(bf16[288,770]{1,0:T(8,128)(2,1)S(1)} %slice.179.refs_0_), channel_id=1, source_target_pairs={{0,2},{1,3},{2,0},{3,1},{4,6},{5,7},{6,4},{7,5},{8,10},{9,11},{10,... | collective-permute-start | bytes 1330568 | tf_op jit(solution)/shard_map/ppermute | solution.py:38
  120.3 41.3 %collective-permute-start.25 = (bf16[288,770]{1,0:T(8,128)(2,1)S(1)}, bf16[288,770]{1,0:T(8,128)(2,1)S(1)}, u32[]{:S(2)}, u32[]{:S(2)}) collective-permute-start(bf16[288,770]{1,0:T(8,128)(2,1)S(1)} %slice.179.refs_0_), channel_id=1, source_target_pairs={{0,3},{1,0},{2,1},{3,2},{4,7},{5,4},{6,5},{7,6},{8,11},{9,8},{10,9... | collective-permute-start | bytes 1330568 | tf_op jit(solution)/shard_map/ppermute | solution.py:38
  170.4 24.4 %collective-permute-start.26 = (bf16[256,1152]{1,0:T(8,128)(2,1)}, bf16[256,1152]{1,0:T(8,128)(2,1)S(1)}, u32[]{:S(2)}, u32[]{:S(2)}) collective-permute-start(bf16[256,1152]{1,0:T(8,128)(2,1)} %get-tuple-element.249), channel_id=1, source_target_pairs={{0,4},{4,0},{8,12},{12,8},{16,20},{20,16},{24,28},{28,24},{1,5},{5... | collective-permute-start | bytes 1769480 | tf_op jit(solution)/shard_map/ppermute | solution.py:33
  183.9 234.4 %reduce-scatter.3.cloned.1.call-start = ((), (), s32[]{:S(2)}) async-start(), calls=%async_computation.7 | async-start | bytes 2867200 | tf_op jit(solution)/shard_map/reduce_scatter | solution.py:1031
  199.6 24.3 %collective-permute-start.36 = (bf16[256,1152]{1,0:T(8,128)(2,1)S(1)}, bf16[256,1152]{1,0:T(8,128)(2,1)S(1)}, u32[]{:S(2)}, u32[]{:S(2)}) collective-permute-start(bf16[256,1152]{1,0:T(8,128)(2,1)S(1)} %multiply_convert_fusion.refs_0_), channel_id=1, source_target_pairs={{0,4},{4,0},{8,12},{12,8},{16,20},{20,16},{24,28},{28,24},{1,5},{5... | collective-permute-start | bytes 1769480 | tf_op jit(solution)/shard_map/ppermute | solution.py:33
  270.4 22.1 %collective-permute-start.45 = (bf16[256,1152]{1,0:T(8,128)(2,1)}, bf16[256,1152]{1,0:T(8,128)(2,1)}, u32[]{:S(2)}, u32[]{:S(2)}) collective-permute-start(bf16[256,1152]{1,0:T(8,128)(2,1)} %get-tuple-element.270), channel_id=1, source_target_pairs={{0,4},{4,0},{8,12},{12,8},{16,20},{20,16},{24,28},{28,24},{1,5},{5... | collective-permute-start | bytes 1769480 | tf_op jit(solution)/shard_map/ppermute | solution.py:33
  313.1 16.7 %collective-permute-start.58 = (bf16[256,1152]{1,0:T(8,128)(2,1)S(1)}, bf16[256,1152]{1,0:T(8,128)(2,1)S(1)}, u32[]{:S(2)}, u32[]{:S(2)}) collective-permute-start(bf16[256,1152]{1,0:T(8,128)(2,1)S(1)} %collective-permute-done.56.refs_2_), channel_id=1, source_target_pairs={{0,4},{4,0},{8,12},{12,8},{16,20},{20,16},{24,28},{28,24},{1,5},{5... | collective-permute-start | bytes 1769480 | tf_op jit(solution)/shard_map/ppermute | solution.py:33
  313.6 17.0 %collective-permute-start.59 = (bf16[256,1152]{1,0:T(8,128)(2,1)}, bf16[256,1152]{1,0:T(8,128)(2,1)S(1)}, u32[]{:S(2)}, u32[]{:S(2)}) collective-permute-start(bf16[256,1152]{1,0:T(8,128)(2,1)} %collective-permute-done.57.refs_4_), channel_id=1, source_target_pairs={{0,4},{4,0},{8,12},{12,8},{16,20},{20,16},{24,28},{28,24},{1,5},{5... | collective-permute-start | bytes 1769480 | tf_op jit(solution)/shard_map/ppermute | solution.py:33
  333.7 131.3 %reduce-scatter.5.cloned.1.call-start = ((), (), s32[]{:S(2)}) async-start(), calls=%async_computation.8 | async-start | bytes 2211840 | tf_op jit(solution)/shard_map/reduce_scatter | solution.py:1016
  333.8 60.7 %collective-permute-start.68 = (bf16[256,1152]{1,0:T(8,128)(2,1)}, bf16[256,1152]{1,0:T(8,128)(2,1)S(1)}, u32[]{:S(2)}, u32[]{:S(2)}) collective-permute-start(bf16[256,1152]{1,0:T(8,128)(2,1)} %add_convert_fusion.4), channel_id=1, source_target_pairs={{0,8},{4,12},{8,0},{12,4},{16,24},{20,28},{24,16},{28,20},{1,9},{5... | collective-permute-start | bytes 1769480 | tf_op jit(solution)/shard_map/ppermute | solution.py:33
  335.2 59.3 %collective-permute-start.69 = (bf16[256,1152]{1,0:T(8,128)(2,1)}, bf16[256,1152]{1,0:T(8,128)(2,1)}, u32[]{:S(2)}, u32[]{:S(2)}) collective-permute-start(bf16[256,1152]{1,0:T(8,128)(2,1)} %add_convert_fusion.3), channel_id=1, source_target_pairs={{0,16},{4,20},{8,24},{12,28},{16,0},{20,4},{24,8},{28,12},{1,17},{... | collective-permute-start | bytes 1769480 | tf_op jit(solution)/shard_map/ppermute | solution.py:33
  335.8 58.7 %collective-permute-start.70 = (bf16[256,1152]{1,0:T(8,128)(2,1)}, bf16[256,1152]{1,0:T(8,128)(2,1)}, u32[]{:S(2)}, u32[]{:S(2)}) collective-permute-start(bf16[256,1152]{1,0:T(8,128)(2,1)} %add_convert_fusion.2), channel_id=1, source_target_pairs={{0,24},{4,28},{8,16},{12,20},{16,8},{20,12},{24,0},{28,4},{1,25},{... | collective-permute-start | bytes 1769480 | tf_op jit(solution)/shard_map/ppermute | solution.py:33
  418.3 26.3 %all-to-all-start.2 = ((bf16[8,36,770]{2,1,0:T(8,128)(2,1)}), bf16[8,36,770]{2,1,0:T(8,128)(2,1)S(1)}, u32[]{:S(2)}, u32[]{:S(2)}) async-start(bf16[8,36,770]{2,1,0:T(8,128)(2,1)} %bitcast.110), calls=%async_computation.3 | async-start | bytes 1146880 | tf_op jit(solution)/shard_map/all_to_all | solution.py:1058
  445.8 43.9 %collective-permute-start.83 = (bf16[72,1408]{1,0:T(8,128)(2,1)}, bf16[72,1408]{1,0:T(8,128)(2,1)S(1)}, u32[]{:S(2)}, u32[]{:S(2)}) collective-permute-start(bf16[72,1408]{1,0:T(8,128)(2,1)} %get-tuple-element.369), channel_id=1, source_target_pairs={{0,1},{1,2},{2,3},{3,0},{4,5},{5,6},{6,7},{7,4},{8,9},{9,10},{10,1... | collective-permute-start | bytes 608264 | tf_op jit(solution)/shard_map/ppermute | solution.py:38
  449.2 40.5 %collective-permute-start.84 = (bf16[72,1408]{1,0:T(8,128)(2,1)}, bf16[72,1408]{1,0:T(8,128)(2,1)}, u32[]{:S(2)}, u32[]{:S(2)}) collective-permute-start(bf16[72,1408]{1,0:T(8,128)(2,1)} %get-tuple-element.370), channel_id=1, source_target_pairs={{0,2},{1,3},{2,0},{3,1},{4,6},{5,7},{6,4},{7,5},{8,10},{9,11},{10,... | collective-permute-start | bytes 608264 | tf_op jit(solution)/shard_map/ppermute | solution.py:38
  451.2 38.6 %collective-permute-start.85 = (bf16[72,1408]{1,0:T(8,128)(2,1)}, bf16[72,1408]{1,0:T(8,128)(2,1)}, u32[]{:S(2)}, u32[]{:S(2)}) collective-permute-start(bf16[72,1408]{1,0:T(8,128)(2,1)} %get-tuple-element.371), channel_id=1, source_target_pairs={{0,3},{1,0},{2,1},{3,2},{4,7},{5,4},{6,5},{7,6},{8,11},{9,8},{10,9... | collective-permute-start | bytes 608264 | tf_op jit(solution)/shard_map/ppermute | solution.py:38
  451.5 53.6 %all-to-all-start.3 = ((bf16[32,36,576]{2,1,0:T(8,128)(2,1)}), bf16[32,36,576]{2,1,0:T(8,128)(2,1)}, u32[]{:S(2)}, u32[]{:S(2)}) async-start(bf16[32,36,576]{2,1,0:T(8,128)(2,1)} %get-tuple-element.377), calls=%async_computation.5 | async-start | bytes 3276800 | tf_op jit(solution)/shard_map/all_to_all | solution.py:196
  (158 other events, 1136.1 us)
Sparse Core Ops, SparseCore 0:
  55.6 48.5 all-gather.3
  184.0 40.8 all-gather.5
  333.9 48.3 reduce-scatter.2
  414.8 41.0 reduce-scatter.4
